TPU v7x, 32 devices: a whole 2x2x4 slice. The times are simulated.
32 devices in a mesh: section: 2 (over y), seq: 4 (over x, core), head: 4 (over z).
Axes of the slice: x: 2, y: 2, z: 4, core: 2. Of those that a mesh axis runs over, the one named last changes fastest.
Arguments:
- tokens: bfloat16 [2, 4096, 1536], P(None, 'seq'), may hold values from -6 to 6
- cotangent: bfloat16 [2, 4096, 1536], P(None, 'seq'), may hold values from -6 to 6
- norm_gain: float32 [2, 1536], P('section'), may hold values from 0.5 to 1.5
- w_z: bfloat16 [2, 1536, 3072], P('section', None, 'head'), may hold values from -0.15625 to 0.15625
- w_x: bfloat16 [2, 1536, 3072], P('section', None, 'head'), may hold values from -0.15625 to 0.15625
- w_bc: bfloat16 [2, 1536, 256], P('section'), may hold values from -0.15625 to 0.15625
- w_dt: bfloat16 [2, 1536, 48], P('section', None, 'head'), may hold values from -0.15625 to 0.15625
- conv_x: float32 [2, 3072, 4], P('section', 'head'), may hold values from -3 to 3
- conv_bc: float32 [2, 256, 4], P('section'), may hold values from -3 to 3
- dt_bias: float32 [2, 48], P('section', 'head'), may hold values from -6 to -2
- a_log: float32 [2, 48], P('section', 'head'), may hold values from -1 to 2.5
- skip_d: float32 [2, 48], P('section', 'head'), may hold values from 0.5 to 1.5
- gate_gain: float32 [2, 3072], P('section', 'head'), may hold values from 0.5 to 1.5
- w_out: bfloat16 [2, 1536, 3072], P('section', None, 'head'), may hold values from -0.109375 to 0.109375
Outputs:
- block_outputs: bfloat16 [2, 2, 4096, 1536], P('section', None, 'seq', 'head')
- input_grads: bfloat16 [2, 2, 4096, 1536], P('section', None, 'seq', 'head')
- grad_norm_gain: float32 [2, 1536], P('section', 'head')
- grad_w_z: float32 [2, 1536, 3072], P('section', 'seq', 'head')
- grad_w_x: float32 [2, 1536, 3072], P('section', 'seq', 'head')
- grad_w_bc: float32 [2, 1536, 256], P('section', 'seq', 'head')
- grad_w_dt: float32 [2, 1536, 48], P('section', 'seq', 'head')
- grad_conv_x: float32 [2, 3072, 4], P('section', 'head')
- grad_conv_bc: float32 [2, 256, 4], P('section')
- grad_dt_bias: float32 [2, 48], P('section', 'head')
- grad_a_log: float32 [2, 48], P('section', 'head')
- grad_skip_d: float32 [2, 48], P('section', 'head')
- grad_gate_gain: float32 [2, 3072], P('section', 'head')
- grad_w_out: float32 [2, 1536, 3072], P('section', 'seq', 'head')
All inputs are finite; a program needn't handle non-finite values.
Results may differ from a plain program's by a relative error of at most 0.02.
Values may be sent and summed in bfloat16 or wider, within the bound.
No kernel may reach another device: no remote copies, remote signals or barrier semaphores. Data moves between devices by JAX's collectives and lax.ppermute only.
A program may use at most 320 MiB of HBM per device.

v0:
```python
from functools import partial

import jax
import jax.numpy as jnp
from jax import lax
from jax.sharding import PartitionSpec as P

INNER = 3072
CONV = 4
SPAN = 256


epsilon = 1e-05
exact_mode = lax.Precision.HIGHEST


def passed_along(block, axis, distance):
    devices = range(lax.axis_size(axis))
    route = [(i - distance, i) for i in devices if i - distance in devices]
    return lax.ppermute(block, axis, route)


def entering(part, axis, combine, identity):
    place = lax.axis_index(axis)
    gathered = jax.tree.map(lambda a: lax.all_gather(a, axis), part)
    state = jax.tree.map(lambda a, e: jnp.zeros_like(a) + jnp.asarray(e, a.dtype), part, identity)

    def one(lap, state):
        return combine(
            state, jax.tree.map(lambda a: lax.dynamic_index_in_dim(a, lap, 0, False), gathered)
        )

    return lax.fori_loop(0, place, one, state)


def carried_in_2(value, axis, combine, identity):
    length, position = (lax.axis_size(axis), lax.axis_index(axis))
    everything = jax.tree.map(
        lambda part, kind: lax.all_gather(part.astype(kind), axis),
        value,
        jax.tree.map(lambda a: jnp.bfloat16 if a.dtype == jnp.float32 else a.dtype, value),
    )
    start = jax.tree.map(
        lambda part, zero: jnp.broadcast_to(jnp.asarray(zero, part.dtype), part.shape),
        value,
        identity,
    )

    def lap(k, before):
        at = length - 1 - k
        reached = at > position
        new = combine(
            before, jax.tree.map(lambda part, own: part[at].astype(own.dtype), everything, value)
        )
        return jax.tree.map(lambda a, b: jnp.where(reached, a, b), new, before)

    return lax.fori_loop(0, length, lap, start)


def swish_value(values):
    return values * jax.nn.sigmoid(values)


def swish_slope(values):
    gate_sigmoid = jax.nn.sigmoid(values)
    return gate_sigmoid * (1.0 + values * (1.0 - gate_sigmoid))


def contract_last(left_side, right_side):
    return lax.dot_general(
        left_side, right_side, (((1,), (1,)), ((), ())), preferred_element_type=jnp.float32
    )


def contract_first(left_side, right_side):
    return lax.dot_general(
        left_side, right_side, (((0,), (0,)), ((), ())), preferred_element_type=jnp.float32
    )


def span_step(decay_rate, carried, inputs):
    span_x, span_dt, span_b, span_c = inputs
    log_decay = span_dt * decay_rate[None, :]
    running = jnp.cumsum(log_decay, axis=0)
    spread = running[:, None, :] - running[None, :, :]
    length = span_dt.shape[0]
    causal = jnp.arange(length)[:, None] >= jnp.arange(length)[None, :]
    factors = jnp.exp(jnp.where(causal[:, :, None], spread, -jnp.inf))
    intersection = jnp.dot(span_c, span_b.T, precision=exact_mode)
    mixing = intersection[:, :, None] * factors * span_dt[None, :, :]
    inner_out = jnp.einsum("tsh,shp->thp", mixing, span_x, precision=exact_mode)
    carried_out = jnp.einsum("tn,hpn->thp", span_c, carried, precision=exact_mode)
    outputs = inner_out + jnp.exp(running)[:, :, None] * carried_out
    to_end = jnp.exp(running[-1][None, :] - running) * span_dt
    new_state = jnp.exp(running[-1])[:, None, None] * carried + jnp.einsum(
        "sh,shp,sn->hpn", to_end, span_x, span_b, precision=exact_mode
    )
    return (new_state, outputs)


def local_states(heads_x, step_sizes, decay_rate, b_in, c_in, start_state):
    row_count, head_count, head_width = heads_x.shape
    blocks = row_count // SPAN
    pieces = (
        heads_x.reshape(blocks, SPAN, head_count, head_width),
        step_sizes.reshape(blocks, SPAN, head_count),
        b_in.reshape(blocks, SPAN, -1),
        c_in.reshape(blocks, SPAN, -1),
    )
    end_state, outputs = lax.scan(
        jax.checkpoint(partial(span_step, decay_rate)), start_state, pieces
    )
    return (end_state, outputs.reshape(row_count, head_count, head_width))


def carry_combine(earlier, latter):
    return (earlier[0] * latter[0], latter[0][:, None, None] * earlier[1] + latter[1])


def causal_mix(extended, weight, row_count):
    summation = extended[0:row_count] * weight[:, 0]
    for offset in range(1, CONV):
        summation = summation + extended[offset : offset + row_count] * weight[:, offset]
    return summation


def project_inputs(x_in, weights):
    norm_gain, w_z, w_x, w_bc, w_dt, conv_x, conv_bc, dt_bias, a_log, skip_d, gate_gain, w_out = (
        weights
    )
    residual = x_in.astype(jnp.float32)
    rescale = lax.rsqrt(jnp.mean(residual * residual, axis=-1, keepdims=True) + epsilon)
    normed = (residual * rescale * norm_gain).astype(jnp.bfloat16)
    gate_in = jnp.dot(normed, w_z, preferred_element_type=jnp.float32)
    inner_raw = jnp.dot(normed, w_x, preferred_element_type=jnp.float32).astype(jnp.bfloat16)
    shared_raw = jnp.dot(normed, w_bc, preferred_element_type=jnp.float32).astype(jnp.bfloat16)
    raw_inputs = jnp.concatenate([inner_raw, shared_raw], axis=1)
    step_raw = jnp.dot(normed, w_dt, preferred_element_type=jnp.float32)
    return (residual, rescale, normed, gate_in, raw_inputs, step_raw)


def conv_states(raw_inputs, edge_rows, step_raw, weights):
    norm_gain, w_z, w_x, w_bc, w_dt, conv_x, conv_bc, dt_bias, a_log, skip_d, gate_gain, w_out = (
        weights
    )
    conv_all = jnp.concatenate([conv_x, conv_bc], axis=0)
    extended = jnp.concatenate([edge_rows, raw_inputs], axis=0).astype(jnp.float32)
    row_count = raw_inputs.shape[0]
    pre_act = causal_mix(extended, conv_all, row_count)
    activated = swish_value(pre_act)
    inner_width = conv_x.shape[0]
    state_width = conv_bc.shape[0] // 2
    head_count = a_log.shape[0]
    heads_x = activated[:, :inner_width].reshape(row_count, head_count, inner_width // head_count)
    b_in = activated[:, inner_width : inner_width + state_width]
    c_in = activated[:, inner_width + state_width :]
    step_sizes = jax.nn.softplus(step_raw + dt_bias)
    decay_rate = -jnp.exp(a_log)
    return (extended, pre_act, heads_x, b_in, c_in, step_sizes, decay_rate)


def mixer_forward(x_in, weights):
    norm_gain, w_z, w_x, w_bc, w_dt, conv_x, conv_bc, dt_bias, a_log, skip_d, gate_gain, w_out = (
        weights
    )
    share_width = x_in.shape[1] // lax.axis_size("head")
    column_start = lax.axis_index("head") * share_width
    residual, rescale, normed, gate_in, raw_inputs, step_raw = project_inputs(x_in, weights)
    edge_rows = passed_along(raw_inputs[raw_inputs.shape[0] - (CONV - 1) :], "seq", 1)
    extended, pre_act, heads_x, b_in, c_in, step_sizes, decay_rate = conv_states(
        raw_inputs, edge_rows, step_raw, weights
    )
    row_count, head_count, head_width = heads_x.shape
    zero_state = jnp.zeros((head_count, head_width, b_in.shape[1]), jnp.float32)
    local_end, local_out = local_states(heads_x, step_sizes, decay_rate, b_in, c_in, zero_state)
    running_all = jnp.cumsum(step_sizes * decay_rate[None, :], axis=0)
    through = jnp.exp(running_all[-1])
    prefix = entering(
        (through, local_end),
        "seq",
        carry_combine,
        (jnp.ones_like(through), jnp.zeros_like(local_end)),
    )
    start_state = prefix[1]
    carried_in = jnp.einsum("tn,hpn->thp", c_in, start_state, precision=exact_mode)
    mixed = (
        local_out + jnp.exp(running_all)[:, :, None] * carried_in + skip_d[None, :, None] * heads_x
    )
    mixed = mixed.reshape(row_count, head_count * head_width)
    gated = mixed * swish_value(gate_in)
    part_squares = jnp.sum(gated * gated, axis=-1)
    scaled = (gated * gate_gain).astype(jnp.bfloat16)
    branch_part = contract_last(scaled, w_out)
    summed, squares = lax.psum((branch_part, part_squares), "head")
    row_scale = lax.rsqrt(squares / INNER + epsilon)
    block_out = (residual + row_scale[:, None] * summed).astype(jnp.bfloat16)
    share_out = lax.dynamic_slice_in_dim(block_out, column_start, share_width, 1)
    kept = (x_in, edge_rows, start_state, summed, row_scale)
    return (block_out, share_out, kept)


def mixer_backward(grad_out, kept, weights):
    norm_gain, w_z, w_x, w_bc, w_dt, conv_x, conv_bc, dt_bias, a_log, skip_d, gate_gain, w_out = (
        weights
    )
    x_in, edge_rows, start_state, summed, row_scale = kept
    model_width = x_in.shape[1]
    share_width = model_width // lax.axis_size("head")
    column_start = lax.axis_index("head") * share_width
    residual, rescale, normed, gate_in, raw_inputs, step_raw = project_inputs(x_in, weights)
    extended, pre_act, heads_x, b_in, c_in, step_sizes, decay_rate = conv_states(
        raw_inputs, edge_rows, step_raw, weights
    )
    row_count, head_count, head_width = heads_x.shape
    grad_summed = (row_scale[:, None] * grad_out).astype(jnp.bfloat16)
    grad_scale = jnp.sum(grad_out * summed, axis=-1)

    def states_given(heads_in, sizes_in, rate_in, b_part, c_part):
        return local_states(heads_in, sizes_in, rate_in, b_part, c_part, start_state)

    (end_state, states_out), states_back = jax.vjp(
        states_given, heads_x, step_sizes, decay_rate, b_in, c_in
    )
    mixed = (states_out + skip_d[None, :, None] * heads_x).reshape(
        row_count, head_count * head_width
    )
    gate_act = swish_value(gate_in)
    gated = mixed * gate_act
    scaled = (gated * gate_gain).astype(jnp.bfloat16)
    grad_scaled = jnp.dot(grad_summed, w_out, preferred_element_type=jnp.float32)
    grad_w_out = contract_first(grad_summed, scaled)
    grad_gate_gain = jnp.sum(grad_scaled * gated, axis=0)
    grad_gated = (
        grad_scaled * gate_gain
        - (grad_scale * row_scale * row_scale * row_scale / INNER)[:, None] * gated
    )
    grad_mixed = grad_gated * gate_act
    grad_gate = (grad_gated * mixed * swish_slope(gate_in)).astype(jnp.bfloat16)
    grad_heads = grad_mixed.reshape(row_count, head_count, head_width)
    grad_skip = jnp.sum(grad_heads * heads_x, axis=(0, 2))
    running_all = jnp.cumsum(step_sizes * decay_rate[None, :], axis=0)
    through = jnp.exp(running_all[-1])
    back_local = jnp.einsum(
        "th,thp,tn->hpn", jnp.exp(running_all), grad_heads, c_in, precision=exact_mode
    )
    suffix = carried_in_2(
        (through, back_local),
        "seq",
        carry_combine,
        (jnp.ones_like(through), jnp.zeros_like(back_local)),
    )
    grad_end = suffix[1]
    grad_x_states, grad_sizes, grad_rate, grad_b, grad_c = states_back((grad_end, grad_heads))
    grad_inner = (grad_x_states + skip_d[None, :, None] * grad_heads).reshape(
        row_count, head_count * head_width
    )
    grad_act = jnp.concatenate([grad_inner, grad_b, grad_c], axis=1)
    grad_pre = grad_act * swish_slope(pre_act)
    conv_all = jnp.concatenate([conv_x, conv_bc], axis=0)
    grad_extended = jnp.zeros_like(extended)
    conv_columns = []
    for offset in range(CONV):
        grad_extended = grad_extended + jnp.pad(
            grad_pre * conv_all[:, offset], ((offset, CONV - 1 - offset), (0, 0))
        )
        conv_columns.append(jnp.sum(grad_pre * extended[offset : offset + row_count], axis=0))
    grad_conv = jnp.stack(conv_columns, axis=1)
    edge_back = passed_along(grad_extended[: CONV - 1], "seq", -1)
    grad_raw = grad_extended[CONV - 1 :] + jnp.pad(edge_back, ((row_count - (CONV - 1), 0), (0, 0)))
    inner_width = conv_x.shape[0]
    grad_inner_raw = grad_raw[:, :inner_width].astype(jnp.bfloat16)
    grad_step_exact = grad_sizes * jax.nn.sigmoid(step_raw + dt_bias)
    grad_dt_bias = jnp.sum(grad_step_exact, axis=0)
    grad_step = grad_step_exact.astype(jnp.bfloat16)
    grad_a_log = grad_rate * decay_rate
    normed_part = (
        contract_last(grad_gate, w_z)
        + contract_last(grad_inner_raw, w_x)
        + contract_last(grad_step, w_dt)
    )
    unit_rows = residual * rescale
    grad_normed_sum, grad_shared_sum, grad_conv_shared = (
        lax.psum(normed_part.astype(jnp.bfloat16), "head").astype(jnp.float32),
        lax.psum(grad_raw[:, inner_width:].astype(jnp.bfloat16), "head").astype(jnp.float32),
        lax.psum(grad_conv[inner_width:].astype(jnp.bfloat16), "head").astype(jnp.float32),
    )
    grad_shared = grad_shared_sum.astype(jnp.bfloat16)
    grad_normed = grad_normed_sum + contract_last(grad_shared, w_bc)
    grad_norm_full = jnp.sum(grad_normed * unit_rows, axis=0)
    grad_norm_gain = lax.dynamic_slice_in_dim(grad_norm_full, column_start, share_width, 0)
    scaled_grad = grad_normed * norm_gain
    grad_x_full = grad_out + rescale * (
        scaled_grad - unit_rows * jnp.mean(scaled_grad * unit_rows, axis=-1, keepdims=True)
    )
    grad_x = grad_x_full.astype(jnp.bfloat16)
    shared_cols = grad_shared.shape[1] // lax.axis_size("head")
    own_shared = lax.dynamic_slice_in_dim(
        grad_shared, lax.axis_index("head") * shared_cols, shared_cols, 1
    )
    grad_w_bc = contract_first(normed, own_shared)
    grad_w_z = contract_first(normed, grad_gate)
    grad_w_x = contract_first(normed, grad_inner_raw)
    grad_w_dt = contract_first(normed, grad_step)
    grads = (
        grad_norm_gain,
        grad_w_z,
        grad_w_x,
        grad_w_bc,
        grad_w_dt,
        grad_conv[:inner_width],
        grad_conv_shared,
        grad_dt_bias,
        grad_a_log,
        grad_skip,
        grad_gate_gain,
        grad_w_out,
    )
    return (grads, grad_x)


def shards(
    tokens,
    cotangent,
    norm_gain,
    w_z,
    w_x,
    w_bc,
    w_dt,
    conv_x,
    conv_bc,
    dt_bias,
    a_log,
    skip_d,
    gate_gain,
    w_out,
):
    weights = tuple(
        (
            member[0]
            for member in (
                norm_gain,
                w_z,
                w_x,
                w_bc,
                w_dt,
                conv_x,
                conv_bc,
                dt_bias,
                a_log,
                skip_d,
                gate_gain,
                w_out,
            )
        )
    )
    first_section = lax.axis_index("section") == 0
    micro_count = tokens.shape[0]
    row_count = tokens.shape[1]
    model_width = tokens.shape[2]
    share_width = model_width // lax.axis_size("head")
    column_start = lax.axis_index("head") * share_width

    def by_section(first_value, second_value):
        return jax.tree.map(
            lambda upper_one, lower_one: jnp.where(first_section, upper_one, lower_one),
            first_value,
            second_value,
        )

    arriving = jnp.zeros((row_count, model_width), jnp.bfloat16)
    kept_ticks = []
    share_ticks = []
    for tick_index in range(micro_count + 1):
        own_rows = tokens[min(tick_index, micro_count - 1)]
        incoming = arriving
        x_in = jnp.where(first_section, own_rows, incoming)
        outgoing, share_out, kept = mixer_forward(x_in, weights)
        kept_ticks.append(kept)
        share_ticks.append(share_out)
        if tick_index < micro_count:
            arriving = passed_along(outgoing, "section", 1)
    block_outputs = jnp.stack(
        [
            by_section(share_ticks[batch_index], share_ticks[batch_index + 1])
            for batch_index in range(micro_count)
        ]
    )
    grad_arriving = jnp.zeros((row_count, model_width), jnp.bfloat16)
    totals = None
    grad_ticks = []
    for tick_index in range(micro_count + 1):
        kept = by_section(
            kept_ticks[max(tick_index - 1, 0)], kept_ticks[min(tick_index + 1, micro_count)]
        )
        grad_incoming = grad_arriving
        grad_in = jnp.where(
            first_section,
            grad_incoming.astype(jnp.float32),
            cotangent[min(tick_index, micro_count - 1)].astype(jnp.float32),
        )
        usable = jnp.where(first_section, tick_index >= 1, tick_index < micro_count)
        grads, grad_x = mixer_backward(grad_in, kept, weights)
        grads = jax.tree.map(lambda member: jnp.where(usable, member, 0.0), grads)
        if totals is None:
            totals = grads
        else:
            totals = jax.tree.map(jnp.add, totals, grads)
        grad_ticks.append(grad_x)
        if tick_index < micro_count:
            grad_arriving = passed_along(grad_x, "section", -1)
    input_grads = jnp.stack(
        [
            lax.dynamic_slice_in_dim(
                by_section(grad_ticks[batch_index + 1], grad_ticks[batch_index]),
                column_start,
                share_width,
                1,
            )
            for batch_index in range(micro_count)
        ]
    )
    (
        norm_total,
        z_total,
        x_total,
        bc_total,
        dt_total,
        convx_total,
        convbc_total,
        bias_total,
        alog_total,
        skip_total,
        gain_total,
        out_total,
    ) = totals
    z_part, x_part, bc_part, dt_part, out_part = (
        lax.psum_scatter(
            z_total.astype(jnp.bfloat16), "seq", scatter_dimension=0, tiled=True
        ).astype(jnp.float32),
        lax.psum_scatter(
            x_total.astype(jnp.bfloat16), "seq", scatter_dimension=0, tiled=True
        ).astype(jnp.float32),
        lax.psum_scatter(
            bc_total.astype(jnp.bfloat16), "seq", scatter_dimension=0, tiled=True
        ).astype(jnp.float32),
        lax.psum_scatter(
            dt_total.astype(jnp.bfloat16), "seq", scatter_dimension=0, tiled=True
        ).astype(jnp.float32),
        lax.psum_scatter(
            out_total.astype(jnp.bfloat16), "seq", scatter_dimension=0, tiled=True
        ).astype(jnp.float32),
    )
    norm_sum, convx_sum, convbc_sum, bias_sum, alog_sum, skip_sum, gain_sum = lax.psum(
        (norm_total, convx_total, convbc_total, bias_total, alog_total, skip_total, gain_total),
        "seq",
    )
    return (
        block_outputs[None],
        input_grads[None],
        norm_sum[None],
        z_part[None],
        x_part[None],
        bc_part[None],
        dt_part[None],
        convx_sum[None],
        convbc_sum[None],
        bias_sum[None],
        alog_sum[None],
        skip_sum[None],
        gain_sum[None],
        out_part[None],
    )


def solution(mesh):
    placed = (
        P(None, "seq", None),
        P(None, "seq", None),
        P("section", None),
        P("section", None, "head"),
        P("section", None, "head"),
        P("section", None, None),
        P("section", None, "head"),
        P("section", "head", None),
        P("section", None, None),
        P("section", "head"),
        P("section", "head"),
        P("section", "head"),
        P("section", "head"),
        P("section", None, "head"),
    )
    return jax.shard_map(
        shards,
        mesh=mesh,
        in_specs=placed,
        out_specs=(
            P("section", None, "seq", "head"),
            P("section", None, "seq", "head"),
            P("section", "head"),
            P("section", "seq", "head"),
            P("section", "seq", "head"),
            P("section", "seq", "head"),
            P("section", "seq", "head"),
            P("section", "head", None),
            P("section", None, None),
            P("section", "head"),
            P("section", "head"),
            P("section", "head"),
            P("section", "head"),
            P("section", "seq", "head"),
        ),
        check_vma=False,
    )
```

profile of v0, /device:TPU:0, one launch (start us, length us, event | category | flops | bytes accessed | tf_op | source)
XLA Modules:
  0.0 3845.0 jit_solution(1533259707767384772)
XLA Ops:
  46.2 140.0 %while.252 = (s32[]{:T(128)}, f32[12,64,128]{2,1,0:T(8,128)S(1)}, f32[4,256,12,64]{1,0,3,2:T(4,128)}, f32[4,256,12]{1,0,2:T(4,128)}, f32[12]{0:T(128)}, /*index=...) while((s32[]{:T(128)}, f32[12,64,128]{2,1,0:T(8,128)S(1)}, ...), condition=%wide.region_4.5_spmd.clone, body=%wide.region_1.4_spmd.clone.sunk | while | flops 1313219584 | bytes 11419048 | solution.py:110
  239.6 214.6 %all-reduce.33.cloned.1.call-done = f32[1024,1536]{1,0:T(8,128)} async-done(((f32[1024,1536]{1,0:T(8,128)}), f32[1024,1536]{1,0:T(8,128)}) %all-reduce.33.cloned.1.call-update) | async-done | bytes 6291472 | tf_op jit(solution)/shard_map/psum | solution.py:194
  465.7 65.8 %collective-permute-done.1 = bf16[1024,1536]{1,0:T(8,128)(2,1)} collective-permute-done((bf16[1024,1536]{1,0:T(8,128)(2,1)}, bf16[1024,1536]{1,0:T(8,128)(2,1)}, u32[]{:S(2)}, u32[]{:S(2)}) %collective-permute-start.1) | collective-permute-done | bytes 3145760 | tf_op jit(solution)/shard_map/ppermute | solution.py:20
  571.4 140.0 %while.253 = (s32[]{:T(128)}, f32[12,64,128]{2,1,0:T(8,128)S(1)}, f32[4,256,12,64]{1,0,3,2:T(4,128)}, f32[4,256,12]{1,0,2:T(4,128)}, f32[12]{0:T(128)}, /*index=...) while((s32[]{:T(128)}, f32[12,64,128]{2,1,0:T(8,128)S(1)}, ...), condition=%wide.region_16.17_spmd.clone, body=%wide.region_13.16_spmd.clone.sunk | while | flops 1313219584 | bytes 11419048 | solution.py:110
  764.8 214.6 %all-reduce.35.cloned.1.call-done = f32[1024,1536]{1,0:T(8,128)} async-done(((f32[1024,1536]{1,0:T(8,128)}), f32[1024,1536]{1,0:T(8,128)}) %all-reduce.35.cloned.1.call-update) | async-done | bytes 6291472 | tf_op jit(solution)/shard_map/psum | solution.py:194
  993.8 64.0 %collective-permute-done.3 = bf16[1024,1536]{1,0:T(8,128)(2,1)} collective-permute-done((bf16[1024,1536]{1,0:T(8,128)(2,1)}, bf16[1024,1536]{1,0:T(8,128)(2,1)}, u32[]{:S(2)}, u32[]{:S(2)}) %collective-permute-start.3) | collective-permute-done | bytes 3145760 | tf_op jit(solution)/shard_map/ppermute | solution.py:20
  1193.5 140.1 %while.254 = (s32[]{:T(128)}, f32[12,64,128]{2,1,0:T(8,128)S(1)}, f32[4,256,12,64]{1,0,3,2:T(4,128)}, f32[4,256,12]{1,0,2:T(4,128)}, f32[12]{0:T(128)}, /*index=...) while((s32[]{:T(128)}, f32[12,64,128]{2,1,0:T(8,128)S(1)}, ...), condition=%wide.region_28.29_spmd.clone, body=%wide.region_25.28_spmd.clone.sunk | while | flops 1313219584 | bytes 11419048 | solution.py:110
  1375.4 129.3 %while.249 = (s32[]{:T(128)}, f32[12,64,128]{2,1,0:T(8,128)S(1)}, f32[4,256,12,64]{1,0,3,2:T(4,128)}, f32[4,12,64,128]{3,2,1,0:T(8,128)}, f32[4,256,12]{1,2,0:T(...) while((s32[]{:T(128)}, f32[12,64,128]{2,1,0:T(8,128)S(1)}, ...), condition=%wide.region_41.42_spmd.clone, body=%wide.region_38.41_spmd.clone.sunk | while | flops 1312957440 | bytes 10507149 | solution.py:110
  1548.9 351.2 %while.256 = (s32[]{:T(128)}, f32[12]{0:T(128)}, f32[12,64,128]{2,1,0:T(8,128)S(1)}, f32[4,256,12,64]{1,0,3,2:T(4,128)}, f32[4,256,12]{1,0,2:T(4,128)}, /*index=...) while((s32[]{:T(128)}, f32[12]{0:T(128)}, ...), condition=%wide.region_59.60_spmd.clone, body=%wide.region_46.59_spmd.clone.sunk | while | flops 3036332032 | bytes 38174520 | solution.py:110
  1613.0 17.9 dynamic_update_slice.213
  1700.7 17.9 dynamic_update_slice.213
  1788.4 17.9 dynamic_update_slice.213
  1876.1 17.9 dynamic_update_slice.213
  1921.3 31.6 broadcast_multiply_fusion.12
  2027.9 94.2 %all-reduce.43.cloned.1.call-done = (bf16[1024,1536]{1,0:T(8,128)(2,1)}, bf16[1024,256]{0,1:T(8,128)(2,1)}) async-done(((bf16[1024,1536]{1,0:T(8,128)(2,1)}, bf16[1024,256]{0,1:T(8,128)(2,1)}), (bf16[1024,1536]{1,0:T(8,128)(2,1)}, bf16[1024,256]{0,1:T(8,128)(2,1)})) %all-reduce.43.cloned.1.call-update) | async-done | bytes 3670032 | tf_op jit(solution)/shard_map/psum | solution.py:283
  2138.6 129.0 %while.250 = (s32[]{:T(128)}, f32[12,64,128]{2,1,0:T(8,128)S(1)}, f32[4,256,12,64]{1,0,3,2:T(4,128)}, f32[4,12,64,128]{3,2,1,0:T(8,128)}, f32[4,256,12]{1,2,0:T(...) while((s32[]{:T(128)}, f32[12,64,128]{2,1,0:T(8,128)S(1)}, ...), condition=%wide.region_68.69_spmd.clone, body=%wide.region_65.68_spmd.clone.sunk | while | flops 1312957440 | bytes 10507149 | solution.py:110
  2281.8 64.9 %all-reduce.37.cloned.1.call-done = f32[1024,1536]{1,0:T(8,128)} async-done(((f32[1024,1536]{1,0:T(8,128)}), f32[1024,1536]{1,0:T(8,128)}) %all-reduce.37.cloned.1.call-update) | async-done | bytes 6291472 | tf_op jit(solution)/shard_map/psum | solution.py:194
  2395.2 351.2 %while.258 = (s32[]{:T(128)}, f32[12]{0:T(128)}, f32[12,64,128]{2,1,0:T(8,128)S(1)}, f32[4,256,12,64]{1,0,3,2:T(4,128)}, f32[4,256,12]{1,0,2:T(4,128)}, /*index=...) while((s32[]{:T(128)}, f32[12]{0:T(128)}, ...), condition=%wide.region_86.87_spmd.clone, body=%wide.region_73.86_spmd.clone.sunk | while | flops 3036332032 | bytes 38174520 | solution.py:110
  2832.5 104.3 %all-reduce.41.cloned.1.call-done = (bf16[1024,1536]{1,0:T(8,128)(2,1)}, bf16[1024,256]{0,1:T(8,128)(2,1)}) async-done(((bf16[1024,1536]{1,0:T(8,128)(2,1)}, bf16[1024,256]{0,1:T(8,128)(2,1)}), (bf16[1024,1536]{1,0:T(8,128)(2,1)}, bf16[1024,256]{0,1:T(8,128)(2,1)})) %all-reduce.41.cloned.1.call-update) | async-done | bytes 3670032 | tf_op jit(solution)/shard_map/psum | solution.py:283
  2954.8 129.6 %while.251 = (s32[]{:T(128)}, f32[12,64,128]{2,1,0:T(8,128)S(1)}, f32[4,256,12,64]{1,0,3,2:T(4,128)}, f32[4,12,64,128]{3,2,1,0:T(8,128)}, f32[4,256,12]{1,2,0:T(...) while((s32[]{:T(128)}, f32[12,64,128]{2,1,0:T(8,128)S(1)}, ...), condition=%wide.region_95.96_spmd.clone, body=%wide.region_92.95_spmd.clone.sunk | while | flops 1312957440 | bytes 10506929 | solution.py:110
  3137.0 351.3 %while.260 = (s32[]{:T(128)}, f32[12]{0:T(128)}, f32[12,64,128]{2,1,0:T(8,128)S(1)}, f32[4,256,12,64]{1,0,3,2:T(4,128)}, f32[4,256,12]{1,0,2:T(4,128)}, /*index=...) while((s32[]{:T(128)}, f32[12]{0:T(128)}, ...), condition=%wide.region_113.114_spmd.clone, body=%wide.region_100.113_spmd.clone.sunk | while | flops 3036332032 | bytes 38174520 | solution.py:110
  3562.0 120.0 %all-reduce.39.cloned.1.call-done = (bf16[1024,1536]{1,0:T(8,128)(2,1)}, bf16[1024,256]{0,1:T(8,128)(2,1)}) async-done(((bf16[1024,1536]{1,0:T(8,128)(2,1)}, bf16[1024,256]{0,1:T(8,128)(2,1)}), (bf16[1024,1536]{1,0:T(8,128)(2,1)}, bf16[1024,256]{0,1:T(8,128)(2,1)})) %all-reduce.39.cloned.1.call-update) | async-done | bytes 3670032 | tf_op jit(solution)/shard_map/psum | solution.py:283
  3776.1 24.3 reduce-scatter.10.cloned.1.call-done
  3802.5 33.4 reduce-scatter.12.cloned.1.call-done
  (2591 shorter events, 2717.9 us)
Async XLA Ops:
  7.2 204.0 %all-gather.16.cloned.1.call-start = ((), (), s32[]{:S(2)}) async-start(), calls=%async_computation.11 | async-start | bytes 1966080 | tf_op jit(solution)/shard_map/all_gather | solution.py:25
  18.3 6.3 collective-permute-start
  187.1 267.2 %all-reduce.33.cloned.1.call-start = ((), (), s32[]{:S(2)}) async-start(), calls=%async_computation.5 | async-start | bytes 12582912 | tf_op jit(solution)/shard_map/psum | solution.py:194
  227.8 508.7 %all-gather.18.cloned.1.call-start = ((), (), s32[]{:S(2)}) async-start(), calls=%async_computation.12 | async-start | bytes 1966080 | tf_op jit(solution)/shard_map/all_gather | solution.py:25
  460.5 71.0 %collective-permute-start.1 = (bf16[1024,1536]{1,0:T(8,128)(2,1)}, bf16[1024,1536]{1,0:T(8,128)(2,1)}, u32[]{:S(2)}, u32[]{:S(2)}) collective-permute-start(bf16[1024,1536]{1,0:T(8,128)(2,1)} %fusion.393), channel_id=1, source_target_pairs={{0,16},{1,17},{2,18},{3,19},{4,20},{5,21},{6,22},{7,23},{8,24},{9,... | collective-permute-start | bytes 9437192 | tf_op jit(solution)/shard_map/ppermute | solution.py:20
  545.5 4.3 collective-permute-start.2
  712.2 267.2 %all-reduce.35.cloned.1.call-start = ((), (), s32[]{:S(2)}) async-start(), calls=%async_computation.6 | async-start | bytes 12582912 | tf_op jit(solution)/shard_map/psum | solution.py:194
  753.1 615.4 %all-gather.20.cloned.1.call-start = ((), (), s32[]{:S(2)}) async-start(), calls=%async_computation.13 | async-start | bytes 1966080 | tf_op jit(solution)/shard_map/all_gather | solution.py:25
  988.6 69.2 %collective-permute-start.3 = (bf16[1024,1536]{1,0:T(8,128)(2,1)}, bf16[1024,1536]{1,0:T(8,128)(2,1)}, u32[]{:S(2)}, u32[]{:S(2)}) collective-permute-start(bf16[1024,1536]{1,0:T(8,128)(2,1)} %get-tuple-element.3475), channel_id=1, source_target_pairs={{0,16},{1,17},{2,18},{3,19},{4,20},{5,21},{6,22},{7,23},{8,24},{9,... | collective-permute-start | bytes 9437192 | tf_op jit(solution)/shard_map/ppermute | solution.py:20
  1092.8 70.0 %collective-permute-start.4 = (bf16[3,1024]{0,1:T(8,128)(2,1)}, bf16[3,1024]{0,1:T(8,128)(2,1)}, u32[]{:S(2)}, u32[]{:S(2)}) collective-permute-start(bf16[3,1024]{0,1:T(8,128)(2,1)} %pad_maximum_fusion), channel_id=1, source_target_pairs={{0,4},{4,8},{8,12},{1,5},{5,9},{9,13},{2,6},{6,10},{10,14},{3,7},{... | collective-permute-start | bytes 18440 | tf_op jit(solution)/shard_map/ppermute | solution.py:20
  1334.4 787.7 %all-reduce.43.cloned.1.call-start = ((), (), s32[]{:S(2)}) async-start(), calls=%async_computation.18 | async-start | bytes 7340032 | tf_op jit(solution)/shard_map/psum | solution.py:283
  1966.5 6.1 collective-permute-start.5
  1979.4 367.2 %all-reduce.37.cloned.1.call-start = ((), (), s32[]{:S(2)}) async-start(), calls=%async_computation.7 | async-start | bytes 12582912 | tf_op jit(solution)/shard_map/psum | solution.py:194
  2027.9 908.8 %all-reduce.41.cloned.1.call-start = ((), (), s32[]{:S(2)}) async-start(), calls=%async_computation.17 | async-start | bytes 7340032 | tf_op jit(solution)/shard_map/psum | solution.py:283
  2133.6 213.1 %collective-permute-start.6 = (bf16[1024,1536]{1,0:T(8,128)(2,1)}, bf16[1024,1536]{1,0:T(8,128)(2,1)}, u32[]{:S(2)}, u32[]{:S(2)}) collective-permute-start(bf16[1024,1536]{1,0:T(8,128)(2,1)} %fusion.399), channel_id=1, source_target_pairs={{16,0},{17,1},{18,2},{19,3},{20,4},{21,5},{22,6},{23,7},{24,8},{25... | collective-permute-start | bytes 9437192 | tf_op jit(solution)/shard_map/ppermute | solution.py:20
  2783.0 5.8 collective-permute-start.7
  2795.5 886.5 %all-reduce.39.cloned.1.call-start = ((), (), s32[]{:S(2)}) async-start(), calls=%async_computation.16 | async-start | bytes 7340032 | tf_op jit(solution)/shard_map/psum | solution.py:283
  2949.4 139.3 %collective-permute-start.8 = (bf16[1024,1536]{1,0:T(8,128)(2,1)}, bf16[1024,1536]{1,0:T(8,128)(2,1)}, u32[]{:S(2)}, u32[]{:S(2)}) collective-permute-start(bf16[1024,1536]{1,0:T(8,128)(2,1)} %fusion.407), channel_id=1, source_target_pairs={{16,0},{17,1},{18,2},{19,3},{20,4},{21,5},{22,6},{23,7},{24,8},{25... | collective-permute-start | bytes 9437192 | tf_op jit(solution)/shard_map/ppermute | solution.py:20
  3525.0 5.3 collective-permute-start.9
  3537.1 205.3 %reduce-scatter.18.cloned.1.call-start = ((), (), s32[]{:S(2)}) async-start(), calls=%async_computation.15 | async-start | bytes 491520
  3561.9 210.3 %reduce-scatter.16.cloned.1.call-start = ((), (), s32[]{:S(2)}) async-start(), calls=%async_computation.14 | async-start | bytes 491520
  3687.4 86.4 %reduce-scatter.14.cloned.1.call-start = ((), (), s32[]{:S(2)}) async-start(), calls=%async_computation.10 | async-start | bytes 2949120 | tf_op jit(solution)/shard_map/reduce_scatter | solution.py:449
  3697.5 102.9 %reduce-scatter.10.cloned.1.call-start = ((), (), s32[]{:S(2)}) async-start(), calls=%async_computation.8 | async-start | bytes 2949120 | tf_op jit(solution)/shard_map/reduce_scatter | solution.py:437
  3709.9 126.0 %reduce-scatter.12.cloned.1.call-start = ((), (), s32[]{:S(2)}) async-start(), calls=%async_computation.9 | async-start | bytes 2949120 | tf_op jit(solution)/shard_map/reduce_scatter | solution.py:440
  (500 other events, 5688.9 us)
Sparse Core Ops, SparseCore 0:
  187.2 24.0 all-gather.15
  227.9 226.2 all-reduce.32
  712.3 24.0 all-gather.17
  753.2 226.2 all-reduce.34
  1334.5 20.2 all-gather.19
  1979.5 142.5 all-reduce.42
  2124.5 222.0 all-reduce.36
  2795.7 141.0 all-reduce.40
  3537.2 144.7 all-reduce.38
  3684.9 19.8 reduce-scatter.17
  3707.9 20.8 reduce-scatter.15
  3731.2 33.2 reduce-scatter.13
  3767.2 33.1 reduce-scatter.9
  3802.8 33.0 reduce-scatter.11
where the time goes:
time: 3890 us; the launch traced here: 3850 us
  local copies, waits for them, and re-layouts  1290 us (33%)
  waiting for transfers between devices  1010 us (26%)
  matrix products  774 us (20%)
  other arithmetic  594 us (15%)
  blocking collectives  125 us (3%)
    dynamic_update_slice x108, local copies, waits for them, and re-layouts, local_states(): lax.scan(jax.checkpoint(partial(span_step, decay_rate)), start_state, pie...  735 us
    psum x3, waiting for transfers between devices, mixer_forward(): summed, squares = lax.psum((branch_part, part_squares), 'head')  494 us
    psum x3, waiting for transfers between devices, mixer_backward(): lax.psum(normed_part.astype(jnp.bfloat16), 'head').astype(jnp.float32)  318 us
    dot_general x48, matrix products, span_step(): inner_out = jnp.einsum('tsh,shp->thp', mixing, span_x, precision=exact_mode)  217 us
    another operation x209, other arithmetic  211 us
    another operation x282, local copies, waits for them, and re-layouts  161 us
    ppermute x10, waiting for transfers between devices, passed_along(): return lax.ppermute(block, axis, route)  130 us
    dot_general x60, matrix products, span_step(): jnp.einsum('tn,hpn->thp', span_c, carried, precision=exact_mode)  114 us
  transfers between devices with their start and end apart: 24, of which 12 were waited for; matrix products, arithmetic and copies ran while one was open for 15% of the time, Pallas kernels for 0%

commit v1 on v0

v1 whole, which is shorter than its diff:
```python
from functools import partial

import jax
import jax.numpy as jnp
from jax import lax
from jax.experimental import pallas as pl
from jax.experimental.pallas import tpu as pltpu
from jax.sharding import PartitionSpec as P

INNER = 3072
CONV = 4
CHUNK = 128
LANES = 128
ROWS = 256

epsilon = 1e-05
exact = lax.Precision.HIGHEST
f32 = jnp.float32
bf16 = jnp.bfloat16


def dot_nn(left, right, precision=None):
    return lax.dot_general(
        left, right, (((1,), (0,)), ((), ())), precision=precision, preferred_element_type=f32
    )


def dot_nt(left, right, precision=None):
    return lax.dot_general(
        left, right, (((1,), (1,)), ((), ())), precision=precision, preferred_element_type=f32
    )


def dot_tn(left, right):
    return lax.dot_general(left, right, (((0,), (0,)), ((), ())), preferred_element_type=f32)


def silu_parts(values):
    gate = jax.nn.sigmoid(values)
    return gate, values * gate


def silu_slope(values, gate):
    return gate * (1.0 + values * (1.0 - gate))


def head_groups(width, heads):
    head_width = width // heads
    per_group = max(LANES // head_width, 1)
    found = []
    for first in range(0, heads, per_group):
        count = min(per_group, heads - first)
        found.append((first, count, first * head_width, count * head_width))
    return found


def spread(tile, first, count, lanes):
    rows = tile.shape[0]
    head_width = lanes // count
    out = jnp.broadcast_to(tile[:, first : first + 1], (rows, lanes))
    lane = lax.broadcasted_iota(jnp.int32, (rows, lanes), 1)
    for k in range(1, count):
        column = jnp.broadcast_to(tile[:, first + k : first + k + 1], (rows, lanes))
        out = jnp.where(lane >= k * head_width, column, out)
    return out


def own_lanes(tile, k, count):
    if count == 1:
        return tile
    head_width = tile.shape[1] // count
    lane = lax.broadcasted_iota(jnp.int32, tile.shape, 1)
    inside = (lane >= k * head_width) & (lane < (k + 1) * head_width)
    return jnp.where(inside, tile, jnp.zeros_like(tile))


def triangle(keep):
    row = lax.broadcasted_iota(jnp.int32, (CHUNK, CHUNK), 0)
    column = lax.broadcasted_iota(jnp.int32, (CHUNK, CHUNK), 1)
    return keep(row, column)


def conv_kernel(
    heads,
    raw_x,
    raw_bc,
    edge_x,
    edge_bc,
    step_raw,
    dt_bias,
    rate,
    taps_x,
    taps_bc,
    pre_x,
    pre_bc,
    act_x,
    act_bc,
    dt_out,
    run_out,
    end_out,
    total_out,
    ext_x,
    ext_bc,
):
    step = pl.program_id(0)
    groups = head_groups(raw_x.shape[1], heads)
    state = act_bc.shape[1] // 2

    @pl.when(step == 0)
    def _():
        ext_x[0:8] = edge_x[...]
        ext_bc[0:8] = edge_bc[...]
        end_out[...] = jnp.zeros_like(end_out)
        total_out[...] = jnp.zeros_like(total_out)

    @pl.when(step > 0)
    def _():
        ext_x[0:8] = ext_x[ROWS : ROWS + 8]
        ext_bc[0:8] = ext_bc[ROWS : ROWS + 8]

    ext_x[8:] = raw_x[...].astype(f32)
    ext_bc[8:] = raw_bc[...].astype(f32)
    for ext, taps, pre, act in ((ext_x, taps_x, pre_x, act_x), (ext_bc, taps_bc, pre_bc, act_bc)):
        total = ext[5 : 5 + ROWS] * taps[0:1]
        for k in range(1, CONV):
            total = total + ext[5 + k : 5 + k + ROWS] * taps[k : k + 1]
        pre[...] = total.astype(bf16)
        act[...] = silu_parts(total)[1].astype(bf16)
    sizes = jax.nn.softplus(step_raw[...] + dt_bias[...])
    dt_out[...] = sizes
    lower = triangle(lambda t, s: t >= s).astype(f32)
    for sub in range(ROWS // CHUNK):
        at = slice(sub * CHUNK, (sub + 1) * CHUNK)
        dt = sizes[at]
        run = dot_nn(lower, dt * rate[...], exact)
        run_out[at] = run
        last = run[CHUNK - 1 : CHUNK]
        weight = jnp.exp(last - run) * dt
        decay = jnp.exp(last)
        b_turned = act_bc[at, :state].astype(f32).T.astype(bf16)
        for first, count, lane, lanes in groups:
            cols = slice(lane, lane + lanes)
            scaled = act_x[at, cols].astype(f32) * spread(weight, first, count, lanes)
            end_out[:, cols] = spread(decay, first, count, lanes) * end_out[:, cols] + dot_nn(
                b_turned, scaled.astype(bf16)
            )
        total_out[...] += jnp.broadcast_to(last, total_out.shape)


def full(shape):
    return pl.BlockSpec(shape, lambda i: (0,) * len(shape))


def rows_of(width, back=0):
    if back:
        return pl.BlockSpec((ROWS, width), lambda i: (back - 1 - i, 0))
    return pl.BlockSpec((ROWS, width), lambda i: (i, 0))


def params():
    return pltpu.CompilerParams(
        dimension_semantics=("arbitrary",), vmem_limit_bytes=48 * 1024 * 1024
    )


def conv_forward(heads, raw_x, raw_bc, edge_x, edge_bc, step_raw, dt_bias, rate, taps_x, taps_bc):
    count, width = raw_x.shape
    shared = raw_bc.shape[1]
    state = shared // 2
    return pl.pallas_call(
        partial(conv_kernel, heads),
        grid=(count // ROWS,),
        in_specs=[
            rows_of(width),
            rows_of(shared),
            full((8, width)),
            full((8, shared)),
            rows_of(LANES),
            full((1, LANES)),
            full((1, LANES)),
            full((CONV, width)),
            full((CONV, shared)),
        ],
        out_specs=[
            rows_of(width),
            rows_of(shared),
            rows_of(width),
            rows_of(shared),
            rows_of(LANES),
            rows_of(LANES),
            full((state, width)),
            full((8, LANES)),
        ],
        out_shape=[
            jax.ShapeDtypeStruct((count, width), bf16),
            jax.ShapeDtypeStruct((count, shared), bf16),
            jax.ShapeDtypeStruct((count, width), bf16),
            jax.ShapeDtypeStruct((count, shared), bf16),
            jax.ShapeDtypeStruct((count, LANES), f32),
            jax.ShapeDtypeStruct((count, LANES), f32),
            jax.ShapeDtypeStruct((state, width), f32),
            jax.ShapeDtypeStruct((8, LANES), f32),
        ],
        scratch_shapes=[
            pltpu.VMEM((8 + ROWS, width), f32),
            pltpu.VMEM((8 + ROWS, shared), f32),
        ],
        compiler_params=params(),
        cost_estimate=pl.CostEstimate(
            flops=2 * count * width * state,
            bytes_accessed=count * (width + shared) * 6,
            transcendentals=count * (width + shared),
        ),
        name="conv_forward",
    )(raw_x, raw_bc, edge_x, edge_bc, step_raw, dt_bias, rate, taps_x, taps_bc)


def mix_kernel(
    heads,
    act_x,
    act_bc,
    dt_in,
    run_in,
    gate_in,
    start,
    skip,
    gain,
    grad_in,
    mixed_out,
    scaled_out,
    sums_out,
    states_out,
    held,
):
    step = pl.program_id(0)
    groups = head_groups(act_x.shape[1], heads)
    state = act_bc.shape[1] // 2

    @pl.when(step == 0)
    def _():
        held[...] = start[...]

    causal = triangle(lambda t, s: t >= s)
    ones = jnp.ones((8, LANES), f32)
    for sub in range(ROWS // CHUNK):
        at = slice(sub * CHUNK, (sub + 1) * CHUNK)
        dt = dt_in[at]
        run = run_in[at]
        last = run[CHUNK - 1 : CHUNK]
        to_end = jnp.exp(last - run)
        decay = jnp.exp(last)
        turned = run.T
        b_part = act_bc[at, :state]
        c_part = act_bc[at, state:]
        b_turned = b_part.astype(f32).T.astype(bf16)
        product = dot_nt(c_part, b_part)
        states_out[sub] = held[...].astype(bf16)
        squares = jnp.zeros((CHUNK, LANES), f32)
        pairs = jnp.zeros((CHUNK, LANES), f32)
        for first, count, lane, lanes in groups:
            cols = slice(lane, lane + lanes)
            x_part = act_x[at, cols].astype(f32)
            stepped = x_part * spread(dt, first, count, lanes)
            low = stepped.astype(bf16)
            weights = []
            stacked = []
            for k in range(count):
                h = first + k
                gap = jnp.broadcast_to(run[:, h : h + 1], (CHUNK, CHUNK)) - turned[h : h + 1]
                factor = jnp.exp(jnp.where(causal, gap, -jnp.inf))
                weights.append((product * factor).astype(bf16))
                stacked.append(own_lanes(low, k, count))
            mixed = dot_nn(jnp.concatenate(weights, axis=1), jnp.concatenate(stacked, axis=0))
            before = held[:, cols]
            mixed = mixed + jnp.exp(spread(run, first, count, lanes)) * dot_nn(
                c_part, before.astype(bf16)
            )
            mixed = mixed + skip[:, cols] * x_part
            held[:, cols] = spread(decay, first, count, lanes) * before + dot_nn(
                b_turned, (stepped * spread(to_end, first, count, lanes)).astype(bf16)
            )
            gated = mixed * silu_parts(gate_in[at, cols])[1]
            scaled = (gated * gain[:, cols]).astype(bf16)
            mixed_out[at, cols] = mixed.astype(bf16)
            scaled_out[at, cols] = scaled
            square = gated * gated
            pair = scaled.astype(f32) * grad_in[at, cols]
            if lanes < LANES:
                fill = jnp.zeros((CHUNK, LANES - lanes), f32)
                square = jnp.concatenate([square, fill], axis=1)
                pair = jnp.concatenate([pair, fill], axis=1)
            squares = squares + square
            pairs = pairs + pair
        square_row = dot_nt(ones, squares, exact)
        pair_row = dot_nt(ones, pairs, exact)
        row = lax.broadcasted_iota(jnp.int32, (8, CHUNK), 0)
        sums_out[:, at] = jnp.where(row == 0, square_row, pair_row)


def mix_forward(heads, act_x, act_bc, dt, run, gate_in, start, skip, gain, grad_in):
    count, width = act_x.shape
    shared = act_bc.shape[1]
    state = shared // 2
    subs = ROWS // CHUNK
    return pl.pallas_call(
        partial(mix_kernel, heads),
        grid=(count // ROWS,),
        in_specs=[
            rows_of(width),
            rows_of(shared),
            rows_of(LANES),
            rows_of(LANES),
            rows_of(width),
            full((state, width)),
            full((1, width)),
            full((1, width)),
            rows_of(width),
        ],
        out_specs=[
            rows_of(width),
            rows_of(width),
            pl.BlockSpec((8, ROWS), lambda i: (0, i)),
            pl.BlockSpec((subs, state, width), lambda i: (i, 0, 0)),
        ],
        out_shape=[
            jax.ShapeDtypeStruct((count, width), bf16),
            jax.ShapeDtypeStruct((count, width), bf16),
            jax.ShapeDtypeStruct((8, count), f32),
            jax.ShapeDtypeStruct((count // CHUNK, state, width), bf16),
        ],
        scratch_shapes=[pltpu.VMEM((state, width), f32)],
        compiler_params=params(),
        cost_estimate=pl.CostEstimate(
            flops=8 * count * width * state,
            bytes_accessed=count * width * 16,
            transcendentals=count * heads * CHUNK,
        ),
        name="mix_forward",
    )(act_x, act_bc, dt, run, gate_in, start, skip, gain, grad_in)


def gate_kernel(
    heads,
    grad_in,
    scales,
    gate_in,
    mixed_in,
    act_x,
    act_bc,
    run_in,
    gain,
    grad_mixed,
    grad_gate,
    gain_sum,
    skip_sum,
    adjoint,
):
    groups = head_groups(act_x.shape[1], heads)
    state = act_bc.shape[1] // 2

    @pl.when(pl.program_id(0) == 0)
    def _():
        gain_sum[...] = jnp.zeros_like(gain_sum)
        skip_sum[...] = jnp.zeros_like(skip_sum)
        adjoint[...] = jnp.zeros_like(adjoint)

    for sub in reversed(range(ROWS // CHUNK)):
        at = slice(sub * CHUNK, (sub + 1) * CHUNK)
        run = run_in[at]
        grown = jnp.exp(run)
        decay = grown[CHUNK - 1 : CHUNK]
        c_turned = act_bc[at, state:].astype(f32).T.astype(bf16)
        row_scale = scales[at, 0:1]
        row_pull = scales[at, 1:2]
        for first, count, lane, lanes in groups:
            cols = slice(lane, lane + lanes)
            gate = gate_in[at, cols]
            mixed = mixed_in[at, cols].astype(f32)
            share, active = silu_parts(gate)
            gated = mixed * active
            d_scaled = grad_in[at, cols] * row_scale
            d_gated = d_scaled * gain[:, cols] - row_pull * gated
            d_mixed = d_gated * active
            low = d_mixed.astype(bf16)
            grad_mixed[at, cols] = low
            grad_gate[at, cols] = (d_gated * mixed * silu_slope(gate, share)).astype(bf16)
            gain_sum[0:1, cols] += jnp.sum(d_scaled * gated, axis=0, keepdims=True)
            skip_sum[0:1, cols] += jnp.sum(
                d_mixed * act_x[at, cols].astype(f32), axis=0, keepdims=True
            )
            adjoint[:, cols] = spread(decay, first, count, lanes) * adjoint[:, cols] + dot_nn(
                c_turned, (d_mixed * spread(grown, first, count, lanes)).astype(bf16)
            )


def gate_backward(heads, grad_in, scales, gate_in, mixed, act_x, act_bc, run, gain):
    count, width = act_x.shape
    shared = act_bc.shape[1]
    state = shared // 2
    steps = count // ROWS
    return pl.pallas_call(
        partial(gate_kernel, heads),
        grid=(steps,),
        in_specs=[
            rows_of(width, steps),
            rows_of(2, steps),
            rows_of(width, steps),
            rows_of(width, steps),
            rows_of(width, steps),
            rows_of(shared, steps),
            rows_of(LANES, steps),
            full((1, width)),
        ],
        out_specs=[
            rows_of(width, steps),
            rows_of(width, steps),
            full((8, width)),
            full((8, width)),
            full((state, width)),
        ],
        out_shape=[
            jax.ShapeDtypeStruct((count, width), bf16),
            jax.ShapeDtypeStruct((count, width), bf16),
            jax.ShapeDtypeStruct((8, width), f32),
            jax.ShapeDtypeStruct((8, width), f32),
            jax.ShapeDtypeStruct((state, width), f32),
        ],
        compiler_params=params(),
        cost_estimate=pl.CostEstimate(
            flops=2 * count * width * state,
            bytes_accessed=count * width * 16,
            transcendentals=count * width,
        ),
        name="gate_backward",
    )(grad_in, scales, gate_in, mixed, act_x, act_bc, run, gain)


def states_kernel(
    heads,
    grad_mixed,
    act_x,
    act_bc,
    pre_x,
    pre_bc,
    raw_x,
    raw_bc,
    edge_x,
    edge_bc,
    dt_in,
    run_in,
    step_raw,
    dt_bias,
    rate_rows,
    states_in,
    end_in,
    skip,
    taps_x,
    taps_bc,
    members,
    d_raw_x,
    d_raw_bc,
    d_step,
    tail_x,
    tail_bc,
    back_x,
    back_bc,
    tap_sum_x,
    tap_sum_bc,
    rate_sum,
    bias_sum,
    adjoint,
    d_pre_x,
    d_pre_bc,
    rows_ref,
    inside_ref,
    carry_ref,
    square_ref,
):
    step = pl.program_id(0)
    steps = pl.num_programs(0)
    groups = head_groups(act_x.shape[1], heads)
    state = act_bc.shape[1] // 2
    padded = members.shape[0]

    @pl.when(step == 0)
    def _():
        adjoint[...] = end_in[...]
        d_pre_x[8:16] = jnp.zeros((8, d_pre_x.shape[1]), f32)
        d_pre_bc[8:16] = jnp.zeros((8, d_pre_bc.shape[1]), f32)
        tap_sum_x[...] = jnp.zeros_like(tap_sum_x)
        tap_sum_bc[...] = jnp.zeros_like(tap_sum_bc)
        rate_sum[...] = jnp.zeros_like(rate_sum)
        bias_sum[...] = jnp.zeros_like(bias_sum)
        rows_ref[...] = jnp.zeros_like(rows_ref)
        square_ref[...] = jnp.zeros_like(square_ref)

    upto = triangle(lambda s, t: s <= t)
    not_before = triangle(lambda s, t: s >= t).astype(f32)
    before = triangle(lambda s, t: s < t).astype(f32)
    ones = jnp.ones((8, CHUNK), bf16)
    for sub in reversed(range(ROWS // CHUNK)):
        at = slice(sub * CHUNK, (sub + 1) * CHUNK)
        dt = dt_in[at]
        run = run_in[at]
        last = run[CHUNK - 1 : CHUNK]
        grown = jnp.exp(run)
        decay = grown[CHUNK - 1 : CHUNK]
        to_end = jnp.exp(last - run)
        run_turned = run.T
        dt_turned = dt.T[0:padded]
        high = dt_turned.astype(bf16)
        rest = dt_turned - high.astype(f32)
        middle = rest.astype(bf16)
        low_part = (rest - middle.astype(f32)).astype(bf16)
        dt_split = jnp.concatenate([high, middle, low_part], axis=0)
        b_part = act_bc[at, :state]
        c_part = act_bc[at, state:]
        c_turned = c_part.astype(f32).T.astype(bf16)
        product = dot_nt(b_part, c_part)
        d_product = jnp.zeros((CHUNK, CHUNK), f32)
        d_b = jnp.zeros((CHUNK, state), f32)
        d_c = jnp.zeros((CHUNK, state), f32)
        d_pre_x[CHUNK + 8 : CHUNK + 16] = d_pre_x[8:16]
        d_pre_bc[CHUNK + 8 : CHUNK + 16] = d_pre_bc[8:16]
        through = []
        for first, count, lane, lanes in groups:
            cols = slice(lane, lane + lanes)
            x_low = act_x[at, cols]
            x_part = x_low.astype(f32)
            dy_low = grad_mixed[at, cols]
            dy = dy_low.astype(f32)
            dt_wide = spread(dt, first, count, lanes)
            ending = spread(to_end, first, count, lanes)
            growing = spread(grown, first, count, lanes)
            lam = adjoint[:, cols]
            lam_low = lam.astype(bf16)
            held_low = states_in[sub][:, cols]
            weights = []
            stacked = []
            for k in range(count):
                h = first + k
                gap = run_turned[h : h + 1] - jnp.broadcast_to(run[:, h : h + 1], (CHUNK, CHUNK))
                factor = jnp.exp(jnp.where(upto, gap, -jnp.inf))
                weights.append((product * factor).astype(bf16))
                stacked.append(own_lanes(dy_low, k, count))
                paired = dot_nt(own_lanes(x_low, k, count), dy_low) * factor
                d_product = d_product + paired * jnp.broadcast_to(dt[:, h : h + 1], (CHUNK, CHUNK))
                inside = (paired * product).astype(bf16)
                split_rows = dot_nn(dt_split, inside)
                rows_ref[h : h + 1] = (
                    split_rows[h : h + 1]
                    + split_rows[padded + h : padded + h + 1]
                    + split_rows[2 * padded + h : 2 * padded + h + 1]
                )
                inside_ref[h : h + 1] = dot_nt(ones, inside)[0:1]
            d_stepped = dot_nn(jnp.concatenate(weights, axis=1), jnp.concatenate(stacked, axis=0))
            from_end = ending * dot_nn(b_part, lam_low)
            d_x = dt_wide * (d_stepped + from_end) + skip[:, cols] * dy
            dy_grown = dy * growing
            dy_grown_low = dy_grown.astype(bf16)
            carry_ref[0, :, cols] = (x_part * from_end).astype(bf16)
            carry_ref[1, :, cols] = (dy_grown * dot_nn(c_part, held_low)).astype(bf16)
            d_b = d_b + dot_nt((x_part * dt_wide * ending).astype(bf16), lam_low)
            d_c = d_c + dot_nt(dy_grown_low, held_low)
            wide_decay = spread(decay, first, count, lanes)
            lam_decayed = wide_decay * lam
            through.append(
                jnp.sum(lam_decayed * held_low.astype(f32), axis=0, keepdims=True)
            )
            adjoint[:, cols] = lam_decayed + dot_nn(c_turned, dy_grown_low)
            pre = pre_x[at, cols].astype(f32)
            d_pre_x[8 : CHUNK + 8, cols] = d_x * silu_slope(pre, jax.nn.sigmoid(pre))
        member = members[...]
        kept = dot_nt(member, carry_ref[0])
        fed = dot_nt(member, carry_ref[1])
        wide_row = jnp.concatenate(through, axis=1)
        across = dot_nt(member.astype(f32), jnp.broadcast_to(wide_row, (8, wide_row.shape[1])), exact)
        inside_rows = inside_ref[...]
        d_log = (
            dot_nn(rows_ref[...] - dt_turned * inside_rows + fed, not_before, exact)
            + dot_nn(dt_turned * kept, before, exact)
            + across[:, 0:1]
        )
        d_log_rate = d_log * rate_rows[...]
        rate_sum[...] += d_log_rate * dt_turned
        square_ref[0:padded] = d_log_rate + inside_rows + kept
        d_step_exact = square_ref[...].T * jax.nn.sigmoid(step_raw[at] + dt_bias[...])
        bias_sum[0:1] += jnp.sum(d_step_exact, axis=0, keepdims=True)
        d_step[at] = d_step_exact.astype(bf16)
        d_product_low = d_product.astype(bf16)
        d_b = d_b + dot_nn(d_product_low, c_part)
        d_c = d_c + dot_nn(d_product.T.astype(bf16), b_part)
        pre = pre_bc[at].astype(f32)
        slope = silu_slope(pre, jax.nn.sigmoid(pre))
        d_pre_bc[8 : CHUNK + 8, :state] = d_b * slope[:, :state]
        d_pre_bc[8 : CHUNK + 8, state:] = d_c * slope[:, state:]
        for d_pre, raw, taps, d_raw, tap_sum, tail in (
            (d_pre_x, raw_x, taps_x, d_raw_x, tap_sum_x, tail_x),
            (d_pre_bc, raw_bc, taps_bc, d_raw_bc, tap_sum_bc, tail_bc),
        ):
            values = raw[at].astype(f32)
            total = jnp.zeros_like(values)
            for k in range(CONV):
                moved = d_pre[11 - k : 11 - k + CHUNK]
                total = total + moved * taps[k : k + 1]
                tap_sum[k : k + 1] += jnp.sum(values * moved, axis=0, keepdims=True)
            d_raw[at] = total.astype(bf16)
            if sub == ROWS // CHUNK - 1:

                @pl.when(step == 0)
                def _():
                    tail[...] = total[CHUNK - 8 :]

    @pl.when(step == steps - 1)
    def _():
        for d_pre, edge, taps, tap_sum, back in (
            (d_pre_x, edge_x, taps_x, tap_sum_x, back_x),
            (d_pre_bc, edge_bc, taps_bc, tap_sum_bc, back_bc),
        ):
            d_pre[0:8] = jnp.zeros((8, d_pre.shape[1]), f32)
            values = edge[...]
            total = jnp.zeros_like(values)
            for k in range(CONV):
                moved = d_pre[3 - k : 11 - k]
                total = total + moved * taps[k : k + 1]
                tap_sum[k : k + 1] += jnp.sum(values * moved, axis=0, keepdims=True)
            back[...] = total


def states_backward(
    heads,
    grad_mixed,
    act_x,
    act_bc,
    pre_x,
    pre_bc,
    raw_x,
    raw_bc,
    edge_x,
    edge_bc,
    dt,
    run,
    step_raw,
    dt_bias,
    rate,
    states,
    end,
    skip,
    taps_x,
    taps_bc,
):
    count, width = act_x.shape
    shared = act_bc.shape[1]
    state = shared // 2
    steps = count // ROWS
    subs = ROWS // CHUNK
    padded = -(-heads // 16) * 16
    head_of = jnp.arange(width)[None, :] // (width // heads)
    members = (jnp.arange(padded)[:, None] == head_of).astype(bf16)
    rate_rows = jnp.broadcast_to(rate[0, :padded, None], (padded, CHUNK))
    return pl.pallas_call(
        partial(states_kernel, heads),
        grid=(steps,),
        in_specs=[
            rows_of(width, steps),
            rows_of(width, steps),
            rows_of(shared, steps),
            rows_of(width, steps),
            rows_of(shared, steps),
            rows_of(width, steps),
            rows_of(shared, steps),
            full((8, width)),
            full((8, shared)),
            rows_of(LANES, steps),
            rows_of(LANES, steps),
            rows_of(LANES, steps),
            full((1, LANES)),
            full((padded, CHUNK)),
            pl.BlockSpec((subs, state, width), lambda i: (steps - 1 - i, 0, 0)),
            full((state, width)),
            full((1, width)),
            full((CONV, width)),
            full((CONV, shared)),
            full((padded, width)),
        ],
        out_specs=[
            rows_of(width, steps),
            rows_of(shared, steps),
            rows_of(LANES, steps),
            full((8, width)),
            full((8, shared)),
            full((8, width)),
            full((8, shared)),
            full((8, width)),
            full((8, shared)),
            full((padded, CHUNK)),
            full((8, LANES)),
        ],
        out_shape=[
            jax.ShapeDtypeStruct((count, width), bf16),
            jax.ShapeDtypeStruct((count, shared), bf16),
            jax.ShapeDtypeStruct((count, LANES), bf16),
            jax.ShapeDtypeStruct((8, width), f32),
            jax.ShapeDtypeStruct((8, shared), f32),
            jax.ShapeDtypeStruct((8, width), f32),
            jax.ShapeDtypeStruct((8, shared), f32),
            jax.ShapeDtypeStruct((8, width), f32),
            jax.ShapeDtypeStruct((8, shared), f32),
            jax.ShapeDtypeStruct((padded, CHUNK), f32),
            jax.ShapeDtypeStruct((8, LANES), f32),
        ],
        scratch_shapes=[
            pltpu.VMEM((state, width), f32),
            pltpu.VMEM((CHUNK + 16, width), f32),
            pltpu.VMEM((CHUNK + 16, shared), f32),
            pltpu.VMEM((padded, CHUNK), f32),
            pltpu.VMEM((padded, CHUNK), f32),
            pltpu.VMEM((2, CHUNK, width), bf16),
            pltpu.VMEM((CHUNK, CHUNK), f32),
        ],
        compiler_params=params(),
        cost_estimate=pl.CostEstimate(
            flops=20 * count * width * state,
            bytes_accessed=count * width * 16,
            transcendentals=count * heads * CHUNK * 2,
        ),
        name="states_backward",
    )(
        grad_mixed,
        act_x,
        act_bc,
        pre_x,
        pre_bc,
        raw_x,
        raw_bc,
        edge_x,
        edge_bc,
        dt,
        run,
        step_raw,
        dt_bias,
        rate_rows,
        states,
        end,
        skip,
        taps_x,
        taps_bc,
        members,
    )


def moved_along(block, axis, distance):
    size = lax.axis_size(axis)
    route = [(i - distance, i) for i in range(size) if 0 <= i - distance < size]
    return lax.ppermute(block, axis, route)


def swapped(block):
    return lax.ppermute(block, "section", [(0, 1), (1, 0)])


def both_blocks(weight):
    size = lax.axis_size("seq")
    rows = weight.shape[0] // size
    part = lax.dynamic_slice_in_dim(weight, lax.axis_index("seq") * rows, rows, 0)
    return lax.all_gather(part, ("section", "seq"), axis=0, tiled=True).reshape(
        (lax.axis_size("section"),) + weight.shape
    )


def entering(end, total, forward):
    size = lax.axis_size("seq")
    place = lax.axis_index("seq")
    ends = lax.all_gather(end.astype(bf16), "seq")
    totals = lax.all_gather(total, "seq")
    state = jnp.zeros_like(end)
    order = range(size) if forward else reversed(range(size))
    for other in order:
        ahead = other < place if forward else other > place
        new = jnp.exp(totals[other])[None, :] * state + ends[other].astype(f32)
        state = jnp.where(ahead, new, state)
    return state


def padded_edge(edge):
    return jnp.pad(edge.astype(f32), ((8 - edge.shape[0], 0), (0, 0)))


def block_forward(x, rescale, normed, weights, grad_in):
    heads = weights["a_log"].shape[0]
    width = weights["w_x"].shape[1]
    raw_x = dot_nn(normed, weights["w_x"]).astype(bf16)
    raw_bc = dot_nn(normed, weights["w_bc"]).astype(bf16)
    step_raw = dot_nn(normed, weights["w_dt"])
    edge = jnp.concatenate([raw_x[-(CONV - 1) :], raw_bc[-(CONV - 1) :]], axis=1)
    edge = padded_edge(moved_along(edge, "seq", 1))
    edge_x, edge_bc = edge[:, :width], edge[:, width:]
    gate_in = dot_nn(normed, weights["w_z"])
    pre_x, pre_bc, act_x, act_bc, dt, run, end, total = conv_forward(
        heads, raw_x, raw_bc, edge_x, edge_bc, step_raw, weights["dt_bias"], weights["rate"],
        weights["taps_x"], weights["taps_bc"],
    )
    wide_total = jnp.repeat(total[0, :heads], width // heads)
    start = entering(end, wide_total, True)
    mixed, scaled, sums, states = mix_forward(
        heads, act_x, act_bc, dt, run, gate_in, start, weights["skip"], weights["gain"], grad_in
    )
    kept = dict(
        raw_x=raw_x, raw_bc=raw_bc, step_raw=step_raw, edge_x=edge_x, edge_bc=edge_bc,
        gate_in=gate_in, pre_x=pre_x, pre_bc=pre_bc, act_x=act_x, act_bc=act_bc, dt=dt, run=run,
        wide_total=wide_total, mixed=mixed, scaled=scaled, states=states, normed=normed,
        rescale=rescale,
    )
    part = dot_nt(scaled, weights["w_out"]).astype(bf16)
    return part, sums[0:2], kept


def block_backward(grad, grad_in, row_scale, d_row, kept, weights):
    heads = weights["a_log"].shape[0]
    width = weights["w_x"].shape[1]
    count = grad.shape[0]
    pull = d_row * row_scale * row_scale * row_scale / INNER
    grad_mixed, grad_gate, gain_sum, skip_sum, adjoint = gate_backward(
        heads, grad_in, jnp.stack([row_scale, pull], axis=1), kept["gate_in"], kept["mixed"],
        kept["act_x"], kept["act_bc"], kept["run"], weights["gain"],
    )
    end = entering(adjoint, kept["wide_total"], False)
    (
        d_raw_x, d_raw_bc, d_step, tail_x, tail_bc, back_x, back_bc, taps_x, taps_bc, rate_sum,
        bias_sum,
    ) = states_backward(
        heads, grad_mixed, kept["act_x"], kept["act_bc"], kept["pre_x"], kept["pre_bc"],
        kept["raw_x"], kept["raw_bc"], kept["edge_x"], kept["edge_bc"], kept["dt"], kept["run"],
        kept["step_raw"], weights["dt_bias"], weights["rate"], kept["states"], end,
        weights["skip"], weights["taps_x"], weights["taps_bc"],
    )
    back = moved_along(jnp.concatenate([back_x, back_bc], axis=1), "seq", -1)
    d_raw_x = d_raw_x.at[count - 8 :].set((tail_x + back[:, :width]).astype(bf16))
    d_raw_bc = d_raw_bc.at[count - 8 :].set((tail_bc + back[:, width:]).astype(bf16))
    normed = kept["normed"]
    d_summed = (row_scale[:, None] * grad.astype(f32)).astype(bf16)
    grads = dict(
        w_out=dot_tn(d_summed, kept["scaled"]).astype(bf16),
        w_z=dot_tn(normed, grad_gate).astype(bf16),
        w_x=dot_tn(normed, d_raw_x).astype(bf16),
        w_bc=dot_tn(normed, d_raw_bc).astype(bf16),
        w_dt=dot_tn(normed, d_step)[:, :heads].astype(bf16),
        conv_x=taps_x[:CONV],
        conv_bc=taps_bc[:CONV],
        dt_bias=bias_sum[0, :heads],
        a_log=jnp.sum(rate_sum[:heads], axis=1),
        skip=jnp.sum(skip_sum[0].reshape(heads, width // heads), axis=1),
        gain=gain_sum[0],
    )
    part = (
        dot_nt(grad_gate, weights["w_z"])
        + dot_nt(d_raw_x, weights["w_x"])
        + dot_nt(d_step, weights["w_dt"])
    ).astype(bf16)
    return jnp.concatenate([part, d_raw_bc], axis=1), grads


def norm_forward(x, gain):
    rescale = lax.rsqrt(jnp.mean(x * x, axis=-1, keepdims=True) + epsilon)
    return rescale, (x * rescale * gain).astype(bf16)


def norm_backward(share, x, rescale, grad, gain, w_bc):
    width = x.shape[1]
    d_normed = share[:, :width].astype(f32) + dot_nt(share[:, width:], w_bc)
    unit = x * rescale
    h = d_normed * gain
    gain_part = jnp.sum(d_normed * unit, axis=0)
    out = grad + rescale * (h - unit * jnp.mean(h * unit, axis=-1, keepdims=True))
    return out.astype(bf16), gain_part


def shards(
    tokens, cotangent, norm_gain, w_z, w_x, w_bc, w_dt, conv_x, conv_bc, dt_bias, a_log, skip_d,
    gate_gain, w_out,
):
    section = lax.axis_index("section")
    count, model = tokens.shape[1:]
    head_size = lax.axis_size("head")
    head_at = lax.axis_index("head")
    heads = a_log.shape[1]
    width = w_x.shape[2]
    share = model // head_size
    row_share = count // head_size
    gathered = dict(
        w_x=both_blocks(w_x[0]),
        w_bc=both_blocks(w_bc[0]),
        w_dt=both_blocks(jnp.pad(w_dt[0], ((0, 0), (0, LANES - heads)))),
        w_z=both_blocks(w_z[0]),
        w_out=both_blocks(w_out[0]),
    )
    small = lax.all_gather(
        jnp.concatenate(
            [
                norm_gain[0], conv_x[0].T.reshape(-1), conv_bc[0].T.reshape(-1), dt_bias[0],
                a_log[0], skip_d[0], gate_gain[0],
            ]
        ),
        "section",
    )
    weights = []
    for b in range(2):
        block = {name: value[b] for name, value in gathered.items()}
        at = 0

        def take(size):
            nonlocal at
            at += size
            return small[b, at - size : at]

        block["norm"] = take(model)
        block["taps_x"] = take(CONV * width).reshape(CONV, width)
        block["taps_bc"] = take(CONV * w_bc.shape[2]).reshape(CONV, w_bc.shape[2])
        block["dt_bias"] = jnp.pad(take(heads), (0, LANES - heads))[None]
        block["a_log"] = take(heads)
        block["rate"] = jnp.pad(-jnp.exp(block["a_log"]), (0, LANES - heads))[None]
        block["skip"] = jnp.repeat(take(heads), width // heads)[None]
        block["gain"] = take(width)[None]
        weights.append(block)

    def own_rows(array):
        return lax.dynamic_slice_in_dim(array, head_at * row_share, row_share, 0)

    def own_columns(array):
        return lax.dynamic_slice_in_dim(array, head_at * share, share, 1)

    first_low = lax.dynamic_index_in_dim(tokens, section, 0, False)
    last_grad = lax.dynamic_index_in_dim(cotangent, section, 0, False)
    first = first_low.astype(f32)
    rescale, normed = norm_forward(first, weights[0]["norm"])
    nothing = jnp.zeros((count, width), f32)
    part, sums, kept_first = block_forward(first, rescale, normed, weights[0], nothing)
    squares = lax.psum(sums[0], "head")
    scale_first = lax.rsqrt(squares / INNER + epsilon)
    summed = lax.psum_scatter(part, "head", scatter_dimension=0, tiled=True).astype(f32)
    second_share = (own_rows(first) + own_rows(scale_first)[:, None] * summed).astype(bf16)
    second_low = lax.all_gather(second_share, "head", axis=0, tiled=True)
    second = second_low.astype(f32)

    grad_second = dot_nn(last_grad, weights[1]["w_out"])
    rescale, normed = norm_forward(second, weights[1]["norm"])
    part, sums, kept_second = block_forward(second, rescale, normed, weights[1], grad_second)
    squares, d_row = lax.psum(sums, "head")
    scale_second = lax.rsqrt(squares / INNER + epsilon)
    summed = lax.psum_scatter(part, "head", scatter_dimension=1, tiled=True).astype(f32)
    last_share = (own_columns(second) + scale_second[:, None] * summed).astype(bf16)

    part, grads_second = block_backward(
        last_grad, grad_second, scale_second, d_row, kept_second, weights[1]
    )
    part = lax.psum_scatter(part, "head", scatter_dimension=0, tiled=True)
    middle_share, norm_second = norm_backward(
        part, own_rows(second), own_rows(kept_second["rescale"]), own_rows(last_grad).astype(f32),
        weights[1]["norm"], weights[1]["w_bc"],
    )
    middle_grad = lax.all_gather(middle_share, "head", axis=0, tiled=True)

    grad_first = dot_nn(middle_grad, weights[0]["w_out"])
    d_row = jnp.sum(middle_grad.astype(f32) * (second - first), axis=1) / scale_first
    part, grads_first = block_backward(
        middle_grad, grad_first, scale_first, d_row, kept_first, weights[0]
    )
    part = lax.psum_scatter(part, "head", scatter_dimension=0, tiled=True)
    first_share, norm_first = norm_backward(
        part, own_rows(first), own_rows(kept_first["rescale"]), own_rows(middle_grad).astype(f32),
        weights[0]["norm"], weights[0]["w_bc"],
    )

    def to_columns(rows):
        pieces = rows.reshape(row_share, head_size, share).swapaxes(0, 1)
        return lax.all_to_all(pieces, "head", 0, 0).reshape(count, share)

    def by_section(of_first, of_second):
        sent = jnp.where(section == 0, of_second, of_first)
        own = jnp.where(section == 0, of_first, of_second)
        arrived = swapped(sent)
        return jnp.where(
            section == 0, jnp.stack([own, arrived]), jnp.stack([arrived, own])
        )

    block_outputs = by_section(own_columns(second_low), last_share)
    input_grads = by_section(to_columns(first_share), own_columns(middle_grad))

    def summed_rows(name):
        both = jnp.concatenate([grads_first[name], grads_second[name]], axis=0)
        return lax.psum_scatter(both, ("section", "seq"), scatter_dimension=0, tiled=True).astype(
            f32
        )

    shared = [
        lax.psum_scatter(block["w_bc"], "head", scatter_dimension=1, tiled=True)
        for block in (grads_first, grads_second)
    ]
    grads_first["w_bc"], grads_second["w_bc"] = shared
    local = jnp.stack(
        [
            jnp.concatenate(
                [
                    block["conv_x"].reshape(-1), block["dt_bias"], block["a_log"], block["skip"],
                    block["gain"],
                ]
            )
            for block in (grads_first, grads_second)
        ]
    )
    whole = jnp.stack(
        [
            jnp.concatenate([norm, block["conv_bc"].reshape(-1)])
            for norm, block in ((norm_first, grads_first), (norm_second, grads_second))
        ]
    )
    local = lax.dynamic_index_in_dim(lax.psum(local, ("section", "seq")), section, 0, False)
    whole = lax.dynamic_index_in_dim(lax.psum(whole, ("section", "seq", "head")), section, 0, False)
    at = CONV * width
    return (
        block_outputs[None],
        input_grads[None],
        lax.dynamic_slice_in_dim(whole, head_at * share, share, 0)[None],
        summed_rows("w_z")[None],
        summed_rows("w_x")[None],
        summed_rows("w_bc")[None],
        summed_rows("w_dt")[None],
        local[:at].reshape(CONV, width).T[None],
        whole[model:].reshape(CONV, w_bc.shape[2]).T[None],
        local[at : at + heads][None],
        local[at + heads : at + 2 * heads][None],
        local[at + 2 * heads : at + 3 * heads][None],
        local[at + 3 * heads :][None],
        summed_rows("w_out")[None],
    )


def solution(mesh):
    placed = (
        P(None, "seq", None),
        P(None, "seq", None),
        P("section", None),
        P("section", None, "head"),
        P("section", None, "head"),
        P("section", None, None),
        P("section", None, "head"),
        P("section", "head", None),
        P("section", None, None),
        P("section", "head"),
        P("section", "head"),
        P("section", "head"),
        P("section", "head"),
        P("section", None, "head"),
    )
    return jax.shard_map(
        shards,
        mesh=mesh,
        in_specs=placed,
        out_specs=(
            P("section", None, "seq", "head"),
            P("section", None, "seq", "head"),
            P("section", "head"),
            P("section", "seq", "head"),
            P("section", "seq", "head"),
            P("section", "seq", "head"),
            P("section", "seq", "head"),
            P("section", "head", None),
            P("section", None, None),
            P("section", "head"),
            P("section", "head"),
            P("section", "head"),
            P("section", "head"),
            P("section", "seq", "head"),
        ),
        check_vma=False,
    )
```

time: 3890 us -> 1110 us (0.29)
  local copies, waits for them, and re-layouts: 1290 us -> 51.2 us
  matrix products: 774 us -> 121 us
  other arithmetic: 594 us -> 62.9 us
  waiting for transfers between devices: 1010 us -> 566 us
  Pallas kernels: 0 us -> 105 us
    psum x6 -> x0, waiting for transfers between devices: 813 us -> none  [the longest x3 494 us: mixer_forward(): summed, squares = lax.psum((branch_part, part_squares), 'head')]
    dynamic_update_slice x108 -> x0, local copies, waits for them, and re-layouts: 735 us -> none  [local_states(): lax.scan(jax.checkpoint(partial(span_step, decay_rate)), start_state, pie...]
    dot_general x279 -> x30, matrix products: 774 us -> 121 us  [the longest x10 43.6 us: dot_nn(): lax.dot_general(left, right, (((1,), (0,)), ((), ())), precision=precisio...]
    reduce_scatter x3 -> x8, waiting for transfers between devices: 57.6 us -> 312 us  [the longest x3 162 us: summed_rows(): lax.psum_scatter(both, ('section', 'seq'), scatter_dimension=0, tiled=True)]
    another operation x213 -> x5, other arithmetic: 218 us -> 2.14 us  [the longest x1 2.06 us: by_section(): jnp.stack([own, arrived])]
    another operation x291 -> x16, local copies, waits for them, and re-layouts: 207 us -> 2.47 us  [the longest x2 1.25 us: block_backward(): jnp.stack([row_scale, pull], axis=1)]
    all_gather x3 -> x6, waiting for transfers between devices: 11.4 us -> 185 us  [the longest x4 68 us: both_blocks(): lax.all_gather(part, ('section', 'seq'), axis=0, tiled=True)]
    reduce_sum x44 -> x7, other arithmetic: 132 us -> 10.9 us  [the longest x2 5.3 us: norm_forward(): rescale = lax.rsqrt(jnp.mean(x * x, axis=-1, keepdims=True) + epsilon)]
  transfers between devices with their start and end apart: 24 -> 24, of which waited for: 12 -> 15; matrix products, arithmetic and copies ran while one was open for 15% -> 16% of each run, Pallas kernels for 0% -> 5%
where the time goes in v1:
time: 1110 us; the launch traced here: 1100 us
  waiting for transfers between devices  566 us (51%)
  blocking collectives  159 us (14%)
  matrix products  121 us (11%)
  Pallas kernels  105 us (9%)
  other arithmetic  62.9 us (6%)
  local copies, waits for them, and re-layouts  51.2 us (5%)
  between operations  16.9 us (2%)
  starting transfers between devices  15.5 us (1%)
    reduce_scatter x3, waiting for transfers between devices, summed_rows(): lax.psum_scatter(both, ('section', 'seq'), scatter_dimension=0, tiled=True)  162 us
    reduce_scatter x2, waiting for transfers between devices, shards(): part = lax.psum_scatter(part, 'head', scatter_dimension=0, tiled=True)  106 us
    all_gather x4, waiting for transfers between devices, both_blocks(): lax.all_gather(part, ('section', 'seq'), axis=0, tiled=True)  68 us
    all_gather x1, waiting for transfers between devices, shards(): middle_grad = lax.all_gather(middle_share, 'head', axis=0, tiled=True)  60.1 us
    all_gather x1, waiting for transfers between devices, shards(): second_low = lax.all_gather(second_share, 'head', axis=0, tiled=True)  56.5 us
    pallas_call x2, Pallas kernels, states_backward(): pl.pallas_call(partial(states_kernel, heads), grid=(steps,), in_specs=[ro...  54.2 us
    unnamed x20, waiting for transfers between devices  52.2 us
    dot_general x10, matrix products, dot_nn(): lax.dot_general(left, right, (((1,), (0,)), ((), ())), precision=precisio...  43.6 us
  transfers between devices with their start and end apart: 24, of which 15 were waited for; matrix products, arithmetic and copies ran while one was open for 16% of the time, Pallas kernels for 5%

profile of v1, /device:TPU:0, one launch (start us, length us, event | category | flops | bytes accessed | tf_op | source)
XLA Modules:
  0.0 1096.8 jit_solution(5539547639968772877)
XLA Ops:
  16.1 10.8 all-reduce.7
  30.1 12.3 %all_gather.63 = bf16[3072,128]{0,1:T(8,128)(2,1)S(1)} all-gather(bf16[384,128]{0,1:T(8,128)(2,1)S(1)} %pad_dynamic-slice_fusion), channel_id=1, replica_groups=mesh['section'=2,'seq'=4,'head'=4] {'section','seq'}, dimensions={0}, use_global_device_ids=true | all-gather | bytes 884736 | tf_op jit(solution)/shard_map/all_gather | solution.py:766
  49.0 34.1 %all-gather.22.cloned.1.call-done = bf16[1,3072,768]{2,1,0:T(8,128)(2,1)} async-done(((bf16[1,384,768]{2,1,0:T(8,128)(2,1)}), bf16[1,3072,768]{2,1,0:T(8,128)(2,1)}) %all-gather.22.cloned.1.call-update) | async-done | bytes 4718608 | tf_op jit(solution)/shard_map/all_gather | solution.py:766
  90.6 33.9 %all-gather.26.cloned.1.call-done = bf16[1,3072,768]{2,1,0:T(8,128)(2,1)} async-done(((bf16[1,384,768]{2,1,0:T(8,128)(2,1)}), bf16[1,3072,768]{2,1,0:T(8,128)(2,1)}) %all-gather.26.cloned.1.call-update) | async-done | bytes 4718608 | tf_op jit(solution)/shard_map/all_gather | solution.py:766
  147.0 13.1 %all-gather.4 = bf16[512,768]{1,0:T(8,128)(2,1)S(1)} all-gather(bf16[128,768]{1,0:T(8,128)(2,1)S(1)} %convert_element_type.259), channel_id=6, replica_groups=mesh['section'=2,'seq'=4,'head'=4] {'seq'}, dimensions={0}, use_global_device_ids=true | all-gather | bytes 983040 | tf_op jit(solution)/shard_map/all_gather | solution.py:774
  162.2 10.7 mix_forward.2
  187.1 11.9 %psum.28 = f32[1024]{0:T(1024)S(1)} all-reduce(f32[1024]{0:T(1024)S(1)} %bitcast.227), channel_id=1, replica_groups=mesh['section'=2,'seq'=4,'head'=4] {'head'}, use_global_device_ids=true, to_apply=%region_1.2 | all-reduce | flops 1024 | bytes 8192 | tf_op jit(solution)/shard_map/psum | solution.py:938
  199.1 43.5 %reduce-scatter.18.cloned.1.call-done = bf16[256,1536]{1,0:T(8,128)(2,1)} async-done(((bf16[1024,1536]{1,0:T(8,128)(2,1)}), bf16[256,1536]{1,0:T(8,128)(2,1)}) %reduce-scatter.18.cloned.1.call-update) | async-done | bytes 786448 | tf_op jit(solution)/shard_map/reduce_scatter | solution.py:940
  252.5 56.5 %all-gather.18.cloned.1.call-done = bf16[1024,1536]{1,0:T(8,128)(2,1)} async-done(((bf16[256,1536]{1,0:T(8,128)(2,1)}), bf16[1024,1536]{1,0:T(8,128)(2,1)}) %all-gather.18.cloned.1.call-update) | async-done | bytes 3145744 | tf_op jit(solution)/shard_map/all_gather | solution.py:942
  355.9 10.7 mix_forward.3
  368.9 9.5 psum.29
  397.4 27.1 %states_backward.2 = (bf16[1024,768]{1,0:T(8,128)(2,1)S(1)}, bf16[1024,256]{1,0:T(8,128)(2,1)S(1)}, bf16[1024,128]{1,0:T(8,128)(2,1)S(1)}, f32[8,768]{1,0:T(8,12...) custom-call(bf16[1024,768]{1,0:T(8,128)(2,1)} %copy-done.16, ...), custom_call_target="tpu_custom_call" | custom-call | flops 2013265920 | bytes 12582912 | tf_op jit(solution)/shard_map/states_backward/pallas_call | solution.py:661
  443.5 61.8 %reduce-scatter.20.cloned.1.call-done = bf16[256,1792]{1,0:T(8,128)(2,1)} async-done(((bf16[1024,1792]{1,0:T(8,128)(2,1)}), bf16[256,1792]{1,0:T(8,128)(2,1)}) %reduce-scatter.20.cloned.1.call-update) | async-done | bytes 917520 | tf_op jit(solution)/shard_map/reduce_scatter | solution.py:956
  515.7 60.1 %all-gather.20.cloned.1.call-done = bf16[1024,1536]{1,0:T(8,128)(2,1)} async-done(((bf16[256,1536]{1,0:T(8,128)(2,1)}), bf16[1024,1536]{1,0:T(8,128)(2,1)}) %all-gather.20.cloned.1.call-update) | async-done | bytes 3145744 | tf_op jit(solution)/shard_map/all_gather | solution.py:961
  605.4 27.1 %states_backward.3 = (bf16[1024,768]{1,0:T(8,128)(2,1)S(1)}, bf16[1024,256]{1,0:T(8,128)(2,1)S(1)}, bf16[1024,128]{1,0:T(8,128)(2,1)S(1)}, f32[8,768]{1,0:T(8,12...) custom-call(bf16[1024,768]{1,0:T(8,128)(2,1)} %copy-done.15, ...), custom_call_target="tpu_custom_call" | custom-call | flops 2013265920 | bytes 12582912 | tf_op jit(solution)/shard_map/states_backward/pallas_call | solution.py:661
  712.1 11.9 %reduce-scatter.34.cloned.1.call-done = bf16[384,1024]{1,0:T(8,128)(2,1)} async-done(((bf16[1536,1024]{1,0:T(8,128)(2,1)}), bf16[384,1024]{1,0:T(8,128)(2,1)}) %reduce-scatter.34.cloned.1.call-update) | async-done | bytes 786448
  733.1 15.0 %collective-permute-done.2 = bf16[1024,384]{1,0:T(8,128)(2,1)S(1)} collective-permute-done((bf16[1024,384]{1,0:T(8,128)(2,1)S(1)}, bf16[1024,384]{1,0:T(8,128)(2,1)S(1)}, u32[]{:S(2)}, u32[]{:S(2)}) %collective-permute-start.2) | collective-permute-done | bytes 786464 | tf_op jit(solution)/shard_map/ppermute | solution.py:759
  750.1 44.6 %reduce-scatter.22.cloned.1.call-done = bf16[256,1792]{1,0:T(8,128)(2,1)} async-done(((bf16[1024,1792]{1,0:T(8,128)(2,1)}), bf16[256,1792]{1,0:T(8,128)(2,1)}) %reduce-scatter.22.cloned.1.call-update) | async-done | bytes 917520 | tf_op jit(solution)/shard_map/reduce_scatter | solution.py:968
  804.4 23.9 %psum.31 = f32[2,3876]{1,0:T(2,128)S(1)} all-reduce(f32[2,3876]{1,0:T(2,128)S(1)} %pad_maximum_fusion.9), channel_id=1, replica_groups=mesh['section'=2,'seq'=4,'head'=4] {'section','seq'}, use_global_device_ids=true, to_apply=%region_24.25 | all-reduce | flops 7752 | bytes 62016 | tf_op jit(solution)/shard_map/psum | solution.py:1017
  834.9 37.0 %reduce-scatter.36.cloned.1.call-done = bf16[384,64]{1,0:T(8,128)(2,1)} async-done(((bf16[3072,64]{1,0:T(8,128)(2,1)}), bf16[384,64]{1,0:T(8,128)(2,1)}) %reduce-scatter.36.cloned.1.call-update) | async-done | bytes 49168
  873.5 55.6 %reduce-scatter.32.cloned.1.call-done = bf16[384,768]{1,0:T(8,128)(2,1)} async-done(((bf16[3072,768]{1,0:T(8,128)(2,1)}), bf16[384,768]{1,0:T(8,128)(2,1)}) %reduce-scatter.32.cloned.1.call-update) | async-done | bytes 589840 | tf_op jit(solution)/shard_map/reduce_scatter | solution.py:991
  935.0 51.7 %reduce-scatter.24.cloned.1.call-done = bf16[384,768]{1,0:T(8,128)(2,1)} async-done(((bf16[3072,768]{1,0:T(8,128)(2,1)}), bf16[384,768]{1,0:T(8,128)(2,1)}) %reduce-scatter.24.cloned.1.call-update) | async-done | bytes 589840 | tf_op jit(solution)/shard_map/reduce_scatter | solution.py:991
  988.8 55.1 %reduce-scatter.26.cloned.1.call-done = bf16[384,768]{1,0:T(8,128)(2,1)} async-done(((bf16[3072,768]{1,0:T(8,128)(2,1)}), bf16[384,768]{1,0:T(8,128)(2,1)}) %reduce-scatter.26.cloned.1.call-update) | async-done | bytes 589840 | tf_op jit(solution)/shard_map/reduce_scatter | solution.py:991
  1046.1 39.5 %psum.30 = f32[2,2560]{1,0:T(2,128)S(1)} all-reduce(f32[2,2560]{1,0:T(2,128)S(1)} %pad_maximum_fusion.10), channel_id=1, replica_groups=mesh['section'=2,'seq'=4,'head'=4] {'section','seq','head'}, use_global_device_ids=true, to_apply=%region_13.14 | all-reduce | flops 5120 | bytes 40960 | tf_op jit(solution)/shard_map/psum | solution.py:1018
  (460 shorter events, 322.8 us)
Async XLA Ops:
  7.3 38.4 %all-gather.24.cloned.1.call-start = ((), (), s32[]{:S(2)}) async-start(), calls=%async_computation.23 | async-start | bytes 1769472 | tf_op jit(solution)/shard_map/all_gather | solution.py:766
  9.1 74.0 %all-gather.22.cloned.1.call-start = ((), (), s32[]{:S(2)}) async-start(), calls=%async_computation.22 | async-start | bytes 5308416 | tf_op jit(solution)/shard_map/all_gather | solution.py:766
  10.1 114.4 %all-gather.26.cloned.1.call-start = ((), (), s32[]{:S(2)}) async-start(), calls=%async_computation.24 | async-start | bytes 5308416 | tf_op jit(solution)/shard_map/all_gather | solution.py:766
  12.1 163.2 %all-gather.28.cloned.1.call-start = ((), (), s32[]{:S(2)}) async-start(), calls=%async_computation.25 | async-start | bytes 5308416 | tf_op jit(solution)/shard_map/all_gather | solution.py:766
  14.1 228.5 %reduce-scatter.18.cloned.1.call-start = ((), (), s32[]{:S(2)}) async-start(), calls=%async_computation.12 | async-start | bytes 3932160 | tf_op jit(solution)/shard_map/reduce_scatter | solution.py:940
  88.4 43.0 %collective-permute-start = (bf16[3,1024]{1,0:T(4,128)(2,1)S(1)}, bf16[3,1024]{1,0:T(4,128)(2,1)S(1)}, u32[]{:S(2)}, u32[]{:S(2)}) collective-permute-start(bf16[3,1024]{1,0:T(4,128)(2,1)S(1)} %pad_maximum_fusion.13), channel_id=1, source_target_pairs={{0,4},{4,8},{8,12},{1,5},{5,9},{9,13},{2,6},{6,10},{10,14},{3,7},{... | collective-permute-start | bytes 18440 | tf_op jit(solution)/shard_map/ppermute | solution.py:755
  181.7 127.3 %all-gather.18.cloned.1.call-start = ((), (), s32[]{:S(2)}) async-start(), calls=%async_computation.13 | async-start | bytes 3932160 | tf_op jit(solution)/shard_map/all_gather | solution.py:942
  245.3 259.9 %reduce-scatter.20.cloned.1.call-start = ((), (), s32[]{:S(2)}) async-start(), calls=%async_computation.14 | async-start | bytes 4587520 | tf_op jit(solution)/shard_map/reduce_scatter | solution.py:956
  320.0 7.5 collective-permute-start.1
  424.6 5.7 collective-permute-start.3
  436.9 138.8 %all-gather.20.cloned.1.call-start = ((), (), s32[]{:S(2)}) async-start(), calls=%async_computation.15 | async-start | bytes 3932160 | tf_op jit(solution)/shard_map/all_gather | solution.py:961
  511.7 163.1 %reduce-scatter.30.cloned.1.call-start = ((), (), s32[]{:S(2)}) async-start(), calls=%async_computation.20 | async-start | bytes 983040 | tf_op jit(solution)/shard_map/reduce_scatter | solution.py:996
  515.6 159.2 %reduce-scatter.28.cloned.1.call-start = ((), (), s32[]{:S(2)}) async-start(), calls=%async_computation.19 | async-start | bytes 983040 | tf_op jit(solution)/shard_map/reduce_scatter | solution.py:996
  633.7 3.1 collective-permute-start.4
  638.8 85.2 %reduce-scatter.34.cloned.1.call-start = ((), (), s32[]{:S(2)}) async-start(), calls=%async_computation.26 | async-start | bytes 3932160
  650.0 144.7 %reduce-scatter.22.cloned.1.call-start = ((), (), s32[]{:S(2)}) async-start(), calls=%async_computation.16 | async-start | bytes 4587520 | tf_op jit(solution)/shard_map/reduce_scatter | solution.py:968
  663.2 170.0 %reduce-scatter.38.cloned.1.call-start = ((), (), s32[]{:S(2)}) async-start(), calls=%async_computation.28 | async-start | bytes 884736
  674.7 197.1 %reduce-scatter.36.cloned.1.call-start = ((), (), s32[]{:S(2)}) async-start(), calls=%async_computation.27 | async-start | bytes 884736
  677.0 252.0 %reduce-scatter.32.cloned.1.call-start = ((), (), s32[]{:S(2)}) async-start(), calls=%async_computation.21 | async-start | bytes 5308416 | tf_op jit(solution)/shard_map/reduce_scatter | solution.py:991
  684.8 301.9 %reduce-scatter.24.cloned.1.call-start = ((), (), s32[]{:S(2)}) async-start(), calls=%async_computation.17 | async-start | bytes 5308416 | tf_op jit(solution)/shard_map/reduce_scatter | solution.py:991
  698.1 345.8 %reduce-scatter.26.cloned.1.call-start = ((), (), s32[]{:S(2)}) async-start(), calls=%async_computation.18 | async-start | bytes 5308416 | tf_op jit(solution)/shard_map/reduce_scatter | solution.py:991
  728.9 19.2 %collective-permute-start.2 = (bf16[1024,384]{1,0:T(8,128)(2,1)S(1)}, bf16[1024,384]{1,0:T(8,128)(2,1)S(1)}, u32[]{:S(2)}, u32[]{:S(2)}) collective-permute-start(bf16[1024,384]{1,0:T(8,128)(2,1)S(1)} %broadcast_select_fusion), channel_id=1, source_target_pairs={{0,16},{16,0},{1,17},{17,1},{2,18},{18,2},{3,19},{19,3},{4,20},{20... | collective-permute-start | bytes 2359304 | tf_op jit(solution)/shard_map/ppermute | solution.py:759
  800.3 130.9 %all-to-all-start = ((bf16[4,256,384]{2,1,0:T(8,128)(2,1)}), bf16[4,256,384]{2,1,0:T(8,128)(2,1)S(1)}, u32[]{:S(2)}, u32[]{:S(2)}) async-start(bf16[4,256,384]{2,1,0:T(8,128)(2,1)} %bitcast.210), calls=%async_computation.3 | async-start | bytes 1572864 | tf_op jit(solution)/shard_map/all_to_all | solution.py:976
  933.6 153.3 %collective-permute-start.5 = (bf16[1024,384]{1,0:T(8,128)(2,1)}, bf16[1024,384]{1,0:T(8,128)(2,1)}, u32[]{:S(2)}, u32[]{:S(2)}) collective-permute-start(bf16[1024,384]{1,0:T(8,128)(2,1)} %get-tuple-element.239), channel_id=1, source_target_pairs={{0,16},{16,0},{1,17},{17,1},{2,18},{18,2},{3,19},{19,3},{4,20},{20... | collective-permute-start | bytes 2359304 | tf_op jit(solution)/shard_map/ppermute | solution.py:759
  (101 other events, 1968.8 us)
Sparse Core Ops, SparseCore 0:
  10.6 31.0 all-gather.23
  44.2 38.8 all-gather.21
  85.6 38.9 all-gather.25
  126.3 42.9 all-gather.27
  181.8 60.6 reduce-scatter.17
  245.5 63.4 all-gather.17
  437.0 68.1 reduce-scatter.19
  511.8 63.8 all-gather.19
  578.6 21.9 reduce-scatter.29
  639.0 23.1 reduce-scatter.27
  664.5 59.4 reduce-scatter.33
  726.2 68.4 reduce-scatter.21
  797.8 35.4 reduce-scatter.37
  836.8 34.9 reduce-scatter.35
  875.1 53.8 reduce-scatter.31
  932.8 53.8 reduce-scatter.23
  990.0 53.8 reduce-scatter.25

commit v2 on v1

v2 whole, which is shorter than its diff:
```python
from functools import partial

import jax
import jax.numpy as jnp
from jax import lax
from jax.experimental import pallas as pl
from jax.experimental.pallas import tpu as pltpu
from jax.sharding import PartitionSpec as P

INNER = 3072
CONV = 4
CHUNK = 128
LANES = 128
ROWS = 256

epsilon = 1e-05
exact = lax.Precision.HIGHEST
f32 = jnp.float32
bf16 = jnp.bfloat16


def dot_nn(left, right, precision=None):
    return lax.dot_general(
        left, right, (((1,), (0,)), ((), ())), precision=precision, preferred_element_type=f32
    )


def dot_nt(left, right, precision=None):
    return lax.dot_general(
        left, right, (((1,), (1,)), ((), ())), precision=precision, preferred_element_type=f32
    )


def dot_tn(left, right):
    return lax.dot_general(left, right, (((0,), (0,)), ((), ())), preferred_element_type=f32)


def silu_parts(values):
    gate = jax.nn.sigmoid(values)
    return gate, values * gate


def silu_slope(values, gate):
    return gate * (1.0 + values * (1.0 - gate))


def weight_fetch(block, sources, held, sem):
    here = lax.axis_index("section") == block
    away = jnp.logical_not(here)

    @pl.when(here)
    def _():
        pltpu.make_async_copy(sources[0], held, sem).start()

    place = lax.axis_index("seq")
    if len(sources) == 3:
        rows = sources[1].shape[1]
        for piece in range(4):
            target = held.at[piece * rows : (piece + 1) * rows]
            for k in range(2):

                @pl.when(away & (lax.rem(place + piece, 2) == k))
                def _():
                    pltpu.make_async_copy(sources[1 + k].at[piece // 2], target, sem).start()

        return
    rows = sources[1].shape[0]
    for piece in range(4):
        target = held.at[piece * rows : (piece + 1) * rows]
        for k, bits in enumerate((0, 2, 1, 3)):
            bit_low = lax.rem(place + piece, 2) == bits % 2
            bit_high = lax.rem(place // 2 + piece // 2, 2) == bits // 2

            @pl.when(away & bit_low & bit_high)
            def _():
                pltpu.make_async_copy(sources[1 + k], target, sem).start()


def weight_wait(sources, held, sem):
    pltpu.make_async_copy(sources[0], held, sem).wait()


def anywhere():
    return pl.BlockSpec(memory_space=pl.ANY)


def weight_scratch(own):
    return [pltpu.VMEM(own.shape, own.dtype), pltpu.SemaphoreType.DMA]


def head_groups(width, heads):
    head_width = width // heads
    per_group = max(LANES // head_width, 1)
    found = []
    for first in range(0, heads, per_group):
        count = min(per_group, heads - first)
        found.append((first, count, first * head_width, count * head_width))
    return found


def spread(tile, first, count, lanes):
    rows = tile.shape[0]
    head_width = lanes // count
    out = jnp.broadcast_to(tile[:, first : first + 1], (rows, lanes))
    lane = lax.broadcasted_iota(jnp.int32, (rows, lanes), 1)
    for k in range(1, count):
        column = jnp.broadcast_to(tile[:, first + k : first + k + 1], (rows, lanes))
        out = jnp.where(lane >= k * head_width, column, out)
    return out


def own_lanes(tile, k, count):
    if count == 1:
        return tile
    head_width = tile.shape[1] // count
    lane = lax.broadcasted_iota(jnp.int32, tile.shape, 1)
    inside = (lane >= k * head_width) & (lane < (k + 1) * head_width)
    return jnp.where(inside, tile, jnp.zeros_like(tile))


def triangle(keep):
    row = lax.broadcasted_iota(jnp.int32, (CHUNK, CHUNK), 0)
    column = lax.broadcasted_iota(jnp.int32, (CHUNK, CHUNK), 1)
    return keep(row, column)


def decay_of(payload, state):
    rows = payload[state : state + 16].astype(f32)
    return jnp.exp(rows[0:1] + rows[8:9] + rows[12:13])


def project_kernel(
    heads,
    block,
    sources,
    x_in,
    x_edge,
    gain,
    *refs,
):
    pack_sources, refs = refs[:sources], refs[sources:]
    (
        dt_bias, rate, taps_x, taps_bc, normed_out, rescale_out, raw_x, raw_bc,
        edge_x, edge_bc, step_raw, pre_x, pre_bc, act_x, act_bc, dt_out,
        run_out, payload, ext_x, ext_bc, end_out, total_out, pack, pack_sem,
    ) = refs
    step = pl.program_id(0)
    groups = head_groups(raw_x.shape[1], heads)
    shared = act_bc.shape[1]
    state = shared // 2

    def normed_of(block):
        x = block.astype(f32)
        rescale = lax.rsqrt(jnp.mean(x * x, axis=-1, keepdims=True) + epsilon)
        return rescale, (x * rescale * gain[...]).astype(bf16)

    @pl.when(step == 0)
    def _():
        weight_fetch(block, pack_sources, pack, pack_sem)
        _, edge = normed_of(x_edge[...])
        weight_wait(pack_sources, pack, pack_sem)
        edge_x[...] = dot_nn(edge, pack[:, shared + LANES :]).astype(bf16).astype(f32)[8:]
        edge_bc[...] = dot_nn(edge, pack[:, :shared]).astype(bf16).astype(f32)[8:]
        ext_x[0:8] = edge_x[...]
        ext_bc[0:8] = edge_bc[...]
        end_out[...] = jnp.zeros_like(end_out)
        total_out[...] = jnp.zeros_like(total_out)

    @pl.when(step > 0)
    def _():
        ext_x[0:8] = ext_x[ROWS : ROWS + 8]
        ext_bc[0:8] = ext_bc[ROWS : ROWS + 8]

    rescale, normed = normed_of(x_in[...])
    rescale_out[...] = rescale
    normed_out[...] = normed
    low = dot_nn(normed, pack[:, :shared]).astype(bf16)
    raw_bc[...] = low
    ext_bc[8:] = low.astype(f32)
    step_in = dot_nn(normed, pack[:, shared : shared + LANES])
    step_raw[...] = step_in
    sizes = jax.nn.softplus(step_in + dt_bias[...])
    dt_out[...] = sizes
    low = dot_nn(normed, pack[:, shared + LANES :]).astype(bf16)
    raw_x[...] = low
    ext_x[8:] = low.astype(f32)
    for ext, taps, pre, act in ((ext_bc, taps_bc, pre_bc, act_bc), (ext_x, taps_x, pre_x, act_x)):
        total = ext[5 : 5 + ROWS] * taps[0:1]
        for k in range(1, CONV):
            total = total + ext[5 + k : 5 + k + ROWS] * taps[k : k + 1]
        pre[...] = total.astype(bf16)
        act[...] = silu_parts(total)[1].astype(bf16)
    lower = triangle(lambda t, s: t >= s).astype(f32)
    for sub in range(ROWS // CHUNK):
        at = slice(sub * CHUNK, (sub + 1) * CHUNK)
        dt = sizes[at]
        run = dot_nn(lower, dt * rate[...], exact)
        run_out[at] = run
        last = run[CHUNK - 1 : CHUNK]
        weight = jnp.exp(last - run) * dt
        decay = jnp.exp(last)
        b_turned = act_bc[at, :state].astype(f32).T.astype(bf16)
        for first, count, lane, lanes in groups:
            cols = slice(lane, lane + lanes)
            scaled = act_x[at, cols].astype(f32) * spread(weight, first, count, lanes)
            end_out[:, cols] = spread(decay, first, count, lanes) * end_out[:, cols] + dot_nn(
                b_turned, scaled.astype(bf16)
            )
        total_out[...] += jnp.broadcast_to(last, total_out.shape)

    @pl.when(step == pl.num_programs(0) - 1)
    def _():
        for first, count, lane, lanes in groups:
            cols = slice(lane, lane + lanes)
            payload[:state, cols] = end_out[:, cols].astype(bf16)
            total = spread(total_out[...], first, count, lanes)
            high = total.astype(bf16).astype(f32)
            middle = (total - high).astype(bf16).astype(f32)
            low = total - high - middle
            row = lax.broadcasted_iota(jnp.int32, (8, lanes), 0)
            rest = jnp.where(row < 4, middle, low)
            payload[state:, cols] = jnp.concatenate([high, rest], axis=0).astype(bf16)


def full(shape):
    return pl.BlockSpec(shape, lambda i: (0,) * len(shape))


def rows_of(width, back=0):
    if back:
        return pl.BlockSpec((ROWS, width), lambda i: (back - 1 - i, 0))
    return pl.BlockSpec((ROWS, width), lambda i: (i, 0))


def pieces_of(pieces, count, model):
    if pieces == 1:
        return rows_of(model), (count, model)
    lanes = model // pieces
    return pl.BlockSpec((pieces, ROWS, lanes), lambda i: (0, i, 0)), (pieces, count, lanes)


def params():
    return pltpu.CompilerParams(
        dimension_semantics=("arbitrary",), vmem_limit_bytes=48 * 1024 * 1024
    )


def project_forward(
    heads, block, x, x_edge, gain, pack, dt_bias, rate, taps_x, taps_bc
):
    count, model = x.shape
    width, shared = taps_x.shape[1], taps_bc.shape[1]
    state = shared // 2
    return pl.pallas_call(
        partial(project_kernel, heads, block, len(pack)),
        grid=(count // ROWS,),
        in_specs=[
            rows_of(model),
            full((16, model)),
            full((1, model)),
            *[anywhere() for _ in pack],
            full((1, LANES)),
            full((1, LANES)),
            full((CONV, width)),
            full((CONV, shared)),
        ],
        out_specs=[
            rows_of(model),
            rows_of(1),
            rows_of(width),
            rows_of(shared),
            full((8, width)),
            full((8, shared)),
            rows_of(LANES),
            rows_of(width),
            rows_of(shared),
            rows_of(width),
            rows_of(shared),
            rows_of(LANES),
            rows_of(LANES),
            full((state + 16, width)),
        ],
        out_shape=[
            jax.ShapeDtypeStruct((count, model), bf16),
            jax.ShapeDtypeStruct((count, 1), f32),
            jax.ShapeDtypeStruct((count, width), bf16),
            jax.ShapeDtypeStruct((count, shared), bf16),
            jax.ShapeDtypeStruct((8, width), f32),
            jax.ShapeDtypeStruct((8, shared), f32),
            jax.ShapeDtypeStruct((count, LANES), f32),
            jax.ShapeDtypeStruct((count, width), bf16),
            jax.ShapeDtypeStruct((count, shared), bf16),
            jax.ShapeDtypeStruct((count, width), bf16),
            jax.ShapeDtypeStruct((count, shared), bf16),
            jax.ShapeDtypeStruct((count, LANES), f32),
            jax.ShapeDtypeStruct((count, LANES), f32),
            jax.ShapeDtypeStruct((state + 16, width), bf16),
        ],
        scratch_shapes=[
            pltpu.VMEM((8 + ROWS, width), f32),
            pltpu.VMEM((8 + ROWS, shared), f32),
            pltpu.VMEM((state, width), f32),
            pltpu.VMEM((8, LANES), f32),
            *weight_scratch(pack[0]),
        ],
        compiler_params=params(),
        cost_estimate=pl.CostEstimate(
            flops=2 * count * model * pack[0].shape[1],
            bytes_accessed=2 * pack[0].size + count * (4 * model + 6 * (width + shared)),
            transcendentals=count * (width + shared),
        ),
        name="project_forward",
    )(x, x_edge, gain, *pack, dt_bias, rate, taps_x, taps_bc)


def inner_kernel(
    heads, block, act_x, act_bc, dt_in, run_in, normed, *refs
):
    *z_sources, gate_out, inner_out, w_z, z_sem = refs

    @pl.when(pl.program_id(0) == 0)
    def _():
        weight_fetch(block, z_sources, w_z, z_sem)
        weight_wait(z_sources, w_z, z_sem)

    groups = head_groups(act_x.shape[1], heads)
    state = act_bc.shape[1] // 2
    gate_out[...] = dot_nn(normed[...], w_z[...])
    causal = triangle(lambda t, s: t >= s)
    for sub in range(ROWS // CHUNK):
        at = slice(sub * CHUNK, (sub + 1) * CHUNK)
        dt = dt_in[at]
        run = run_in[at]
        turned = run.T
        product = dot_nt(act_bc[at, state:], act_bc[at, :state])
        for first, count, lane, lanes in groups:
            cols = slice(lane, lane + lanes)
            stepped = act_x[at, cols].astype(f32) * spread(dt, first, count, lanes)
            low = stepped.astype(bf16)
            weights = []
            stacked = []
            for k in range(count):
                h = first + k
                gap = jnp.broadcast_to(run[:, h : h + 1], (CHUNK, CHUNK)) - turned[h : h + 1]
                factor = jnp.exp(jnp.where(causal, gap, -jnp.inf))
                weights.append((product * factor).astype(bf16))
                stacked.append(own_lanes(low, k, count))
            inner_out[at, cols] = dot_nn(
                jnp.concatenate(weights, axis=1), jnp.concatenate(stacked, axis=0)
            )


def inner_forward(heads, block, act_x, act_bc, dt, run, normed, w_z):
    count, width = act_x.shape
    model = normed.shape[1]
    shared = act_bc.shape[1]
    return pl.pallas_call(
        partial(inner_kernel, heads, block),
        grid=(count // ROWS,),
        in_specs=[
            rows_of(width),
            rows_of(shared),
            rows_of(LANES),
            rows_of(LANES),
            rows_of(model),
            *[anywhere() for _ in w_z],
        ],
        out_specs=[rows_of(width), rows_of(width)],
        out_shape=[
            jax.ShapeDtypeStruct((count, width), f32),
            jax.ShapeDtypeStruct((count, width), f32),
        ],
        scratch_shapes=weight_scratch(w_z[0]),
        compiler_params=params(),
        cost_estimate=pl.CostEstimate(
            flops=2 * count * width * (4 * CHUNK + model),
            bytes_accessed=count * (10 * width + 2 * model) + 2 * w_z[0].size,
            transcendentals=count * heads * CHUNK,
        ),
        name="inner_forward",
    )(act_x, act_bc, dt, run, normed, *w_z)


def outer_kernel(
    heads,
    block,
    sources,
    pieces,
    shards,
    act_x,
    act_bc,
    dt_in,
    run_in,
    gate_in,
    inner_in,
    *refs,
):
    out_sources, refs = refs[:sources], refs[sources:]
    skip, gain, *refs = refs
    arrived, refs = refs[: shards - 1], refs[shards - 1 :]
    grad_in, refs = (refs[0], refs[1:]) if len(refs) == 9 else (None, refs)
    mixed_out, scaled_out, part_out, sums_out, states_out, held, w_out, out_sem = refs
    groups = head_groups(act_x.shape[1], heads)
    state = act_bc.shape[1] // 2

    @pl.when(pl.program_id(0) == 0)
    def _():
        weight_fetch(block, out_sources, w_out, out_sem)
        place = lax.axis_index("seq")
        held[...] = jnp.zeros_like(held)
        for distance in reversed(range(1, shards)):

            @pl.when(place >= distance)
            def _():
                payload = arrived[distance - 1]
                held[...] = decay_of(payload, state) * held[...] + payload[:state].astype(f32)

        weight_wait(out_sources, w_out, out_sem)

    square_rows = []
    ones = jnp.ones((8, LANES), f32)
    for sub in range(ROWS // CHUNK):
        at = slice(sub * CHUNK, (sub + 1) * CHUNK)
        run = run_in[at]
        last = run[CHUNK - 1 : CHUNK]
        weight = jnp.exp(last - run) * dt_in[at]
        decay = jnp.exp(last)
        grown = jnp.exp(run)
        c_part = act_bc[at, state:]
        b_turned = act_bc[at, :state].astype(f32).T.astype(bf16)
        states_out[sub] = held[...].astype(bf16)
        squares = jnp.zeros((CHUNK, LANES), f32)
        for first, count, lane, lanes in groups:
            cols = slice(lane, lane + lanes)
            x_part = act_x[at, cols].astype(f32)
            before = held[:, cols]
            mixed = inner_in[at, cols] + spread(grown, first, count, lanes) * dot_nn(
                c_part, before.astype(bf16)
            )
            mixed = mixed + skip[:, cols] * x_part
            held[:, cols] = spread(decay, first, count, lanes) * before + dot_nn(
                b_turned, (x_part * spread(weight, first, count, lanes)).astype(bf16)
            )
            gated = mixed * silu_parts(gate_in[at, cols])[1]
            mixed_out[at, cols] = mixed.astype(bf16)
            scaled_out[at, cols] = (gated * gain[:, cols]).astype(bf16)
            square = gated * gated
            if lanes < LANES:
                fill = jnp.zeros((CHUNK, LANES - lanes), f32)
                square = jnp.concatenate([square, fill], axis=1)
            squares = squares + square
        square_rows.append(dot_nt(ones, squares, exact))
    part = dot_nt(scaled_out[...], w_out[...])
    if pieces == 1:
        part_out[...] = part.astype(bf16)
    else:
        wide = part.shape[1] // pieces
        for k in range(pieces):
            part_out[k] = part[:, k * wide : (k + 1) * wide].astype(bf16)
    row = lax.broadcasted_iota(jnp.int32, (8, CHUNK), 0)
    for sub in range(ROWS // CHUNK):
        at = slice(sub * CHUNK, (sub + 1) * CHUNK)
        pair_row = jnp.zeros((8, CHUNK), f32)
        if grad_in is not None:
            pairs = jnp.zeros((CHUNK, LANES), f32)
            for lane in range(0, part.shape[1], LANES):
                cols = slice(lane, lane + LANES)
                pairs = pairs + part[at, cols] * grad_in[at, cols].astype(f32)
            pair_row = dot_nt(ones, pairs, exact)
        sums_out[:, at] = jnp.where(row == 0, square_rows[sub], pair_row)


def outer_forward(
    heads, block, pieces, act_x, act_bc, dt, run, gate_in, inner, w_out, skip, gain, arrived, grad_in
):
    count, width = act_x.shape
    model = w_out[0].shape[0]
    part_spec, part_shape = pieces_of(pieces, count, model)
    shared = act_bc.shape[1]
    state = shared // 2
    subs = ROWS // CHUNK
    extra, extra_specs = [], []
    if grad_in is not None:
        extra, extra_specs = [grad_in], [rows_of(model)]
    return pl.pallas_call(
        partial(outer_kernel, heads, block, len(w_out), pieces, len(arrived) + 1),
        grid=(count // ROWS,),
        in_specs=[
            rows_of(width),
            rows_of(shared),
            rows_of(LANES),
            rows_of(LANES),
            rows_of(width),
            rows_of(width),
            *[anywhere() for _ in w_out],
            full((1, width)),
            full((1, width)),
            *[full(payload.shape) for payload in arrived],
            *extra_specs,
        ],
        out_specs=[
            rows_of(width),
            rows_of(width),
            part_spec,
            pl.BlockSpec((8, ROWS), lambda i: (0, i)),
            pl.BlockSpec((subs, state, width), lambda i: (i, 0, 0)),
        ],
        out_shape=[
            jax.ShapeDtypeStruct((count, width), bf16),
            jax.ShapeDtypeStruct((count, width), bf16),
            jax.ShapeDtypeStruct(part_shape, bf16),
            jax.ShapeDtypeStruct((8, count), f32),
            jax.ShapeDtypeStruct((count // CHUNK, state, width), bf16),
        ],
        scratch_shapes=[pltpu.VMEM((state, width), f32), *weight_scratch(w_out[0])],
        compiler_params=params(),
        cost_estimate=pl.CostEstimate(
            flops=2 * count * width * (2 * state + model),
            bytes_accessed=count * width * 18,
            transcendentals=count * width,
        ),
        name="outer_forward",
    )(
        act_x, act_bc, dt, run, gate_in, inner, *w_out, skip, gain, *arrived, *extra
    )


def gate_kernel(
    heads,
    block,
    sources,
    addends,
    between,
    grad,
    gate_in,
    mixed_in,
    scaled_in,
    act_x,
    act_bc,
    run_in,
    gain,
    *refs,
):
    out_sources, refs = refs[:sources], refs[sources:]
    sums, refs = refs[:addends], refs[addends:]
    later, earlier = refs[:2] if between else (None, None)
    refs = refs[2:] if between else refs
    grad_mixed, grad_gate, scaled_out, gain_sum, skip_sum, adjoint_out, *refs = refs
    grad_in, adjoint, scales, w_out, out_sem = refs
    step = pl.program_id(0)
    groups = head_groups(act_x.shape[1], heads)
    state = act_bc.shape[1] // 2

    @pl.when(step == 0)
    def _():
        weight_fetch(block, out_sources, w_out, out_sem)
        gain_sum[...] = jnp.zeros_like(gain_sum)
        skip_sum[...] = jnp.zeros_like(skip_sum)
        adjoint[...] = jnp.zeros_like(adjoint)
        scales[...] = jnp.zeros_like(scales)
        weight_wait(out_sources, w_out, out_sem)

    grad_in[...] = dot_nn(grad[...], w_out[...])
    total = sums[0][...]
    for more in sums[1:]:
        total = total + more[...]
    scale_row = lax.rsqrt(total[0:1] / INNER + epsilon)
    pull_row = total[1:2] * scale_row * scale_row * scale_row / INNER
    for sub in reversed(range(ROWS // CHUNK)):
        at = slice(sub * CHUNK, (sub + 1) * CHUNK)
        run = run_in[at]
        grown = jnp.exp(run)
        decay = grown[CHUNK - 1 : CHUNK]
        c_turned = act_bc[at, state:].astype(f32).T.astype(bf16)
        scales[0:1] = scale_row[:, at]
        scales[1:2] = pull_row[:, at]
        columns = scales[...].T
        row_scale = columns[:, 0:1]
        row_pull = columns[:, 1:2]
        if later is not None:
            moved = later[at].astype(f32) - earlier[at].astype(f32)
            pulled = jnp.sum(grad[at].astype(f32) * moved, axis=1, keepdims=True)
            row_pull = pulled * row_scale * row_scale * (1.0 / INNER)
        for first, count, lane, lanes in groups:
            cols = slice(lane, lane + lanes)
            gate = gate_in[at, cols]
            mixed = mixed_in[at, cols].astype(f32)
            share, active = silu_parts(gate)
            gated = mixed * active
            d_scaled = grad_in[at, cols] * row_scale
            d_gated = d_scaled * gain[:, cols] - row_pull * gated
            d_mixed = d_gated * active
            grad_mixed[at, cols] = d_mixed.astype(bf16)
            grad_gate[at, cols] = (d_gated * mixed * silu_slope(gate, share)).astype(bf16)
            scaled_out[at, cols] = (scaled_in[at, cols].astype(f32) * row_scale).astype(bf16)
            gain_sum[0:1, cols] += jnp.sum(d_scaled * gated, axis=0, keepdims=True)
            skip_sum[0:1, cols] += jnp.sum(
                d_mixed * act_x[at, cols].astype(f32), axis=0, keepdims=True
            )
            adjoint[:, cols] = spread(decay, first, count, lanes) * adjoint[:, cols] + dot_nn(
                c_turned, (d_mixed * spread(grown, first, count, lanes)).astype(bf16)
            )

    @pl.when(step == pl.num_programs(0) - 1)
    def _():
        adjoint_out[...] = adjoint[...].astype(bf16)


def gate_backward(
    heads, block, grad, w_out, gate_in, mixed, scaled, act_x, act_bc, run, gain, sums, ends
):
    count, width = act_x.shape
    model = grad.shape[1]
    shared = act_bc.shape[1]
    state = shared // 2
    steps = count // ROWS
    return pl.pallas_call(
        partial(gate_kernel, heads, block, len(w_out), len(sums), len(ends) > 0),
        grid=(steps,),
        in_specs=[
            rows_of(model, steps),
            rows_of(width, steps),
            rows_of(width, steps),
            rows_of(width, steps),
            rows_of(width, steps),
            rows_of(shared, steps),
            rows_of(LANES, steps),
            full((1, width)),
            *[anywhere() for _ in w_out],
            *[pl.BlockSpec((8, ROWS), lambda i: (0, steps - 1 - i)) for _ in sums],
            *[rows_of(model, steps) for _ in ends],
        ],
        out_specs=[
            rows_of(width, steps),
            rows_of(width, steps),
            rows_of(width, steps),
            full((8, width)),
            full((8, width)),
            full((state, width)),
        ],
        out_shape=[
            jax.ShapeDtypeStruct((count, width), bf16),
            jax.ShapeDtypeStruct((count, width), bf16),
            jax.ShapeDtypeStruct((count, width), bf16),
            jax.ShapeDtypeStruct((8, width), f32),
            jax.ShapeDtypeStruct((8, width), f32),
            jax.ShapeDtypeStruct((state, width), bf16),
        ],
        scratch_shapes=[
            pltpu.VMEM((ROWS, width), f32),
            pltpu.VMEM((state, width), f32),
            pltpu.VMEM((CHUNK, CHUNK), f32),
            *weight_scratch(w_out[0]),
        ],
        compiler_params=params(),
        cost_estimate=pl.CostEstimate(
            flops=2 * count * width * (state + model),
            bytes_accessed=count * width * 16,
            transcendentals=count * width,
        ),
        name="gate_backward",
    )(
        grad, gate_in, mixed, scaled, act_x, act_bc, run, gain, *w_out, *sums, *ends
    )


def states_kernel(
    heads,
    shards,
    grad_mixed,
    act_x,
    act_bc,
    pre_x,
    pre_bc,
    raw_x,
    raw_bc,
    edge_x,
    edge_bc,
    dt_in,
    run_in,
    step_raw,
    dt_bias,
    rate_rows,
    states_in,
    skip,
    taps_x,
    taps_bc,
    members,
    *refs,
):
    arrived, payloads, refs = refs[: shards - 1], refs[shards - 1 : 2 * shards - 2], refs[2 * shards - 2 :]
    packed, tail, back, tap_sum_x, tap_sum_bc, rate_sum, bias_sum, *refs = refs
    adjoint, d_pre_x, d_pre_bc, rows_ref, carry_ref, square_ref = refs
    step = pl.program_id(0)
    steps = pl.num_programs(0)
    groups = head_groups(act_x.shape[1], heads)
    shared = act_bc.shape[1]
    state = shared // 2
    padded = members.shape[0]

    @pl.when(step == 0)
    def _():
        place = lax.axis_index("seq")
        adjoint[...] = jnp.zeros_like(adjoint)
        for distance in reversed(range(1, shards)):

            @pl.when(place + distance < shards)
            def _():
                decay = decay_of(payloads[shards - 1 - distance], state)
                adjoint[...] = decay * adjoint[...] + arrived[distance - 1][...].astype(f32)

        d_pre_x[8:16] = jnp.zeros((8, d_pre_x.shape[1]), f32)
        d_pre_bc[8:16] = jnp.zeros((8, d_pre_bc.shape[1]), f32)
        tap_sum_x[...] = jnp.zeros_like(tap_sum_x)
        tap_sum_bc[...] = jnp.zeros_like(tap_sum_bc)
        rate_sum[...] = jnp.zeros_like(rate_sum)
        bias_sum[...] = jnp.zeros_like(bias_sum)
        rows_ref[...] = jnp.zeros_like(rows_ref)
        square_ref[...] = jnp.zeros_like(square_ref)

    upto = triangle(lambda s, t: s <= t)
    not_before = triangle(lambda s, t: s >= t).astype(f32)
    before = triangle(lambda s, t: s < t).astype(f32)
    head_lane = lax.broadcasted_iota(jnp.int32, (CHUNK, LANES), 1)
    for sub in reversed(range(ROWS // CHUNK)):
        at = slice(sub * CHUNK, (sub + 1) * CHUNK)
        dt = dt_in[at]
        run = run_in[at]
        last = run[CHUNK - 1 : CHUNK]
        grown = jnp.exp(run)
        decay = grown[CHUNK - 1 : CHUNK]
        to_end = jnp.exp(last - run)
        run_turned = run.T
        dt_turned = dt.T[0:padded]
        inside_tile = jnp.zeros((CHUNK, LANES), f32)
        b_part = act_bc[at, :state]
        c_part = act_bc[at, state:]
        c_turned = c_part.astype(f32).T.astype(bf16)
        product = dot_nt(b_part, c_part)
        d_product = jnp.zeros((CHUNK, CHUNK), f32)
        d_b = jnp.zeros((CHUNK, state), f32)
        d_c = jnp.zeros((CHUNK, state), f32)
        d_pre_x[CHUNK + 8 : CHUNK + 16] = d_pre_x[8:16]
        d_pre_bc[CHUNK + 8 : CHUNK + 16] = d_pre_bc[8:16]
        through = []
        for first, count, lane, lanes in groups:
            cols = slice(lane, lane + lanes)
            x_low = act_x[at, cols]
            x_part = x_low.astype(f32)
            dy_low = grad_mixed[at, cols]
            dy = dy_low.astype(f32)
            dt_wide = spread(dt, first, count, lanes)
            ending = spread(to_end, first, count, lanes)
            growing = spread(grown, first, count, lanes)
            lam = adjoint[:, cols]
            lam_low = lam.astype(bf16)
            held_low = states_in[sub][:, cols]
            weights = []
            stacked = []
            for k in range(count):
                h = first + k
                gap = run_turned[h : h + 1] - jnp.broadcast_to(run[:, h : h + 1], (CHUNK, CHUNK))
                factor = jnp.exp(jnp.where(upto, gap, -jnp.inf))
                weights.append((product * factor).astype(bf16))
                stacked.append(own_lanes(dy_low, k, count))
                paired = dot_nt(own_lanes(x_low, k, count), dy_low) * factor
                dt_column = jnp.broadcast_to(dt[:, h : h + 1], (CHUNK, CHUNK))
                d_product = d_product + paired * dt_column
                inside = paired * product
                rows_ref[h : h + 1] = jnp.sum(inside * dt_column, axis=0, keepdims=True)
                inside_tile = jnp.where(
                    head_lane == h, jnp.sum(inside, axis=1, keepdims=True), inside_tile
                )
            d_stepped = dot_nn(jnp.concatenate(weights, axis=1), jnp.concatenate(stacked, axis=0))
            from_end = ending * dot_nn(b_part, lam_low)
            d_x = dt_wide * (d_stepped + from_end) + skip[:, cols] * dy
            dy_grown = dy * growing
            dy_grown_low = dy_grown.astype(bf16)
            carry_ref[0, :, cols] = (x_part * from_end).astype(bf16)
            carry_ref[1, :, cols] = (dy_grown * dot_nn(c_part, held_low)).astype(bf16)
            d_b = d_b + dot_nt((x_part * dt_wide * ending).astype(bf16), lam_low)
            d_c = d_c + dot_nt(dy_grown_low, held_low)
            wide_decay = spread(decay, first, count, lanes)
            lam_decayed = wide_decay * lam
            through.append(
                jnp.sum(lam_decayed * held_low.astype(f32), axis=0, keepdims=True)
            )
            adjoint[:, cols] = lam_decayed + dot_nn(c_turned, dy_grown_low)
            pre = pre_x[at, cols].astype(f32)
            d_pre_x[8 : CHUNK + 8, cols] = d_x * silu_slope(pre, jax.nn.sigmoid(pre))
        member = members[...]
        kept = dot_nt(member, carry_ref[0])
        fed = dot_nt(member, carry_ref[1])
        wide_row = jnp.concatenate(through, axis=1)
        across = dot_nt(member.astype(f32), jnp.broadcast_to(wide_row, (8, wide_row.shape[1])), exact)
        inside_rows = inside_tile.T[0:padded]
        d_log = (
            dot_nn(rows_ref[...] - dt_turned * inside_rows + fed, not_before, exact)
            + dot_nn(dt_turned * kept, before, exact)
            + across[:, 0:1]
        )
        d_log_rate = d_log * rate_rows[...]
        rate_sum[...] += d_log_rate * dt_turned
        square_ref[0:padded] = d_log_rate + inside_rows + kept
        d_step_exact = square_ref[...].T * jax.nn.sigmoid(step_raw[at] + dt_bias[...])
        bias_sum[0:1] += jnp.sum(d_step_exact, axis=0, keepdims=True)
        packed[at, shared : shared + LANES] = d_step_exact.astype(bf16)
        if sub == ROWS // CHUNK - 1:

            @pl.when(step == 0)
            def _():
                tail[:, shared : shared + LANES] = d_step_exact[CHUNK - 16 :]

        d_product_low = d_product.astype(bf16)
        d_b = d_b + dot_nn(d_product_low, c_part)
        d_c = d_c + dot_nn(d_product.T.astype(bf16), b_part)
        pre = pre_bc[at].astype(f32)
        slope = silu_slope(pre, jax.nn.sigmoid(pre))
        d_pre_bc[8 : CHUNK + 8, :state] = d_b * slope[:, :state]
        d_pre_bc[8 : CHUNK + 8, state:] = d_c * slope[:, state:]
        for d_pre, raw, taps, place, tap_sum in (
            (d_pre_x, raw_x, taps_x, slice(shared + LANES, None), tap_sum_x),
            (d_pre_bc, raw_bc, taps_bc, slice(0, shared), tap_sum_bc),
        ):
            values = raw[at].astype(f32)
            total = jnp.zeros_like(values)
            for k in range(CONV):
                moved = d_pre[11 - k : 11 - k + CHUNK]
                total = total + moved * taps[k : k + 1]
                tap_sum[k : k + 1] += jnp.sum(values * moved, axis=0, keepdims=True)
            packed[at, place] = total.astype(bf16)
            if sub == ROWS // CHUNK - 1:

                @pl.when(step == 0)
                def _():
                    tail[:, place] = total[CHUNK - 16 :]

    @pl.when(step == steps - 1)
    def _():
        back[...] = jnp.zeros_like(back)
        for d_pre, edge, taps, tap_sum, place in (
            (d_pre_x, edge_x, taps_x, tap_sum_x, slice(shared + LANES, None)),
            (d_pre_bc, edge_bc, taps_bc, tap_sum_bc, slice(0, shared)),
        ):
            d_pre[0:8] = jnp.zeros((8, d_pre.shape[1]), f32)
            values = edge[...]
            total = jnp.zeros_like(values)
            for k in range(CONV):
                moved = d_pre[3 - k : 11 - k]
                total = total + moved * taps[k : k + 1]
                tap_sum[k : k + 1] += jnp.sum(values * moved, axis=0, keepdims=True)
            back[8:, place] = total


def states_backward(
    heads,
    grad_mixed,
    act_x,
    act_bc,
    pre_x,
    pre_bc,
    raw_x,
    raw_bc,
    edge_x,
    edge_bc,
    dt,
    run,
    step_raw,
    dt_bias,
    rate,
    states,
    skip,
    taps_x,
    taps_bc,
    arrived,
    payloads,
):
    count, width = act_x.shape
    shared = act_bc.shape[1]
    state = shared // 2
    steps = count // ROWS
    subs = ROWS // CHUNK
    padded = -(-heads // 16) * 16
    head_of = jnp.arange(width)[None, :] // (width // heads)
    members = (jnp.arange(padded)[:, None] == head_of).astype(bf16)
    rate_rows = jnp.broadcast_to(rate[0, :padded, None], (padded, CHUNK))
    return pl.pallas_call(
        partial(states_kernel, heads, len(arrived) + 1),
        grid=(steps,),
        in_specs=[
            rows_of(width, steps),
            rows_of(width, steps),
            rows_of(shared, steps),
            rows_of(width, steps),
            rows_of(shared, steps),
            rows_of(width, steps),
            rows_of(shared, steps),
            full((8, width)),
            full((8, shared)),
            rows_of(LANES, steps),
            rows_of(LANES, steps),
            rows_of(LANES, steps),
            full((1, LANES)),
            full((padded, CHUNK)),
            pl.BlockSpec((subs, state, width), lambda i: (steps - 1 - i, 0, 0)),
            full((1, width)),
            full((CONV, width)),
            full((CONV, shared)),
            full((padded, width)),
            *[full(array.shape) for array in (*arrived, *payloads)],
        ],
        out_specs=[
            rows_of(shared + LANES + width, steps),
            full((16, shared + LANES + width)),
            full((16, shared + LANES + width)),
            full((8, width)),
            full((8, shared)),
            full((padded, CHUNK)),
            full((8, LANES)),
        ],
        out_shape=[
            jax.ShapeDtypeStruct((count, shared + LANES + width), bf16),
            jax.ShapeDtypeStruct((16, shared + LANES + width), f32),
            jax.ShapeDtypeStruct((16, shared + LANES + width), f32),
            jax.ShapeDtypeStruct((8, width), f32),
            jax.ShapeDtypeStruct((8, shared), f32),
            jax.ShapeDtypeStruct((padded, CHUNK), f32),
            jax.ShapeDtypeStruct((8, LANES), f32),
        ],
        scratch_shapes=[
            pltpu.VMEM((state, width), f32),
            pltpu.VMEM((CHUNK + 16, width), f32),
            pltpu.VMEM((CHUNK + 16, shared), f32),
            pltpu.VMEM((padded, CHUNK), f32),
            pltpu.VMEM((2, CHUNK, width), bf16),
            pltpu.VMEM((CHUNK, CHUNK), f32),
        ],
        compiler_params=params(),
        cost_estimate=pl.CostEstimate(
            flops=20 * count * width * state,
            bytes_accessed=count * width * 16,
            transcendentals=count * heads * CHUNK * 2,
        ),
        name="states_backward",
    )(
        grad_mixed,
        act_x,
        act_bc,
        pre_x,
        pre_bc,
        raw_x,
        raw_bc,
        edge_x,
        edge_bc,
        dt,
        run,
        step_raw,
        dt_bias,
        rate_rows,
        states,
        skip,
        taps_x,
        taps_bc,
        members,
        *arrived,
        *payloads,
    )


def part_kernel(
    pieces,
    block,
    sources,
    grad_gate,
    packed,
    x_in,
    gain,
    *refs,
):
    z_sources, refs = refs[:sources], refs[sources:]
    *pack_sources, part_out, row_sum, norm_sum, part_ref, w_z, z_sem, pack, pack_sem = refs

    @pl.when(pl.program_id(0) == 0)
    def _():
        weight_fetch(block, z_sources, w_z, z_sem)
        weight_fetch(block, pack_sources, pack, pack_sem)
        weight_wait(z_sources, w_z, z_sem)
        weight_wait(pack_sources, pack, pack_sem)
        norm_sum[...] = jnp.zeros_like(norm_sum)

    x = x_in[...].astype(f32)
    rescale = lax.rsqrt(jnp.mean(x * x, axis=-1, keepdims=True) + epsilon)
    part_ref[...] = dot_nt(grad_gate[...], w_z[...]) + dot_nt(packed[...], pack[...])
    total = jnp.zeros((ROWS, LANES), f32)
    for lane in range(0, x.shape[1], LANES):
        cols = slice(lane, lane + LANES)
        pulled = part_ref[:, cols] * (x_in[:, cols].astype(f32) * rescale)
        norm_sum[0:1, cols] += jnp.sum(pulled, axis=0, keepdims=True)
        total = total + pulled * gain[:, cols]
    row_sum[...] = dot_nt(jnp.ones((8, LANES), f32), total, exact)
    if pieces == 1:
        part_out[...] = part_ref[...].astype(bf16)
    else:
        lanes = x.shape[1] // pieces
        for k in range(pieces):
            part_out[k] = part_ref[:, k * lanes : (k + 1) * lanes].astype(bf16)


def part_backward(
    pieces, block, grad_gate, packed, w_z, pack, x, gain
):
    count, width = grad_gate.shape
    model = x.shape[1]
    part_spec, part_shape = pieces_of(pieces, count, model)
    return pl.pallas_call(
        partial(part_kernel, pieces, block, len(w_z)),
        grid=(count // ROWS,),
        in_specs=[
            rows_of(width),
            rows_of(packed.shape[1]),
            rows_of(model),
            full((1, model)),
            *[anywhere() for _ in (*w_z, *pack)],
        ],
        out_specs=[part_spec, pl.BlockSpec((8, ROWS), lambda i: (0, i)), full((8, model))],
        out_shape=[
            jax.ShapeDtypeStruct(part_shape, bf16),
            jax.ShapeDtypeStruct((8, count), f32),
            jax.ShapeDtypeStruct((8, model), f32),
        ],
        scratch_shapes=[
            pltpu.VMEM((ROWS, model), f32),
            *weight_scratch(w_z[0]),
            *weight_scratch(pack[0]),
        ],
        compiler_params=params(),
        cost_estimate=pl.CostEstimate(
            flops=2 * count * model * (width + packed.shape[1]),
            bytes_accessed=2 * (w_z[0].size + pack[0].size) + 8 * count * model,
            transcendentals=0,
        ),
        name="part_backward",
    )(grad_gate, packed, x, gain, *w_z, *pack)


def weights_kernel(count, low, *refs):
    lefts, rights, out = refs[:count], refs[count : 2 * count], refs[2 * count]
    lane = 0
    for left, right in zip(lefts, rights):
        lanes = right.shape[1]
        out[0, :, lane : lane + lanes] = dot_tn(left[...], right[...]).astype(bf16)
        lane += lanes


def weights_backward(lefts, rights, kept):
    count, model = lefts[0].shape
    rows = model // 4
    lanes = sum(right.shape[1] for right in rights)
    low = lax.rem(lax.axis_index("seq"), 2)
    low = (low if kept else 1 - low).astype(jnp.int32).reshape(1)
    return pl.pallas_call(
        partial(weights_kernel, len(lefts)),
        grid_spec=pltpu.PrefetchScalarGridSpec(
            num_scalar_prefetch=1,
            grid=(2,),
            in_specs=[
                *[pl.BlockSpec((count, rows), lambda i, low: (0, 2 * i + low[0])) for _ in lefts],
                *[pl.BlockSpec(right.shape, lambda i, low: (0, 0)) for right in rights],
            ],
            out_specs=pl.BlockSpec((1, rows, lanes), lambda i, low: (i, 0, 0)),
        ),
        out_shape=jax.ShapeDtypeStruct((2, rows, lanes), bf16),
        compiler_params=params(),
        cost_estimate=pl.CostEstimate(
            flops=count * model * lanes,
            bytes_accessed=2 * (len(lefts) * count * model + count * lanes + model * lanes),
            transcendentals=0,
        ),
        name="weights_backward",
    )(low, *lefts, *rights)


def traded(block, axis, bit):
    return lax.ppermute(block, axis, [(i, i ^ bit) for i in range(lax.axis_size(axis))])


def rotated(block, axis, distance):
    size = lax.axis_size(axis)
    return lax.ppermute(block, axis, [(i, (i + distance) % size) for i in range(size)])


def others(block, axis, sign):
    return [rotated(block, axis, sign * d) for d in range(1, lax.axis_size(axis))]


def bits_of(axis):
    bit = 1
    while bit < lax.axis_size(axis):
        yield bit
        bit *= 2


def butterfly(block, axis):
    for bit in bits_of(axis):
        block = block + traded(block, axis, bit)
    return block


def halved(pieces, axis, bit):
    pairs = pieces.reshape((pieces.shape[0] // 2, 2) + pieces.shape[1:])
    mine = lax.rem(lax.axis_index(axis) // bit, 2)
    kept = lax.dynamic_index_in_dim(pairs, mine, 1, False)
    sent = lax.dynamic_index_in_dim(pairs, 1 - mine, 1, False)
    return kept + traded(sent, axis, bit)


def core_sum(kept, arrived, earlier):
    high = lax.axis_index("seq") // 2

    def summed(at):
        own = lax.dynamic_index_in_dim(kept, at, 0, False)
        return after(own + lax.dynamic_index_in_dim(arrived, at, 0, False), earlier)

    return summed(1 - high), summed(high)


def after(value, earlier):
    return value + (0.0 * earlier.reshape(-1)[0].astype(f32)).astype(value.dtype)


def moved_along(block, axis, distance):
    size, place = lax.axis_size(axis), lax.axis_index(axis)
    arrived = rotated(block, axis, distance)
    outside = (place < distance) | (place >= size + distance)
    return jnp.where(outside, jnp.zeros_like(arrived), arrived)


def tied(*values):
    return lax.optimization_barrier(values)


def block_forward(
    block, x, x_edge, weights, grad, pieces, mixed_inside=lambda inner, payloads: (inner, payloads)
):
    heads = weights["heads"]
    (
        normed, rescale, raw_x, raw_bc, edge_x, edge_bc, step_raw, pre_x, pre_bc, act_x, act_bc,
        dt, run, payload,
    ) = project_forward(
        heads, block, x, x_edge, weights["norm"], weights["pack"], weights["dt_bias"],
        weights["rate"], weights["taps_x"], weights["taps_bc"],
    )
    payloads = others(payload, "seq", 1)
    gate_in, inner = inner_forward(
        heads, block, act_x, act_bc, dt, run, normed, weights["w_z"]
    )
    inner, payloads = mixed_inside(inner, payloads)
    mixed, scaled, part, sums, states = outer_forward(
        heads, block, pieces, act_x, act_bc, dt, run, gate_in, inner, weights["w_out"],
        weights["skip"], weights["gain"], payloads, grad,
    )
    kept = dict(
        raw_x=raw_x, raw_bc=raw_bc, step_raw=step_raw, edge_x=edge_x, edge_bc=edge_bc,
        gate_in=gate_in, pre_x=pre_x, pre_bc=pre_bc, act_x=act_x, act_bc=act_bc, dt=dt, run=run,
        payloads=payloads, mixed=mixed, scaled=scaled, states=states, normed=normed,
        rescale=rescale,
    )
    return part, sums, kept


def gate_step(block, grad, sums, ends, kept, weights):
    return gate_backward(
        weights["heads"], block, grad, weights["w_out"], kept["gate_in"], kept["mixed"],
        kept["scaled"], kept["act_x"], kept["act_bc"], kept["run"], weights["gain"], sums, ends,
    )


def states_step(grad_mixed, arrived, kept, weights):
    return states_backward(
        weights["heads"], grad_mixed, kept["act_x"], kept["act_bc"], kept["pre_x"],
        kept["pre_bc"], kept["raw_x"], kept["raw_bc"], kept["edge_x"], kept["edge_bc"],
        kept["dt"], kept["run"], kept["step_raw"], weights["dt_bias"], weights["rate"],
        kept["states"], weights["skip"], weights["taps_x"], weights["taps_bc"], arrived,
        kept["payloads"],
    )


def fixed_tail(packed, tail, back):
    rows = tail + moved_along(back, "seq", -1)
    return packed.at[packed.shape[0] - 16 :].set(rows.astype(bf16))


def vectors_of(heads, taps_x, gain_sum, skip_sum, bias_sum, rate_sum, norm_sum, taps_bc):
    return (
        jnp.concatenate(
            [
                taps_x[:CONV].reshape(-1), gain_sum[0], skip_sum[0], bias_sum[0, :heads],
                jnp.sum(rate_sum[:heads], axis=1),
            ]
        ),
        jnp.concatenate([norm_sum[0], taps_bc[:CONV].reshape(-1)]),
    )


def norm_backward(d_normed, row_sum, x, rescale, grad, gain, model):
    unit = x.astype(f32) * rescale
    h = d_normed.astype(f32) * gain
    out = grad.astype(f32) + rescale * (h - unit * (row_sum / model)[:, None])
    return out.astype(bf16)


def shards(
    tokens, cotangent, norm_gain, w_z, w_x, w_bc, w_dt, conv_x, conv_bc, dt_bias, a_log, skip_d,
    gate_gain, w_out,
):
    section = lax.axis_index("section")
    seq_at = lax.axis_index("seq")
    seq_size = lax.axis_size("seq")
    count, model = tokens.shape[1:]
    head_size = lax.axis_size("head")
    head_at = lax.axis_index("head")
    heads = a_log.shape[1]
    width = w_x.shape[2]
    shared = w_bc.shape[2]
    share = model // head_size
    row_share = count // head_size
    quarter = model // seq_size

    def mine_first(of_first, of_second):
        return (
            jnp.where(section == 0, of_first, of_second),
            jnp.where(section == 0, of_second, of_first),
        )

    def quarter_of(weight):
        return lax.dynamic_slice_in_dim(weight, seq_at * quarter, quarter, 0)

    def half_of(weight):
        pairs = weight.reshape(2, 2, quarter, weight.shape[1])
        return lax.dynamic_index_in_dim(pairs, lax.rem(seq_at, 2), 1, False)

    def own_rows(array):
        return lax.dynamic_slice_in_dim(array, head_at * row_share, row_share, 0)

    def own_columns(array):
        return lax.dynamic_slice_in_dim(array, head_at * share, share, 1)

    def edge_of(x):
        return jnp.pad(moved_along(x[count - (CONV - 1) :], "seq", 1), ((16 - (CONV - 1), 0), (0, 0)))

    def section_sum(of_first, of_second, earlier=None):
        mine, other = mine_first(of_first, of_second)
        arrived = traded(other, "section", 1)
        if earlier is not None:
            arrived = after(arrived, earlier)
        return mine.astype(f32) + arrived.astype(f32)

    def both_sequences(of_first, of_second, earlier=None):
        mine, other = mine_first(of_first, of_second)
        arrived = traded(other, "section", 1)
        if earlier is not None:
            arrived = after(arrived, earlier)
        return jnp.stack(mine_first(mine, arrived))

    padded_dt = jnp.pad(w_dt[0], ((0, 0), (0, LANES - heads)))
    got_pack = traded(
        jnp.concatenate([quarter_of(w) for w in (w_bc[0], padded_dt, w_x[0])], axis=1),
        "section", 1,
    )
    pack = jnp.concatenate([w_bc[0], padded_dt, w_x[0]], axis=1)
    vector = jnp.concatenate(
        [
            norm_gain[0], conv_x[0].T.reshape(-1), conv_bc[0].T.reshape(-1), dt_bias[0], a_log[0],
            skip_d[0], gate_gain[0],
        ]
    )
    got_pack, part_z, vector = tied(got_pack, half_of(w_z[0]), vector)
    vectors = mine_first(vector, traded(vector, "section", 1))
    first = lax.dynamic_index_in_dim(tokens, section, 0, False)
    first_edge = edge_of(first)
    got_z = traded(part_z, "section", 1)
    far_pack = traded(got_pack, "seq", 2)
    far_pack, got_z, part_out, pack, first, first_edge, *vectors = tied(
        far_pack, got_z, half_of(w_out[0]), pack, first, first_edge, *vectors
    )
    got_out = traded(part_out, "section", 1)
    sources_pack = (got_pack, far_pack, traded(got_pack, "seq", 1), traded(far_pack, "seq", 1))
    sources = dict(
        pack=(pack, *sources_pack), w_z=(w_z[0], got_z, traded(got_z, "seq", 1)), w_out=[w_out[0]]
    )
    weights = []
    for b in range(2):
        at = 0

        def take(size):
            nonlocal at
            at += size
            return vectors[b][at - size : at]

        block = dict(heads=heads, **sources)
        block["norm"] = take(model)[None]
        block["taps_x"] = take(CONV * width).reshape(CONV, width)
        block["taps_bc"] = take(CONV * shared).reshape(CONV, shared)
        block["dt_bias"] = jnp.pad(take(heads), (0, LANES - heads))[None]
        block["rate"] = jnp.pad(-jnp.exp(take(heads)), (0, LANES - heads))[None]
        block["skip"] = jnp.repeat(take(heads), width // heads)[None]
        block["gain"] = take(width)[None]
        weights.append(block)

    last_grad = lax.dynamic_index_in_dim(cotangent, section, 0, False)

    def fetch_out(inner, payloads):
        inner, part, *payloads = tied(inner, got_out, *payloads)
        sources["w_out"] += [part, traded(part, "seq", 1)]
        return inner, payloads

    part, sums, kept_first = block_forward(
        0, first, first_edge, weights[0], None, 1, fetch_out
    )
    summed = lax.psum_scatter(part, "head", scatter_dimension=0, tiled=True).astype(f32)
    sums_first = [sums, *others(sums, "head", 1)]
    scale_first = lax.rsqrt(sum(part[0] for part in sums_first) / INNER + epsilon)
    second_share = own_rows(first).astype(f32) + own_rows(scale_first)[:, None] * summed
    second = lax.all_gather(second_share.astype(bf16), "head", axis=0, tiled=True)

    outward, sums, kept_second = block_forward(
        1, second, edge_of(second), weights[1], last_grad, head_size
    )
    sums_second = [sums, *others(sums, "head", 1)]
    bits = list(bits_of("head"))

    grad_mixed, grad_gate, scaled, gain_sum, skip_sum, adjoint = gate_step(
        1, last_grad, sums_second, (), kept_second, weights[1]
    )
    normed = kept_second["normed"]
    early_sent = weights_backward([last_grad, normed], [scaled, grad_gate], False)
    grad_mixed, early_sent, outward, *arrived = tied(
        grad_mixed, early_sent, outward, *others(adjoint, "seq", -1)
    )
    packed, tail, back, taps_x, taps_bc, rate_sum, bias_sum = states_step(
        grad_mixed, arrived, kept_second, weights[1]
    )
    outward = after(halved(outward, "head", bits[0]), tail)
    packed, outward = tied(fixed_tail(packed, tail, back), outward)
    part, row_sum, norm_sum = part_backward(
        1, 1, grad_gate, packed, weights[1]["w_z"], weights[1]["pack"], second,
        weights[1]["norm"],
    )
    norm_sum, taps_x, gain_sum, skip_sum, bias_sum, rate_sum, taps_bc = tied(
        norm_sum, taps_x, gain_sum, skip_sum, bias_sum, rate_sum, taps_bc
    )
    local_second, whole_second = vectors_of(
        heads, taps_x, gain_sum, skip_sum, bias_sum, rate_sum, norm_sum, taps_bc
    )
    part, packed, scaled, grad_gate = tied(part, packed, scaled, grad_gate)
    rows_part = lax.psum_scatter(part, "head", scatter_dimension=0, tiled=True)
    row_sums = [row_sum, *others(row_sum, "head", 1)]
    row_sum = sum(part[0] for part in row_sums)
    kept = weights_backward([last_grad, normed], [scaled, grad_gate], True)
    early_sent, early = core_sum(kept, traded(early_sent, "seq", 1), norm_sum)
    late_sent = weights_backward([normed], [packed], False)
    kept = weights_backward([normed], [packed], True)
    late_sent, late = core_sum(kept, traded(late_sent, "seq", 1), norm_sum)
    rows_part, early_sent, late_sent = tied(rows_part, early_sent, late_sent)
    early = early + traded(early_sent, "seq", 2)
    late = late + traded(late_sent, "seq", 2)
    middle_share = norm_backward(
        rows_part, own_rows(row_sum), own_rows(second), own_rows(kept_second["rescale"]),
        own_rows(last_grad), weights[1]["norm"], model,
    )
    middle_grad = lax.all_gather(middle_share, "head", axis=0, tiled=True)
    middle_grad, early_second, late_second, outward = tied(middle_grad, early, late, outward)

    grad_mixed, grad_gate, scaled, gain_sum, skip_sum, adjoint = gate_step(
        0, middle_grad, sums_first, (second, first), kept_first, weights[0]
    )
    normed = kept_first["normed"]
    early_sent = weights_backward([middle_grad, normed], [scaled, grad_gate], False)
    grad_mixed, early_sent, outward, *arrived = tied(
        grad_mixed, early_sent, outward, *others(adjoint, "seq", -1)
    )
    packed, tail, back, taps_x, taps_bc, rate_sum, bias_sum = states_step(
        grad_mixed, arrived, kept_first, weights[0]
    )
    for bit in bits[1:]:
        outward = after(halved(outward, "head", bit), tail)
    packed, outward = tied(fixed_tail(packed, tail, back), outward)
    late_sent = weights_backward([normed], [packed], False)
    kept = weights_backward([normed], [packed], True)
    late_sent, late = core_sum(kept, traded(late_sent, "seq", 1), tail)
    packed, late_sent, late = tied(packed, late_sent, late)
    part, row_sum, norm_sum = part_backward(
        head_size, 0, grad_gate, packed, weights[0]["w_z"], weights[0]["pack"], first,
        weights[0]["norm"],
    )
    norm_sum, scaled, grad_gate, outward, *sums_second = tied(
        norm_sum, scaled, grad_gate, outward, *sums_second
    )
    columns_part = lax.psum_scatter(part, "head", scatter_dimension=0, tiled=True)[0]
    row_sums = [row_sum, *others(row_sum, "head", 1)]
    row_sum = sum(part[0] for part in row_sums)
    kept = weights_backward([middle_grad, normed], [scaled, grad_gate], True)
    sent, early = core_sum(kept, traded(early_sent, "seq", 1), norm_sum)
    sent, late_arrived = tied(sent, traded(late_sent, "seq", 2))
    late = late + late_arrived
    late, sent, norm_sum, taps_x, gain_sum, skip_sum, bias_sum, rate_sum, taps_bc = tied(
        late, sent, norm_sum, taps_x, gain_sum, skip_sum, bias_sum, rate_sum, taps_bc
    )
    local_first, whole_first = vectors_of(
        heads, taps_x, gain_sum, skip_sum, bias_sum, rate_sum, norm_sum, taps_bc
    )
    vector = jnp.stack(
        [
            jnp.concatenate([whole_first, local_first]),
            jnp.concatenate([whole_second, local_second]),
        ]
    )
    vector = butterfly(vector, "seq")
    first_share = norm_backward(
        columns_part, row_sum, own_columns(first), kept_first["rescale"],
        own_columns(middle_grad), own_columns(weights[0]["norm"]), model,
    )
    vector = section_sum(vector[0], vector[1], first_share)
    late = section_sum(late, late_second, first_share)
    early = section_sum(early + traded(sent, "seq", 2), early_second, first_share)
    whole = butterfly(vector[: whole_first.shape[0]], "head")
    local = vector[whole_first.shape[0] :]
    last_share = lax.rsqrt(sum(part[0] for part in sums_second) / INNER + epsilon)
    last_share = last_share[:, None] * outward[0].astype(f32)
    last_share = (own_columns(second).astype(f32) + last_share).astype(bf16)
    block_outputs = both_sequences(own_columns(second), last_share, first_share)
    grad_w_bc = late[:, :shared].astype(bf16).reshape(quarter, head_size, shared // head_size)
    grad_w_bc = grad_w_bc.swapaxes(0, 1)
    for bit in bits:
        grad_w_bc = halved(grad_w_bc, "head", bit)
    input_grads = both_sequences(first_share, own_columns(middle_grad))
    at = 0

    def taken(size):
        nonlocal at
        at += size
        return local[at - size : at]

    grad_norm = lax.dynamic_slice_in_dim(whole, head_at * share, share, 0)
    grad_conv_bc = whole[model:].reshape(CONV, shared).T
    grad_conv_x = taken(CONV * width).reshape(CONV, width).T
    grad_gain = taken(width)
    grad_skip = jnp.sum(taken(width).reshape(heads, width // heads), axis=1)
    grad_bias = taken(heads)
    grad_rate = taken(heads)
    return (
        block_outputs[None],
        input_grads[None],
        grad_norm[None],
        early[None, :, width:],
        late[None, :, shared + LANES :],
        grad_w_bc.astype(f32),
        late[None, :, shared : shared + heads],
        grad_conv_x[None],
        grad_conv_bc[None],
        grad_bias[None],
        grad_rate[None],
        grad_skip[None],
        grad_gain[None],
        early[None, :, :width],
    )


def solution(mesh):
    placed = (
        P(None, "seq", None),
        P(None, "seq", None),
        P("section", None),
        P("section", None, "head"),
        P("section", None, "head"),
        P("section", None, None),
        P("section", None, "head"),
        P("section", "head", None),
        P("section", None, None),
        P("section", "head"),
        P("section", "head"),
        P("section", "head"),
        P("section", "head"),
        P("section", None, "head"),
    )
    return jax.shard_map(
        shards,
        mesh=mesh,
        in_specs=placed,
        out_specs=(
            P("section", None, "seq", "head"),
            P("section", None, "seq", "head"),
            P("section", "head"),
            P("section", "seq", "head"),
            P("section", "seq", "head"),
            P("section", "seq", "head"),
            P("section", "seq", "head"),
            P("section", "head", None),
            P("section", None, None),
            P("section", "head"),
            P("section", "head"),
            P("section", "head"),
            P("section", "head"),
            P("section", "seq", "head"),
        ),
        check_vma=False,
    )
```

time: 1110 us -> 750 us (0.68)
  waiting for transfers between devices: 566 us -> 291 us
  blocking collectives: 159 us -> 0 us
  matrix products: 121 us -> 0 us
  Pallas kernels: 105 us -> 223 us
  local copies, waits for them, and re-layouts: 51.2 us -> 94.5 us
  starting transfers between devices: 15.5 us -> 52.4 us
    reduce_scatter x7 -> x2, waiting for transfers between devices: 269 us -> 29.9 us  [the longest x1 29.9 us: shards(): rows_part = lax.psum_scatter(part, 'head', scatter_dimension=0, tiled=True)]
    ppermute x6 -> x58, waiting for transfers between devices: 16.8 us -> 140 us  [the longest x30 125 us: traded(): lax.ppermute(block, axis, [(i, i ^ bit) for i in range(lax.axis_size(axis...]
    dot_general x30 -> x0, matrix products: 121 us -> none  [the longest x10 43.6 us: dot_nn(): lax.dot_general(left, right, (((1,), (0,)), ((), ())), precision=precisio...]
    pallas_call x8 -> x20, Pallas kernels: 105 us -> 223 us  [the longest x2 57.5 us: states_backward(): pl.pallas_call(partial(states_kernel, heads, len(arrived) + 1), grid=(ste...]
    psum x4 -> x0, blocking collectives: 84.8 us -> none  [the longest x1 39.5 us: shards(): lax.psum(whole, ('section', 'seq', 'head'))]
    all_gather x5 -> x1, waiting for transfers between devices: 125 us -> 58.3 us  [shards(): lax.all_gather(second_share.astype(bf16), 'head', axis=0, tiled=True)]
    all_gather x7 -> x0, blocking collectives: 63 us -> none  [the longest x4 40.4 us: entering(): ends = lax.all_gather(end.astype(bf16), 'seq')]
    unnamed x20 -> x5, waiting for transfers between devices: 52.2 us -> 0.08 us
  transfers between devices with their start and end apart: 24 -> 63, of which waited for: 15 -> 25; matrix products, arithmetic and copies ran while one was open for 16% -> 11% of each run, Pallas kernels for 5% -> 19%
where the time goes in v2:
time: 750 us; the launch traced here: 739 us
  waiting for transfers between devices  291 us (39%)
  Pallas kernels  223 us (30%)
  local copies, waits for them, and re-layouts  94.5 us (13%)
  other arithmetic  59 us (8%)
  starting transfers between devices  52.4 us (7%)
  between operations  19.3 us (3%)
    ppermute x30, waiting for transfers between devices, traded(): lax.ppermute(block, axis, [(i, i ^ bit) for i in range(lax.axis_size(axis...  125 us
    all_gather x1, waiting for transfers between devices, shards(): lax.all_gather(second_share.astype(bf16), 'head', axis=0, tiled=True)  58.3 us
    pallas_call x2, Pallas kernels, states_backward(): pl.pallas_call(partial(states_kernel, heads, len(arrived) + 1), grid=(ste...  57.5 us
    unnamed x295, local copies, waits for them, and re-layouts  54.2 us
    reduce_scatter x1, waiting for transfers between devices, shards(): lax.psum_scatter(part, 'head', scatter_dimension=0, tiled=True).astype(f32)  48.6 us
    pallas_call x2, Pallas kernels, project_forward(): pl.pallas_call(partial(project_kernel, heads, block, len(pack)), grid=(co...  34.9 us
    pallas_call x8, Pallas kernels, weights_backward(): pl.pallas_call(partial(weights_kernel, len(lefts)), grid_spec=pltpu.Prefe...  34.2 us
    reduce_scatter x1, waiting for transfers between devices, shards(): rows_part = lax.psum_scatter(part, 'head', scatter_dimension=0, tiled=True)  29.9 us
  transfers between devices with their start and end apart: 63, of which 25 were waited for; matrix products, arithmetic and copies ran while one was open for 11% of the time, Pallas kernels for 19%

profile of v2, /device:TPU:0, one launch (start us, length us, event | category | flops | bytes accessed | tf_op | source)
XLA Modules:
  0.0 738.8 jit_solution(14075492928660433693)
XLA Ops:
  17.1 16.1 %collective-permute-done.refs_1_.refs_4_ = bf16[384,1152]{1,0:T(8,128)(2,1)S(1)} collective-permute-done((bf16[384,1152]{1,0:T(8,128)(2,1)S(1)}, bf16[384,1152]{1,0:T(8,128)(2,1)S(1)}, u32[]{:S(2)}, u32[]{:S(2)}) %collective-permute-start) | collective-permute-done | bytes 884768 | tf_op jit(solution)/shard_map/ppermute | solution.py:1084
  45.3 15.9 %collective-permute-done.4 = f32[6436]{0:T(1024)S(1)} collective-permute-done((f32[6436]{0:T(1024)S(1)}, f32[6436]{0:T(1024)S(1)}, u32[]{:S(2)}, u32[]{:S(2)}) %collective-permute-start.4) | collective-permute-done | bytes 25776 | tf_op jit(solution)/shard_map/ppermute | solution.py:1084
  66.3 17.5 %project_forward.2 = (bf16[1024,1536]{1,0:T(8,128)(2,1)}, f32[1024,1]{1,0:T(8,128)S(1)}, bf16[1024,768]{1,0:T(8,128)(2,1)}, bf16[1024,256]{1,0:T(8,128)(2,1)S(1)...) custom-call(bf16[1024,1536]{1,0:T(8,128)(2,1)} %dynamic-slice_bitcas, ...), custom_call_target="tpu_custom_call" | custom-call | flops 3623878656 | bytes 16121856 | tf_op jit(solution)/shard_map/project_forward/pallas_call | solution.py:254
  90.2 9.4 %inner_forward.2 = (f32[1024,768]{1,0:T(8,128)}, f32[1024,768]{1,0:T(8,128)}) custom-call(bf16[1024,768]{1,0:T(8,128)(2,1)S(1)} %copy-done.1, bf16[1024,256]{1,0:T(8,128)(2,1)S(1)} %get-tuple-element.193.act_bc, f32[1024,128]{1,0:T(8,128)S(1)} %get-tuple-element.194.dt_in, f32[1024,128]{1,0:T(8,128)S(1)} %get-tuple-element.195.run_in, ...), custom_call_target="tpu_custom_call" | custom-call | flops 3221225472 | bytes 13369344 | tf_op jit(solution)/shard_map/inner_forward/pallas_call | solution.py:357
  109.6 13.5 %outer_forward.2 = (bf16[1024,768]{1,0:T(8,128)(2,1)S(1)}, bf16[1024,768]{1,0:T(8,128)(2,1)}, bf16[1024,1536]{1,0:T(8,128)(2,1)}, f32[8,1024]{1,0:T(8,128)S(1)}, bf16[8,128,768]{2,1,0:T(8,128)(2,1)}) custom-call(bf16[1024,768]{1,0:T(8,128)(2,1)} %get-tuple-element.192.act_x, bf16[1024,256]{1,0:T(8,128)(2,1)S(1)} %get-tuple-element.193.act_bc, ...), custom_call_target="tpu_custom_call" | custom-call | flops 2818572288 | bytes 14155776 | tf_op jit(solution)/shard_map/outer_forward/pallas_call | solution.py:485
  129.8 6.3 collective-permute-done.14.refs_5_
  136.1 48.6 %reduce-scatter.4.cloned.1.call-done = bf16[256,1536]{1,0:T(8,128)(2,1)} async-done(((bf16[1024,1536]{1,0:T(8,128)(2,1)}), bf16[256,1536]{1,0:T(8,128)(2,1)}) %reduce-scatter.4.cloned.1.call-update) | async-done | bytes 786448 | tf_op jit(solution)/shard_map/reduce_scatter | solution.py:1320
  192.0 58.3 %all-gather.3.cloned.1.call-done.x_in.refs_7_ = bf16[1024,1536]{1,0:T(8,128)(2,1)} async-done(((bf16[256,1536]{1,0:T(8,128)(2,1)}), bf16[1024,1536]{1,0:T(8,128)(2,1)}) %all-gather.3.cloned.1.call-update) | async-done | bytes 3145744 | tf_op jit(solution)/shard_map/all_gather | solution.py:1324
  255.7 17.4 %project_forward.3 = (bf16[1024,1536]{1,0:T(8,128)(2,1)}, f32[1024,1]{1,0:T(8,128)S(1)}, bf16[1024,768]{1,0:T(8,128)(2,1)}, bf16[1024,256]{1,0:T(8,128)(2,1)S(1)...) custom-call(bf16[1024,1536]{1,0:T(8,128)(2,1)} %all-gather.3.cloned., ...), custom_call_target="tpu_custom_call" | custom-call | flops 3623878656 | bytes 16121856 | tf_op jit(solution)/shard_map/project_forward/pallas_call | solution.py:254
  279.4 9.0 %inner_forward.3 = (f32[1024,768]{1,0:T(8,128)}, f32[1024,768]{1,0:T(8,128)}) custom-call(bf16[1024,768]{1,0:T(8,128)(2,1)S(1)} %copy-done, bf16[1024,256]{1,0:T(8,128)(2,1)S(1)} %get-tuple-element.212.act_bc, f32[1024,128]{1,0:T(8,128)S(1)} %get-tuple-element.213.dt_in, f32[1024,128]{1,0:T(8,128)S(1)} %get-tuple-element.214.run_in, ...), custom_call_target="tpu_custom_call" | custom-call | flops 3221225472 | bytes 13369344 | tf_op jit(solution)/shard_map/inner_forward/pallas_call | solution.py:357
  288.8 13.9 %outer_forward.3 = (bf16[1024,768]{1,0:T(8,128)(2,1)S(1)}, bf16[1024,768]{1,0:T(8,128)(2,1)}, bf16[4,1024,384]{2,1,0:T(8,128)(2,1)}, f32[8,1024]{1,0:T(8,128)S(1)}, bf16[8,128,768]{2,1,0:T(8,128)(2,1)}) custom-call(bf16[1024,768]{1,0:T(8,128)(2,1)} %get-tuple-element.211.act_x, bf16[1024,256]{1,0:T(8,128)(2,1)S(1)} %get-tuple-element.212.act_bc, ...), custom_call_target="tpu_custom_call" | custom-call | flops 2818572288 | bytes 14155776 | tf_op jit(solution)/shard_map/outer_forward/pallas_call | solution.py:485
  312.9 9.9 %gate_backward.2 = (bf16[1024,768]{1,0:T(8,128)(2,1)S(1)}, bf16[1024,768]{1,0:T(8,128)(2,1)}, bf16[1024,768]{1,0:T(8,128)(2,1)}, f32[8,768]{1,0:T(8,128)S(1)}, f...) custom-call(bf16[1024,1536]{1,0:T(8,128)(2,1)} %dynamic-slice_bitcast_fusion.refs_8_.grad.refs_0_, ...), custom_call_target="tpu_custom_call" | custom-call | flops 2617245696 | bytes 12582912 | tf_op jit(solution)/shard_map/gate_backward/pallas_call | solution.py:617
  339.2 28.7 %states_backward.2 = (bf16[1024,1152]{1,0:T(8,128)(2,1)}, f32[16,1152]{1,0:T(8,128)S(1)}, f32[16,1152]{1,0:T(8,128)}, f32[8,768]{1,0:T(8,128)S(1)}, f32[8,256]{1...) custom-call(bf16[1024,768]{1,0:T(8,128)(2,1)} %copy-done.32, bf16[1024,768]{1,0:T(8,128)(2,1)} %get-tuple-element.211.act_x, ...), custom_call_target="tpu_custom_call" | custom-call | flops 2013265920 | bytes 12582912 | tf_op jit(solution)/shard_map/states_backward/pallas_call | solution.py:887
  377.9 13.1 %part_backward.2 = (bf16[1024,1536]{1,0:T(8,128)(2,1)}, f32[8,1024]{1,0:T(8,128)S(1)}, f32[8,1536]{1,0:T(8,128)S(1)}) custom-call(bf16[1024,768]{1,0:T(8,128)(2,1)} %get-tuple-element.247.refs_3_.grad_gate, bf16[1024,1152]{1,0:T(8,128)(2,1)} %fusion.11.packed.refs_1_, bf16[1024,1536]{1,0:T(8,128)(2,1)} %all-gather.3.cloned.1.call-done.x_in.refs_7_, ...), custom_call_target="tpu_custom_call" | custom-call | flops 6039797760 | bytes 18481152 | tf_op jit(solution)/shard_map/part_backward/pallas_call | solution.py:1015
  425.7 29.9 %reduce-scatter.6.cloned.1.call-done = bf16[256,1536]{1,0:T(8,128)(2,1)} async-done(((bf16[1024,1536]{1,0:T(8,128)(2,1)}), bf16[256,1536]{1,0:T(8,128)(2,1)}) %reduce-scatter.6.cloned.1.call-update) | async-done | bytes 786448 | tf_op jit(solution)/shard_map/reduce_scatter | solution.py:1356
  461.0 20.8 %collective-permute-done.34 = bf16[384,1152]{1,0:T(8,128)(2,1)} collective-permute-done((bf16[384,1152]{1,0:T(8,128)(2,1)}, bf16[384,1152]{1,0:T(8,128)(2,1)}, u32[]{:S(2)}, u32[]{:S(2)}) %collective-permute-start.34) | collective-permute-done | bytes 884768 | tf_op jit(solution)/shard_map/ppermute | solution.py:1084
  484.6 21.5 %collective-permute-done.33 = bf16[384,1536]{1,0:T(8,128)(2,1)} collective-permute-done((bf16[384,1536]{1,0:T(8,128)(2,1)}, bf16[384,1536]{1,0:T(8,128)(2,1)}, u32[]{:S(2)}, u32[]{:S(2)}) %collective-permute-start.33) | collective-permute-done | bytes 1179680 | tf_op jit(solution)/shard_map/ppermute | solution.py:1084
  508.9 14.0 %all-gather.5.cloned.1.call-done.grad.refs_0_ = bf16[1024,1536]{1,0:T(8,128)(2,1)} async-done(((bf16[256,1536]{1,0:T(8,128)(2,1)}), bf16[1024,1536]{1,0:T(8,128)(2,1)}) %all-gather.5.cloned.1.call-update) | async-done | bytes 3145744 | tf_op jit(solution)/shard_map/all_gather | solution.py:1371
  525.2 13.4 %gate_backward.3 = (bf16[1024,768]{1,0:T(8,128)(2,1)S(1)}, bf16[1024,768]{1,0:T(8,128)(2,1)}, bf16[1024,768]{1,0:T(8,128)(2,1)}, f32[8,768]{1,0:T(8,128)S(1)}, f...) custom-call(bf16[1024,1536]{1,0:T(8,128)(2,1)} %all-gather.5.cloned.1.call-done.grad.refs_0_, ...), custom_call_target="tpu_custom_call" | custom-call | flops 2617245696 | bytes 12582912 | tf_op jit(solution)/shard_map/gate_backward/pallas_call | solution.py:617
  555.2 28.8 %states_backward.3 = (bf16[1024,1152]{1,0:T(8,128)(2,1)}, f32[16,1152]{1,0:T(8,128)S(1)}, f32[16,1152]{1,0:T(8,128)S(1)}, f32[8,768]{1,0:T(8,128)S(1)}, f32[8,25...) custom-call(bf16[1024,768]{1,0:T(8,128)(2,1)} %copy-done.31, ...), custom_call_target="tpu_custom_call" | custom-call | flops 2013265920 | bytes 12582912 | tf_op jit(solution)/shard_map/states_backward/pallas_call | solution.py:887
  607.1 13.9 %part_backward.3 = (bf16[4,1024,384]{2,1,0:T(8,128)(2,1)}, f32[8,1024]{1,0:T(8,128)S(1)}, f32[8,1536]{1,0:T(8,128)S(1)}) custom-call(bf16[1024,768]{1,0:T(8,128)(2,1)} %get-tuple-element.301.refs_3_.grad_gate, bf16[1024,1152]{1,0:T(8,128)(2,1)} %fusion.12.refs_1_.packed, bf16[1024,1536]{1,0:T(8,128)(2,1)} %dynamic-slice_bitcast_fusion.1.x_in.refs_8_, ...), custom_call_target="tpu_custom_call" | custom-call | flops 6039797760 | bytes 18481152 | tf_op jit(solution)/shard_map/part_backward/pallas_call | solution.py:1015
  640.3 6.7 collective-permute-done.47
  657.5 24.8 %collective-permute-done.53 = bf16[384,1536]{1,0:T(8,128)(2,1)S(1)} collective-permute-done((bf16[384,1536]{1,0:T(8,128)(2,1)S(1)}, bf16[384,1536]{1,0:T(8,128)(2,1)S(1)}, u32[]{:S(2)}, u32[]{:S(2)}) %collective-permute-start.53) | collective-permute-done | bytes 1179680 | tf_op jit(solution)/shard_map/ppermute | solution.py:1084
  701.7 12.8 %collective-permute-done.54 = bf16[384,1536]{1,0:T(8,128)(2,1)} collective-permute-done((bf16[384,1536]{1,0:T(8,128)(2,1)}, bf16[384,1536]{1,0:T(8,128)(2,1)}, u32[]{:S(2)}, u32[]{:S(2)}) %collective-permute-start.54) | collective-permute-done | bytes 1179680 | tf_op jit(solution)/shard_map/ppermute | solution.py:1084
  (570 shorter events, 255.2 us)
Async XLA Ops:
  7.2 177.6 %reduce-scatter.4.cloned.1.call-start = ((), (), s32[]{:S(2)}) async-start(), calls=%async_computation.3 | async-start | bytes 3932160 | tf_op jit(solution)/shard_map/reduce_scatter | solution.py:1320
  14.3 30.8 %collective-permute-start.3 = (bf16[3,1536]{1,0:T(4,128)(2,1)S(1)}, bf16[3,1536]{1,0:T(4,128)(2,1)S(1)}, u32[]{:S(2)}, u32[]{:S(2)}) collective-permute-start(bf16[3,1536]{1,0:T(4,128)(2,1)S(1)} %fusion.15), channel_id=1, source_target_pairs={{0,4},{4,8},{8,12},{12,0},{1,5},{5,9},{9,13},{13,1},{2,6},{6,10},{... | collective-permute-start | bytes 27656 | tf_op jit(solution)/shard_map/ppermute | solution.py:1089
  33.2 28.6 %collective-permute-start.2 = (bf16[2,384,768]{2,1,0:T(8,128)(2,1)}, bf16[2,384,768]{2,1,0:T(8,128)(2,1)S(1)}, u32[]{:S(2)}, u32[]{:S(2)}) collective-permute-start(bf16[2,384,768]{2,1,0:T(8,128)(2,1)} %dynamic-slice_bitcast_fusion.4), channel_id=1, source_target_pairs={{0,16},{16,0},{1,17},{17,1},{2,18},{18,2},{3,19},{19,3},{4,20},{20... | collective-permute-start | bytes 3538952 | tf_op jit(solution)/shard_map/ppermute | solution.py:1084
  61.9 26.9 %collective-permute-start.7 = (bf16[2,384,768]{2,1,0:T(8,128)(2,1)S(1)}, bf16[2,384,768]{2,1,0:T(8,128)(2,1)}, u32[]{:S(2)}, u32[]{:S(2)}) collective-permute-start(bf16[2,384,768]{2,1,0:T(8,128)(2,1)S(1)} %collective-permute-done.2.refs_1_), channel_id=1, source_target_pairs={{0,4},{4,0},{8,12},{12,8},{1,5},{5,1},{9,13},{13,9},{2,6},{6,2},{1... | collective-permute-start | bytes 3538952 | tf_op jit(solution)/shard_map/ppermute | solution.py:1084
  62.4 39.3 %collective-permute-start.8 = (bf16[2,384,768]{2,1,0:T(8,128)(2,1)}, bf16[2,384,768]{2,1,0:T(8,128)(2,1)S(1)}, u32[]{:S(2)}, u32[]{:S(2)}) collective-permute-start(bf16[2,384,768]{2,1,0:T(8,128)(2,1)} %dynamic-slice_bitcast_fusion.3), channel_id=1, source_target_pairs={{0,16},{16,0},{1,17},{17,1},{2,18},{18,2},{3,19},{19,3},{4,20},{20... | collective-permute-start | bytes 3538952 | tf_op jit(solution)/shard_map/ppermute | solution.py:1084
  124.3 126.1 %all-gather.3.cloned.1.call-start = ((), (), s32[]{:S(2)}) async-start(), calls=%async_computation.4 | async-start | bytes 3932160 | tf_op jit(solution)/shard_map/all_gather | solution.py:1324
  187.4 268.2 %reduce-scatter.6.cloned.1.call-start = ((), (), s32[]{:S(2)}) async-start(), calls=%async_computation.5 | async-start | bytes 3932160 | tf_op jit(solution)/shard_map/reduce_scatter | solution.py:1356
  338.4 36.1 %collective-permute-start.27 = (bf16[2,1024,384]{2,1,0:T(8,128)(2,1)}, bf16[2,1024,384]{2,1,0:T(8,128)(2,1)}, u32[]{:S(2)}, u32[]{:S(2)}) collective-permute-start(bf16[2,1024,384]{2,1,0:T(8,128)(2,1)} %dynamic-slice_bitcast_fusion.2), channel_id=1, source_target_pairs={{0,1},{1,0},{2,3},{3,2},{4,5},{5,4},{6,7},{7,6},{8,9},{9,8},{10,11... | collective-permute-start | bytes 4718600 | tf_op jit(solution)/shard_map/ppermute | solution.py:1084
  391.0 131.9 %all-gather.5.cloned.1.call-start = ((), (), s32[]{:S(2)}) async-start(), calls=%async_computation.6 | async-start | bytes 3932160 | tf_op jit(solution)/shard_map/all_gather | solution.py:1371
  391.1 29.4 %collective-permute-start.28 = (bf16[2,384,1536]{2,1,0:T(8,128)(2,1)}, bf16[2,384,1536]{2,1,0:T(8,128)(2,1)}, u32[]{:S(2)}, u32[]{:S(2)}) collective-permute-start(bf16[2,384,1536]{2,1,0:T(8,128)(2,1)} %copy-done.24), channel_id=1, source_target_pairs={{0,4},{4,0},{8,12},{12,8},{1,5},{5,1},{9,13},{13,9},{2,6},{6,2},{1... | collective-permute-start | bytes 7077896 | tf_op jit(solution)/shard_map/ppermute | solution.py:1084
  458.8 228.1 %reduce-scatter.8.cloned.1.call-start = ((), (), s32[]{:S(2)}) async-start(), calls=%async_computation.7 | async-start | bytes 3932160 | tf_op jit(solution)/shard_map/reduce_scatter | solution.py:1399
  460.1 45.9 %collective-permute-start.33 = (bf16[384,1536]{1,0:T(8,128)(2,1)}, bf16[384,1536]{1,0:T(8,128)(2,1)}, u32[]{:S(2)}, u32[]{:S(2)}) collective-permute-start(bf16[384,1536]{1,0:T(8,128)(2,1)} %add_bitcast_fusion.1), channel_id=1, source_target_pairs={{0,8},{4,12},{8,0},{12,4},{1,9},{5,13},{9,1},{13,5},{2,10},{6,14},... | collective-permute-start | bytes 3538952 | tf_op jit(solution)/shard_map/ppermute | solution.py:1084
  553.9 35.5 %collective-permute-start.39 = (bf16[1,1024,384]{2,1,0:T(8,128)(2,1)}, bf16[1,1024,384]{2,1,0:T(8,128)(2,1)}, u32[]{:S(2)}, u32[]{:S(2)}) collective-permute-start(bf16[1,1024,384]{2,1,0:T(8,128)(2,1)} %constant_dynamic-slice_fusion.5), channel_id=1, source_target_pairs={{0,2},{1,3},{2,0},{3,1},{4,6},{5,7},{6,4},{7,5},{8,10},{9,11},{10,... | collective-permute-start | bytes 2359304 | tf_op jit(solution)/shard_map/ppermute | solution.py:1084
  597.5 40.2 %collective-permute-start.46 = (bf16[2,384,1536]{2,1,0:T(8,128)(2,1)}, bf16[2,384,1536]{2,1,0:T(8,128)(2,1)}, u32[]{:S(2)}, u32[]{:S(2)}) collective-permute-start(bf16[2,384,1536]{2,1,0:T(8,128)(2,1)} %copy-done.23), channel_id=1, source_target_pairs={{0,4},{4,0},{8,12},{12,8},{1,5},{5,1},{9,13},{13,9},{2,6},{6,2},{1... | collective-permute-start | bytes 7077896 | tf_op jit(solution)/shard_map/ppermute | solution.py:1084
  621.0 29.7 %collective-permute-start.44 = (f32[8,1024]{1,0:T(8,128)S(1)}, f32[8,1024]{1,0:T(8,128)S(1)}, u32[]{:S(2)}, u32[]{:S(2)}) collective-permute-start(f32[8,1024]{1,0:T(8,128)S(1)} %get-tuple-element.298), channel_id=1, source_target_pairs={{0,3},{1,0},{2,1},{3,2},{4,7},{5,4},{6,5},{7,6},{8,11},{9,8},{10,9... | collective-permute-start | bytes 98312 | tf_op jit(solution)/shard_map/ppermute | solution.py:1089
  623.2 27.6 %collective-permute-start.43 = (f32[8,1024]{1,0:T(8,128)S(1)}, f32[8,1024]{1,0:T(8,128)S(1)}, u32[]{:S(2)}, u32[]{:S(2)}) collective-permute-start(f32[8,1024]{1,0:T(8,128)S(1)} %get-tuple-element.298), channel_id=1, source_target_pairs={{0,2},{1,3},{2,0},{3,1},{4,6},{5,7},{6,4},{7,5},{8,10},{9,11},{10,... | collective-permute-start | bytes 98312 | tf_op jit(solution)/shard_map/ppermute | solution.py:1089
  623.2 27.6 %collective-permute-start.42 = (f32[8,1024]{1,0:T(8,128)S(1)}, f32[8,1024]{1,0:T(8,128)}, u32[]{:S(2)}, u32[]{:S(2)}) collective-permute-start(f32[8,1024]{1,0:T(8,128)S(1)} %get-tuple-element.298), channel_id=1, source_target_pairs={{0,1},{1,2},{2,3},{3,0},{4,5},{5,6},{6,7},{7,4},{8,9},{9,10},{10,1... | collective-permute-start | bytes 98312 | tf_op jit(solution)/shard_map/ppermute | solution.py:1089
  637.7 80.1 %collective-permute-start.41 = (bf16[1024,384]{1,0:T(8,128)(2,1)}, bf16[1024,384]{1,0:T(8,128)(2,1)}, u32[]{:S(2)}, u32[]{:S(2)}) collective-permute-start(bf16[1024,384]{1,0:T(8,128)(2,1)} %fusion.8), channel_id=1, source_target_pairs={{0,16},{16,0},{1,17},{17,1},{2,18},{18,2},{3,19},{19,3},{4,20},{20... | collective-permute-start | bytes 2359304 | tf_op jit(solution)/shard_map/ppermute | solution.py:1084
  654.5 40.2 %collective-permute-start.55 = (bf16[384,1152]{1,0:T(8,128)(2,1)}, bf16[384,1152]{1,0:T(8,128)(2,1)}, u32[]{:S(2)}, u32[]{:S(2)}) collective-permute-start(bf16[384,1152]{1,0:T(8,128)(2,1)} %broadcast_select_fusion.1), channel_id=1, source_target_pairs={{0,16},{16,0},{1,17},{17,1},{2,18},{18,2},{3,19},{19,3},{4,20},{20... | collective-permute-start | bytes 2654216 | tf_op jit(solution)/shard_map/ppermute | solution.py:1084
  654.9 27.5 %collective-permute-start.53 = (bf16[384,1536]{1,0:T(8,128)(2,1)S(1)}, bf16[384,1536]{1,0:T(8,128)(2,1)S(1)}, u32[]{:S(2)}, u32[]{:S(2)}) collective-permute-start(bf16[384,1536]{1,0:T(8,128)(2,1)S(1)} %copy-done.132), channel_id=1, source_target_pairs={{0,8},{4,12},{8,0},{12,4},{1,9},{5,13},{9,1},{13,5},{2,10},{6,14},... | collective-permute-start | bytes 3538952 | tf_op jit(solution)/shard_map/ppermute | solution.py:1084
  656.5 35.6 %collective-permute-start.50 = (f32[7192]{0:T(1024)S(1)}, f32[7192]{0:T(1024)S(1)}, u32[]{:S(2)}, u32[]{:S(2)}) collective-permute-start(f32[7192]{0:T(1024)S(1)} %get-tuple-element.372), channel_id=1, source_target_pairs={{0,16},{16,0},{1,17},{17,1},{2,18},{18,2},{3,19},{19,3},{4,20},{20... | collective-permute-start | bytes 86312 | tf_op jit(solution)/shard_map/ppermute | solution.py:1084
  685.3 29.2 %collective-permute-start.54 = (bf16[384,1536]{1,0:T(8,128)(2,1)}, bf16[384,1536]{1,0:T(8,128)(2,1)}, u32[]{:S(2)}, u32[]{:S(2)}) collective-permute-start(bf16[384,1536]{1,0:T(8,128)(2,1)} %get-tuple-element.374), channel_id=1, source_target_pairs={{0,16},{16,0},{1,17},{17,1},{2,18},{18,2},{3,19},{19,3},{4,20},{20... | collective-permute-start | bytes 3538952 | tf_op jit(solution)/shard_map/ppermute | solution.py:1084
  691.7 37.2 %collective-permute-start.45 = (bf16[1024,384]{1,0:T(8,128)(2,1)}, bf16[1024,384]{1,0:T(8,128)(2,1)S(1)}, u32[]{:S(2)}, u32[]{:S(2)}) collective-permute-start(bf16[1024,384]{1,0:T(8,128)(2,1)} %get-tuple-element.376), channel_id=1, source_target_pairs={{0,16},{16,0},{1,17},{17,1},{2,18},{18,2},{3,19},{19,3},{4,20},{20... | collective-permute-start | bytes 2359304 | tf_op jit(solution)/shard_map/ppermute | solution.py:1084
  692.1 27.7 %collective-permute-start.51 = (f32[2560]{0:T(1024)S(1)}, f32[2560]{0:T(1024)S(1)}, u32[]{:S(2)}, u32[]{:S(2)}) collective-permute-start(f32[2560]{0:T(1024)S(1)} %slice.350), channel_id=1, source_target_pairs={{0,1},{1,0},{2,3},{3,2},{4,5},{5,4},{6,7},{7,6},{8,9},{9,8},{10,11... | collective-permute-start | bytes 30728 | tf_op jit(solution)/shard_map/ppermute | solution.py:1084
  (183 other events, 1668.2 us)
Sparse Core Ops, SparseCore 0:
  124.4 60.2 reduce-scatter.3
  187.5 62.8 all-gather.2
  391.1 64.3 reduce-scatter.5
  458.9 63.9 all-gather.4
  624.4 60.1 reduce-scatter.7

commit v3 on v2

--- a/solution.py
+++ b/solution.py
@@ -33,6 +33,30 @@
 
 def dot_tn(left, right):
     return lax.dot_general(left, right, (((0,), (0,)), ((), ())), preferred_element_type=f32)
+
+
+def three_parts(values):
+    high = values.astype(bf16)
+    rest = values - high.astype(f32)
+    middle = rest.astype(bf16)
+    return high, middle, (rest - middle.astype(f32)).astype(bf16)
+
+
+def lane_sums(values):
+    ones = jnp.ones((8, values.shape[1]), bf16)
+    return sum(dot_nt(ones, part) for part in three_parts(values))
+
+
+def times_mask(values, mask):
+    rows = values.shape[0]
+    product = dot_nn(jnp.concatenate(three_parts(values), axis=0), mask)
+    return product[:rows] + product[rows : 2 * rows] + product[2 * rows :]
+
+
+def mask_times(mask, values):
+    columns = values.shape[1]
+    product = dot_nn(mask, jnp.concatenate(three_parts(values), axis=1))
+    return product[:, :columns] + product[:, columns : 2 * columns] + product[:, 2 * columns :]
 
 
 def silu_parts(values):
@@ -190,11 +214,11 @@
             total = total + ext[5 + k : 5 + k + ROWS] * taps[k : k + 1]
         pre[...] = total.astype(bf16)
         act[...] = silu_parts(total)[1].astype(bf16)
-    lower = triangle(lambda t, s: t >= s).astype(f32)
+    lower = triangle(lambda t, s: t >= s).astype(bf16)
     for sub in range(ROWS // CHUNK):
         at = slice(sub * CHUNK, (sub + 1) * CHUNK)
         dt = sizes[at]
-        run = dot_nn(lower, dt * rate[...], exact)
+        run = mask_times(lower, dt * rate[...])
         run_out[at] = run
         last = run[CHUNK - 1 : CHUNK]
         weight = jnp.exp(last - run) * dt
@@ -241,7 +265,7 @@
 
 def params():
     return pltpu.CompilerParams(
-        dimension_semantics=("arbitrary",), vmem_limit_bytes=48 * 1024 * 1024
+        dimension_semantics=("arbitrary",), vmem_limit_bytes=60 * 1024 * 1024
     )
 
 
@@ -449,7 +473,7 @@
                 fill = jnp.zeros((CHUNK, LANES - lanes), f32)
                 square = jnp.concatenate([square, fill], axis=1)
             squares = squares + square
-        square_rows.append(dot_nt(ones, squares, exact))
+        square_rows.append(lane_sums(squares))
     part = dot_nt(scaled_out[...], w_out[...])
     if pieces == 1:
         part_out[...] = part.astype(bf16)
@@ -466,7 +490,7 @@
             for lane in range(0, part.shape[1], LANES):
                 cols = slice(lane, lane + LANES)
                 pairs = pairs + part[at, cols] * grad_in[at, cols].astype(f32)
-            pair_row = dot_nt(ones, pairs, exact)
+            pair_row = lane_sums(pairs)
         sums_out[:, at] = jnp.where(row == 0, square_rows[sub], pair_row)
 
 
@@ -719,8 +743,8 @@
         square_ref[...] = jnp.zeros_like(square_ref)
 
     upto = triangle(lambda s, t: s <= t)
-    not_before = triangle(lambda s, t: s >= t).astype(f32)
-    before = triangle(lambda s, t: s < t).astype(f32)
+    not_before = triangle(lambda s, t: s >= t).astype(bf16)
+    before = triangle(lambda s, t: s < t).astype(bf16)
     head_lane = lax.broadcasted_iota(jnp.int32, (CHUNK, LANES), 1)
     for sub in reversed(range(ROWS // CHUNK)):
         at = slice(sub * CHUNK, (sub + 1) * CHUNK)
@@ -792,12 +816,12 @@
         kept = dot_nt(member, carry_ref[0])
         fed = dot_nt(member, carry_ref[1])
         wide_row = jnp.concatenate(through, axis=1)
-        across = dot_nt(member.astype(f32), jnp.broadcast_to(wide_row, (8, wide_row.shape[1])), exact)
+        across = jnp.sum(member.astype(f32) * wide_row, axis=1, keepdims=True)
         inside_rows = inside_tile.T[0:padded]
         d_log = (
-            dot_nn(rows_ref[...] - dt_turned * inside_rows + fed, not_before, exact)
-            + dot_nn(dt_turned * kept, before, exact)
-            + across[:, 0:1]
+            times_mask(rows_ref[...] - dt_turned * inside_rows + fed, not_before)
+            + times_mask(dt_turned * kept, before)
+            + across
         )
         d_log_rate = d_log * rate_rows[...]
         rate_sum[...] += d_log_rate * dt_turned
@@ -997,7 +1021,7 @@
         pulled = part_ref[:, cols] * (x_in[:, cols].astype(f32) * rescale)
         norm_sum[0:1, cols] += jnp.sum(pulled, axis=0, keepdims=True)
         total = total + pulled * gain[:, cols]
-    row_sum[...] = dot_nt(jnp.ones((8, LANES), f32), total, exact)
+    row_sum[...] = lane_sums(total)
     if pieces == 1:
         part_out[...] = part_ref[...].astype(bf16)
     else:
@@ -1106,11 +1130,17 @@
     return block
 
 
-def halved(pieces, axis, bit):
+def parted(pieces, axis, bit):
     pairs = pieces.reshape((pieces.shape[0] // 2, 2) + pieces.shape[1:])
     mine = lax.rem(lax.axis_index(axis) // bit, 2)
-    kept = lax.dynamic_index_in_dim(pairs, mine, 1, False)
-    sent = lax.dynamic_index_in_dim(pairs, 1 - mine, 1, False)
+    return (
+        lax.dynamic_index_in_dim(pairs, mine, 1, False),
+        lax.dynamic_index_in_dim(pairs, 1 - mine, 1, False),
+    )
+
+
+def halved(pieces, axis, bit):
+    kept, sent = parted(pieces, axis, bit)
     return kept + traded(sent, axis, bit)
 
 
@@ -1340,15 +1370,18 @@
     packed, tail, back, taps_x, taps_bc, rate_sum, bias_sum = states_step(
         grad_mixed, arrived, kept_second, weights[1]
     )
-    outward = after(halved(outward, "head", bits[0]), tail)
-    packed, outward = tied(fixed_tail(packed, tail, back), outward)
+    kept, sent = parted(outward, "head", bits[0])
+    packed, kept, arrived = tied(
+        fixed_tail(packed, tail, back), kept, traded(sent, "head", bits[0])
+    )
     part, row_sum, norm_sum = part_backward(
         1, 1, grad_gate, packed, weights[1]["w_z"], weights[1]["pack"], second,
         weights[1]["norm"],
     )
-    norm_sum, taps_x, gain_sum, skip_sum, bias_sum, rate_sum, taps_bc = tied(
-        norm_sum, taps_x, gain_sum, skip_sum, bias_sum, rate_sum, taps_bc
-    )
+    norm_sum, kept, taps_x, gain_sum, skip_sum, bias_sum, rate_sum, taps_bc = tied(
+        norm_sum, kept, taps_x, gain_sum, skip_sum, bias_sum, rate_sum, taps_bc
+    )
+    outward = kept + arrived
     local_second, whole_second = vectors_of(
         heads, taps_x, gain_sum, skip_sum, bias_sum, rate_sum, norm_sum, taps_bc
     )
@@ -1369,22 +1402,27 @@
         own_rows(last_grad), weights[1]["norm"], model,
     )
     middle_grad = lax.all_gather(middle_share, "head", axis=0, tiled=True)
-    middle_grad, early_second, late_second, outward = tied(middle_grad, early, late, outward)
+    middle_grad, early_second, late_second, outward, local_second, whole_second = tied(
+        middle_grad, early, late, outward, local_second, whole_second
+    )
+    for bit in bits[1:-1]:
+        outward = halved(outward, "head", bit)
+    out_kept, out_sent = parted(outward, "head", bits[-1])
 
     grad_mixed, grad_gate, scaled, gain_sum, skip_sum, adjoint = gate_step(
         0, middle_grad, sums_first, (second, first), kept_first, weights[0]
     )
     normed = kept_first["normed"]
     early_sent = weights_backward([middle_grad, normed], [scaled, grad_gate], False)
-    grad_mixed, early_sent, outward, *arrived = tied(
-        grad_mixed, early_sent, outward, *others(adjoint, "seq", -1)
+    grad_mixed, early_sent, out_sent, *arrived = tied(
+        grad_mixed, early_sent, out_sent, *others(adjoint, "seq", -1)
     )
     packed, tail, back, taps_x, taps_bc, rate_sum, bias_sum = states_step(
         grad_mixed, arrived, kept_first, weights[0]
     )
-    for bit in bits[1:]:
-        outward = after(halved(outward, "head", bit), tail)
-    packed, outward = tied(fixed_tail(packed, tail, back), outward)
+    packed, out_arrived = tied(
+        fixed_tail(packed, tail, back), traded(out_sent, "head", bits[-1])
+    )
     late_sent = weights_backward([normed], [packed], False)
     kept = weights_backward([normed], [packed], True)
     late_sent, late = core_sum(kept, traded(late_sent, "seq", 1), tail)
@@ -1393,9 +1431,10 @@
         head_size, 0, grad_gate, packed, weights[0]["w_z"], weights[0]["pack"], first,
         weights[0]["norm"],
     )
-    norm_sum, scaled, grad_gate, outward, *sums_second = tied(
-        norm_sum, scaled, grad_gate, outward, *sums_second
-    )
+    norm_sum, scaled, grad_gate, out_kept, *sums_second = tied(
+        norm_sum, scaled, grad_gate, out_kept, *sums_second
+    )
+    outward = out_kept + out_arrived
     columns_part = lax.psum_scatter(part, "head", scatter_dimension=0, tiled=True)[0]
     row_sums = [row_sum, *others(row_sum, "head", 1)]
     row_sum = sum(part[0] for part in row_sums)

time: 750 us -> 730 us (0.973)
  local copies, waits for them, and re-layouts: 94.5 us -> 55.2 us
  Pallas kernels: 223 us -> 242 us
    unnamed x295 -> x135, local copies, waits for them, and re-layouts: 54.2 us -> 6.67 us
    pallas_call x8, Pallas kernels: 34.2 us -> 47.3 us  [weights_backward(): pl.pallas_call(partial(weights_kernel, len(lefts)), grid_spec=pltpu.Prefe...]
    ppermute x30, waiting for transfers between devices: 125 us -> 113 us  [traded(): lax.ppermute(block, axis, [(i, i ^ bit) for i in range(lax.axis_size(axis...]
    add x6 -> x4, other arithmetic: 16.4 us -> 9.45 us  [after(): value + (0.0 * earlier.reshape(-1)[0].astype(f32)).astype(value.dtype)]
  transfers between devices with their start and end apart: 63 -> 63, of which waited for: 25 -> 26; matrix products, arithmetic and copies ran while one was open for 11% -> 13% of each run, Pallas kernels for 19% -> 21%
where the time goes in v3:
time: 730 us; the launch traced here: 720 us
  waiting for transfers between devices  287 us (39%)
  Pallas kernels  242 us (33%)
  other arithmetic  60 us (8%)
  starting transfers between devices  58 us (8%)
  local copies, waits for them, and re-layouts  55.2 us (8%)
  between operations  18.1 us (2%)
    ppermute x30, waiting for transfers between devices, traded(): lax.ppermute(block, axis, [(i, i ^ bit) for i in range(lax.axis_size(axis...  113 us
    all_gather x1, waiting for transfers between devices, shards(): lax.all_gather(second_share.astype(bf16), 'head', axis=0, tiled=True)  58.7 us
    pallas_call x2, Pallas kernels, states_backward(): pl.pallas_call(partial(states_kernel, heads, len(arrived) + 1), grid=(ste...  57.7 us
    reduce_scatter x1, waiting for transfers between devices, shards(): lax.psum_scatter(part, 'head', scatter_dimension=0, tiled=True).astype(f32)  48.8 us
    pallas_call x8, Pallas kernels, weights_backward(): pl.pallas_call(partial(weights_kernel, len(lefts)), grid_spec=pltpu.Prefe...  47.3 us
    pallas_call x2, Pallas kernels, project_forward(): pl.pallas_call(partial(project_kernel, heads, block, len(pack)), grid=(co...  34.1 us
    reduce_scatter x1, waiting for transfers between devices, shards(): rows_part = lax.psum_scatter(part, 'head', scatter_dimension=0, tiled=True)  34 us
    ppermute x28, starting transfers between devices, rotated(): lax.ppermute(block, axis, [(i, (i + distance) % size) for i in range(size)])  29.6 us
  transfers between devices with their start and end apart: 63, of which 26 were waited for; matrix products, arithmetic and copies ran while one was open for 13% of the time, Pallas kernels for 21%

profile of v3, /device:TPU:0, one launch (start us, length us, event | category | flops | bytes accessed | tf_op | source)
XLA Modules:
  0.0 719.8 jit_solution(6599482031022954727)
XLA Ops:
  18.1 16.3 %collective-permute-done.refs_1_.refs_4_ = bf16[384,1152]{1,0:T(8,128)(2,1)} collective-permute-done((bf16[384,1152]{1,0:T(8,128)(2,1)}, bf16[384,1152]{1,0:T(8,128)(2,1)}, u32[]{:S(2)}, u32[]{:S(2)}) %collective-permute-start) | collective-permute-done | bytes 884768 | tf_op jit(solution)/shard_map/ppermute | solution.py:1108
  45.6 16.7 %collective-permute-done.4 = f32[6436]{0:T(1024)S(1)} collective-permute-done((f32[6436]{0:T(1024)S(1)}, f32[6436]{0:T(1024)S(1)}, u32[]{:S(2)}, u32[]{:S(2)}) %collective-permute-start.4) | collective-permute-done | bytes 25776 | tf_op jit(solution)/shard_map/ppermute | solution.py:1108
  66.8 17.1 %project_forward.2 = (bf16[1024,1536]{1,0:T(8,128)(2,1)}, f32[1024,1]{1,0:T(8,128)}, bf16[1024,768]{1,0:T(8,128)(2,1)}, bf16[1024,256]{1,0:T(8,128)(2,1)}, f32[8...) custom-call(bf16[1024,1536]{1,0:T(8,128)(2,1)} %dynamic-slice_bitcas, ...), custom_call_target="tpu_custom_call" | custom-call | flops 3623878656 | bytes 16121856 | tf_op jit(solution)/shard_map/project_forward/pallas_call | solution.py:278
  85.7 10.0 %inner_forward.2 = (f32[1024,768]{1,0:T(8,128)}, f32[1024,768]{1,0:T(8,128)}) custom-call(bf16[1024,768]{1,0:T(8,128)(2,1)} %get-tuple-element.196.act_x, bf16[1024,256]{1,0:T(8,128)(2,1)} %get-tuple-element.197.act_bc, f32[1024,128]{1,0:T(8,128)} %get-tuple-element.198.dt_in, f32[1024,128]{1,0:T(8,128)} %get-tuple-element.199.run_in, ...), custom_call_target="tpu_custom_call" | custom-call | flops 3221225472 | bytes 13369344 | tf_op jit(solution)/shard_map/inner_forward/pallas_call | solution.py:381
  100.7 13.6 %outer_forward.2 = (bf16[1024,768]{1,0:T(8,128)(2,1)}, bf16[1024,768]{1,0:T(8,128)(2,1)}, bf16[1024,1536]{1,0:T(8,128)(2,1)}, f32[8,1024]{1,0:T(8,128)}, bf16[8,128,768]{2,1,0:T(8,128)(2,1)}) custom-call(bf16[1024,768]{1,0:T(8,128)(2,1)} %get-tuple-element.196.act_x, bf16[1024,256]{1,0:T(8,128)(2,1)} %get-tuple-element.197.act_bc, ...), custom_call_target="tpu_custom_call" | custom-call | flops 2818572288 | bytes 14155776 | tf_op jit(solution)/shard_map/outer_forward/pallas_call | solution.py:509
  126.7 48.8 %reduce-scatter.4.cloned.1.call-done = bf16[256,1536]{1,0:T(8,128)(2,1)} async-done(((bf16[1024,1536]{1,0:T(8,128)(2,1)}), bf16[256,1536]{1,0:T(8,128)(2,1)}) %reduce-scatter.4.cloned.1.call-update) | async-done | bytes 786448 | tf_op jit(solution)/shard_map/reduce_scatter | solution.py:1350
  182.5 58.7 %all-gather.3.cloned.1.call-done.x_in.refs_7_ = bf16[1024,1536]{1,0:T(8,128)(2,1)} async-done(((bf16[256,1536]{1,0:T(8,128)(2,1)}), bf16[1024,1536]{1,0:T(8,128)(2,1)}) %all-gather.3.cloned.1.call-update) | async-done | bytes 3145744 | tf_op jit(solution)/shard_map/all_gather | solution.py:1354
  246.6 17.0 %project_forward.3 = (bf16[1024,1536]{1,0:T(8,128)(2,1)}, f32[1024,1]{1,0:T(8,128)}, bf16[1024,768]{1,0:T(8,128)(2,1)}, bf16[1024,256]{1,0:T(8,128)(2,1)}, f32[8...) custom-call(bf16[1024,1536]{1,0:T(8,128)(2,1)} %all-gather.3.cloned., ...), custom_call_target="tpu_custom_call" | custom-call | flops 3623878656 | bytes 16121856 | tf_op jit(solution)/shard_map/project_forward/pallas_call | solution.py:278
  266.9 9.9 %inner_forward.3 = (f32[1024,768]{1,0:T(8,128)}, f32[1024,768]{1,0:T(8,128)}) custom-call(bf16[1024,768]{1,0:T(8,128)(2,1)} %get-tuple-element.215.act_x, bf16[1024,256]{1,0:T(8,128)(2,1)} %get-tuple-element.216.act_bc, f32[1024,128]{1,0:T(8,128)} %get-tuple-element.217.dt_in, f32[1024,128]{1,0:T(8,128)} %get-tuple-element.218.run_in, ...), custom_call_target="tpu_custom_call" | custom-call | flops 3221225472 | bytes 13369344 | tf_op jit(solution)/shard_map/inner_forward/pallas_call | solution.py:381
  278.4 15.1 %outer_forward.3 = (bf16[1024,768]{1,0:T(8,128)(2,1)}, bf16[1024,768]{1,0:T(8,128)(2,1)}, bf16[4,1024,384]{2,1,0:T(8,128)(2,1)}, f32[8,1024]{1,0:T(8,128)}, bf16[8,128,768]{2,1,0:T(8,128)(2,1)}) custom-call(bf16[1024,768]{1,0:T(8,128)(2,1)} %get-tuple-element.215.act_x, bf16[1024,256]{1,0:T(8,128)(2,1)} %get-tuple-element.216.act_bc, ...), custom_call_target="tpu_custom_call" | custom-call | flops 2818572288 | bytes 14155776 | tf_op jit(solution)/shard_map/outer_forward/pallas_call | solution.py:509
  301.3 12.2 %gate_backward.2 = (bf16[1024,768]{1,0:T(8,128)(2,1)}, bf16[1024,768]{1,0:T(8,128)(2,1)}, bf16[1024,768]{1,0:T(8,128)(2,1)}, f32[8,768]{1,0:T(8,128)}, f32[8,768]{1,0:T(8,128)}, /*index=5*/bf16[128,768]{1,0:T(8,128)(2,1)}) custom-call(bf16[1024,1536]{1,0:T(8,128)(2,1)} %dynamic-slice_bitcast_fusion.refs_8_.grad.refs_0_, ...), custom_call_target="tpu_custom_call" | custom-call | flops 2617245696 | bytes 12582912 | tf_op jit(solution)/shard_map/gate_backward/pallas_call | solution.py:641
  316.2 6.4 weights_backward.8
  327.0 28.8 %states_backward.2 = (bf16[1024,1152]{1,0:T(8,128)(2,1)}, f32[16,1152]{1,0:T(8,128)}, f32[16,1152]{1,0:T(8,128)}, f32[8,768]{1,0:T(8,128)}, f32[8,256]{1,0:T(8,1...) custom-call(bf16[1024,768]{1,0:T(8,128)(2,1)} %get-tuple-element.231.grad_mixed, bf16[1024,768]{1,0:T(8,128)(2,1)} %get-tuple-element.215.act_x, ...), custom_call_target="tpu_custom_call" | custom-call | flops 2013265920 | bytes 12582912 | tf_op jit(solution)/shard_map/states_backward/pallas_call | solution.py:911
  362.9 13.8 %part_backward.2 = (bf16[1024,1536]{1,0:T(8,128)(2,1)}, f32[8,1024]{1,0:T(8,128)}, f32[8,1536]{1,0:T(8,128)}) custom-call(bf16[1024,768]{1,0:T(8,128)(2,1)} %get-tuple-element.251.refs_3_.grad_gate, bf16[1024,1152]{1,0:T(8,128)(2,1)} %fusion.10.packed.refs_1_, bf16[1024,1536]{1,0:T(8,128)(2,1)} %all-gather.3.cloned.1.call-done.x_in.refs_7_, ...), custom_call_target="tpu_custom_call" | custom-call | flops 6039797760 | bytes 18481152 | tf_op jit(solution)/shard_map/part_backward/pallas_call | solution.py:1039
  404.3 34.0 %reduce-scatter.6.cloned.1.call-done = bf16[256,1536]{1,0:T(8,128)(2,1)} async-done(((bf16[1024,1536]{1,0:T(8,128)(2,1)}), bf16[256,1536]{1,0:T(8,128)(2,1)}) %reduce-scatter.6.cloned.1.call-update) | async-done | bytes 786448 | tf_op jit(solution)/shard_map/reduce_scatter | solution.py:1389
  449.7 14.7 %collective-permute-done.34 = bf16[384,1152]{1,0:T(8,128)(2,1)} collective-permute-done((bf16[384,1152]{1,0:T(8,128)(2,1)S(1)}, bf16[384,1152]{1,0:T(8,128)(2,1)}, u32[]{:S(2)}, u32[]{:S(2)}) %collective-permute-start.34) | collective-permute-done | bytes 884768 | tf_op jit(solution)/shard_map/ppermute | solution.py:1108
  466.3 22.1 %collective-permute-done.33 = bf16[384,1536]{1,0:T(8,128)(2,1)} collective-permute-done((bf16[384,1536]{1,0:T(8,128)(2,1)}, bf16[384,1536]{1,0:T(8,128)(2,1)}, u32[]{:S(2)}, u32[]{:S(2)}) %collective-permute-start.33) | collective-permute-done | bytes 1179680 | tf_op jit(solution)/shard_map/ppermute | solution.py:1108
  491.2 14.1 %all-gather.5.cloned.1.call-done.grad.refs_0_ = bf16[1024,1536]{1,0:T(8,128)(2,1)} async-done(((bf16[256,1536]{1,0:T(8,128)(2,1)}), bf16[1024,1536]{1,0:T(8,128)(2,1)}) %all-gather.5.cloned.1.call-update) | async-done | bytes 3145744 | tf_op jit(solution)/shard_map/all_gather | solution.py:1404
  505.3 14.4 %gate_backward.3 = (bf16[1024,768]{1,0:T(8,128)(2,1)}, bf16[1024,768]{1,0:T(8,128)(2,1)}, bf16[1024,768]{1,0:T(8,128)(2,1)}, f32[8,768]{1,0:T(8,128)}, f32[8,768]{1,0:T(8,128)}, /*index=5*/bf16[128,768]{1,0:T(8,128)(2,1)}) custom-call(bf16[1024,1536]{1,0:T(8,128)(2,1)} %all-gather.5.cloned.1.call-done.grad.refs_0_, f32[1024,768]{1,0:T(8,128)} %get-tuple-element.202.gate_in, ...), custom_call_target="tpu_custom_call" | custom-call | flops 2617245696 | bytes 12582912 | tf_op jit(solution)/shard_map/gate_backward/pallas_call | solution.py:641
  523.9 6.6 weights_backward.12
  532.4 28.9 %states_backward.3 = (bf16[1024,1152]{1,0:T(8,128)(2,1)}, f32[16,1152]{1,0:T(8,128)}, f32[16,1152]{1,0:T(8,128)}, f32[8,768]{1,0:T(8,128)}, f32[8,256]{1,0:T(8,1...) custom-call(bf16[1024,768]{1,0:T(8,128)(2,1)} %get-tuple-element.283.grad_mixed, bf16[1024,768]{1,0:T(8,128)(2,1)} %get-tuple-element.196.act_x, ...), custom_call_target="tpu_custom_call" | custom-call | flops 2013265920 | bytes 12582912 | tf_op jit(solution)/shard_map/states_backward/pallas_call | solution.py:911
  583.1 13.6 %part_backward.3 = (bf16[4,1024,384]{2,1,0:T(8,128)(2,1)}, f32[8,1024]{1,0:T(8,128)}, f32[8,1536]{1,0:T(8,128)}) custom-call(bf16[1024,768]{1,0:T(8,128)(2,1)} %get-tuple-element.313.refs_3_.grad_gate, bf16[1024,1152]{1,0:T(8,128)(2,1)} %fusion.11.refs_1_.packed, bf16[1024,1536]{1,0:T(8,128)(2,1)} %dynamic-slice_bitcast_fusion.1.x_in.refs_8_, ...), custom_call_target="tpu_custom_call" | custom-call | flops 6039797760 | bytes 18481152 | tf_op jit(solution)/shard_map/part_backward/pallas_call | solution.py:1039
  633.5 25.6 %collective-permute-done.53 = bf16[384,1536]{1,0:T(8,128)(2,1)S(1)} collective-permute-done((bf16[384,1536]{1,0:T(8,128)(2,1)}, bf16[384,1536]{1,0:T(8,128)(2,1)S(1)}, u32[]{:S(2)}, u32[]{:S(2)}) %collective-permute-start.53) | collective-permute-done | bytes 1179680 | tf_op jit(solution)/shard_map/ppermute | solution.py:1108
  683.0 8.5 %collective-permute-done.54 = bf16[384,1536]{1,0:T(8,128)(2,1)} collective-permute-done((bf16[384,1536]{1,0:T(8,128)(2,1)}, bf16[384,1536]{1,0:T(8,128)(2,1)}, u32[]{:S(2)}, u32[]{:S(2)}) %collective-permute-start.54) | collective-permute-done | bytes 1179680 | tf_op jit(solution)/shard_map/ppermute | solution.py:1108
  (410 shorter events, 234.8 us)
Async XLA Ops:
  7.2 168.3 %reduce-scatter.4.cloned.1.call-start = ((), (), s32[]{:S(2)}) async-start(), calls=%async_computation.3 | async-start | bytes 3932160 | tf_op jit(solution)/shard_map/reduce_scatter | solution.py:1350
  15.2 29.8 %collective-permute-start.3 = (bf16[3,1536]{1,0:T(4,128)(2,1)S(1)}, bf16[3,1536]{1,0:T(4,128)(2,1)S(1)}, u32[]{:S(2)}, u32[]{:S(2)}) collective-permute-start(bf16[3,1536]{1,0:T(4,128)(2,1)S(1)} %fusion.14), channel_id=1, source_target_pairs={{0,4},{4,8},{8,12},{12,0},{1,5},{5,9},{9,13},{13,1},{2,6},{6,10},{... | collective-permute-start | bytes 27656 | tf_op jit(solution)/shard_map/ppermute | solution.py:1113
  34.4 28.0 %collective-permute-start.2 = (bf16[2,384,768]{2,1,0:T(8,128)(2,1)}, bf16[2,384,768]{2,1,0:T(8,128)(2,1)}, u32[]{:S(2)}, u32[]{:S(2)}) collective-permute-start(bf16[2,384,768]{2,1,0:T(8,128)(2,1)} %dynamic-slice_bitcast_fusion.5), channel_id=1, source_target_pairs={{0,16},{16,0},{1,17},{17,1},{2,18},{18,2},{3,19},{19,3},{4,20},{20... | collective-permute-start | bytes 3538952 | tf_op jit(solution)/shard_map/ppermute | solution.py:1108
  63.0 33.7 %collective-permute-start.8 = (bf16[2,384,768]{2,1,0:T(8,128)(2,1)S(1)}, bf16[2,384,768]{2,1,0:T(8,128)(2,1)S(1)}, u32[]{:S(2)}, u32[]{:S(2)}) collective-permute-start(bf16[2,384,768]{2,1,0:T(8,128)(2,1)S(1)} %dynamic-slice_bitcast_fusion.4), channel_id=1, source_target_pairs={{0,16},{16,0},{1,17},{17,1},{2,18},{18,2},{3,19},{19,3},{4,20},{20... | collective-permute-start | bytes 3538952 | tf_op jit(solution)/shard_map/ppermute | solution.py:1108
  114.3 126.9 %all-gather.3.cloned.1.call-start = ((), (), s32[]{:S(2)}) async-start(), calls=%async_computation.4 | async-start | bytes 3932160 | tf_op jit(solution)/shard_map/all_gather | solution.py:1354
  178.1 260.2 %reduce-scatter.6.cloned.1.call-start = ((), (), s32[]{:S(2)}) async-start(), calls=%async_computation.5 | async-start | bytes 3932160 | tf_op jit(solution)/shard_map/reduce_scatter | solution.py:1389
  325.6 37.2 %collective-permute-start.27 = (bf16[2,1024,384]{2,1,0:T(8,128)(2,1)}, bf16[2,1024,384]{2,1,0:T(8,128)(2,1)S(1)}, u32[]{:S(2)}, u32[]{:S(2)}) collective-permute-start(bf16[2,1024,384]{2,1,0:T(8,128)(2,1)} %get-tuple-element.392), channel_id=1, source_target_pairs={{0,1},{1,0},{2,3},{3,2},{4,5},{5,4},{6,7},{7,6},{8,9},{9,8},{10,11... | collective-permute-start | bytes 4718600 | tf_op jit(solution)/shard_map/ppermute | solution.py:1108
  376.7 128.6 %all-gather.5.cloned.1.call-start = ((), (), s32[]{:S(2)}) async-start(), calls=%async_computation.6 | async-start | bytes 3932160 | tf_op jit(solution)/shard_map/all_gather | solution.py:1404
  376.8 23.6 %collective-permute-start.28 = (bf16[2,384,1536]{2,1,0:T(8,128)(2,1)}, bf16[2,384,1536]{2,1,0:T(8,128)(2,1)}, u32[]{:S(2)}, u32[]{:S(2)}) collective-permute-start(bf16[2,384,1536]{2,1,0:T(8,128)(2,1)} %weights_backward.8), channel_id=1, source_target_pairs={{0,4},{4,0},{8,12},{12,8},{1,5},{5,1},{9,13},{13,9},{2,6},{6,2},{1... | collective-permute-start | bytes 7077896 | tf_op jit(solution)/shard_map/ppermute | solution.py:1108
  441.6 221.5 %reduce-scatter.8.cloned.1.call-start = ((), (), s32[]{:S(2)}) async-start(), calls=%async_computation.7 | async-start | bytes 3932160 | tf_op jit(solution)/shard_map/reduce_scatter | solution.py:1438
  447.4 40.9 %collective-permute-start.33 = (bf16[384,1536]{1,0:T(8,128)(2,1)}, bf16[384,1536]{1,0:T(8,128)(2,1)}, u32[]{:S(2)}, u32[]{:S(2)}) collective-permute-start(bf16[384,1536]{1,0:T(8,128)(2,1)} %add_bitcast_fusion.1), channel_id=1, source_target_pairs={{0,8},{4,12},{8,0},{12,4},{1,9},{5,13},{9,1},{13,5},{2,10},{6,14},... | collective-permute-start | bytes 3538952 | tf_op jit(solution)/shard_map/ppermute | solution.py:1108
  530.6 36.4 %collective-permute-start.39 = (bf16[1,1024,384]{2,1,0:T(8,128)(2,1)S(1)}, bf16[1,1024,384]{2,1,0:T(8,128)(2,1)S(1)}, u32[]{:S(2)}, u32[]{:S(2)}) collective-permute-start(bf16[1,1024,384]{2,1,0:T(8,128)(2,1)S(1)} %copy-done.27), channel_id=1, source_target_pairs={{0,2},{1,3},{2,0},{3,1},{4,6},{5,7},{6,4},{7,5},{8,10},{9,11},{10,... | collective-permute-start | bytes 2359304 | tf_op jit(solution)/shard_map/ppermute | solution.py:1108
  573.1 40.2 %collective-permute-start.46 = (bf16[2,384,1536]{2,1,0:T(8,128)(2,1)}, bf16[2,384,1536]{2,1,0:T(8,128)(2,1)}, u32[]{:S(2)}, u32[]{:S(2)}) collective-permute-start(bf16[2,384,1536]{2,1,0:T(8,128)(2,1)} %weights_backward.12), channel_id=1, source_target_pairs={{0,4},{4,0},{8,12},{12,8},{1,5},{5,1},{9,13},{13,9},{2,6},{6,2},{1... | collective-permute-start | bytes 7077896 | tf_op jit(solution)/shard_map/ppermute | solution.py:1108
  596.7 29.6 %collective-permute-start.44 = (f32[8,1024]{1,0:T(8,128)}, f32[8,1024]{1,0:T(8,128)S(1)}, u32[]{:S(2)}, u32[]{:S(2)}) collective-permute-start(f32[8,1024]{1,0:T(8,128)} %get-tuple-element.310), channel_id=1, source_target_pairs={{0,3},{1,0},{2,1},{3,2},{4,7},{5,4},{6,5},{7,6},{8,11},{9,8},{10,9... | collective-permute-start | bytes 98312 | tf_op jit(solution)/shard_map/ppermute | solution.py:1113
  598.9 27.4 %collective-permute-start.43 = (f32[8,1024]{1,0:T(8,128)}, f32[8,1024]{1,0:T(8,128)S(1)}, u32[]{:S(2)}, u32[]{:S(2)}) collective-permute-start(f32[8,1024]{1,0:T(8,128)} %get-tuple-element.310), channel_id=1, source_target_pairs={{0,2},{1,3},{2,0},{3,1},{4,6},{5,7},{6,4},{7,5},{8,10},{9,11},{10,... | collective-permute-start | bytes 98312 | tf_op jit(solution)/shard_map/ppermute | solution.py:1113
  598.9 27.4 %collective-permute-start.42 = (f32[8,1024]{1,0:T(8,128)}, f32[8,1024]{1,0:T(8,128)S(1)}, u32[]{:S(2)}, u32[]{:S(2)}) collective-permute-start(f32[8,1024]{1,0:T(8,128)} %get-tuple-element.310), channel_id=1, source_target_pairs={{0,1},{1,2},{2,3},{3,0},{4,5},{5,6},{6,7},{7,4},{8,9},{9,10},{10,1... | collective-permute-start | bytes 98312 | tf_op jit(solution)/shard_map/ppermute | solution.py:1113
  613.3 81.6 %collective-permute-start.41 = (bf16[1024,384]{1,0:T(8,128)(2,1)}, bf16[1024,384]{1,0:T(8,128)(2,1)}, u32[]{:S(2)}, u32[]{:S(2)}) collective-permute-start(bf16[1024,384]{1,0:T(8,128)(2,1)} %fusion.7), channel_id=1, source_target_pairs={{0,16},{16,0},{1,17},{17,1},{2,18},{18,2},{3,19},{19,3},{4,20},{20... | collective-permute-start | bytes 2359304 | tf_op jit(solution)/shard_map/ppermute | solution.py:1108
  630.0 43.5 %collective-permute-start.55 = (bf16[384,1152]{1,0:T(8,128)(2,1)}, bf16[384,1152]{1,0:T(8,128)(2,1)}, u32[]{:S(2)}, u32[]{:S(2)}) collective-permute-start(bf16[384,1152]{1,0:T(8,128)(2,1)} %broadcast_select_fusion.1), channel_id=1, source_target_pairs={{0,16},{16,0},{1,17},{17,1},{2,18},{18,2},{3,19},{19,3},{4,20},{20... | collective-permute-start | bytes 2654216 | tf_op jit(solution)/shard_map/ppermute | solution.py:1108
  631.3 27.7 %collective-permute-start.53 = (bf16[384,1536]{1,0:T(8,128)(2,1)}, bf16[384,1536]{1,0:T(8,128)(2,1)S(1)}, u32[]{:S(2)}, u32[]{:S(2)}) collective-permute-start(bf16[384,1536]{1,0:T(8,128)(2,1)} %add_bitcast_fusion), channel_id=1, source_target_pairs={{0,8},{4,12},{8,0},{12,4},{1,9},{5,13},{9,1},{13,5},{2,10},{6,14},... | collective-permute-start | bytes 3538952 | tf_op jit(solution)/shard_map/ppermute | solution.py:1108
  632.2 39.4 %collective-permute-start.50 = (f32[7192]{0:T(1024)S(1)}, f32[7192]{0:T(1024)S(1)}, u32[]{:S(2)}, u32[]{:S(2)}) collective-permute-start(f32[7192]{0:T(1024)S(1)} %get-tuple-element.380), channel_id=1, source_target_pairs={{0,16},{16,0},{1,17},{17,1},{2,18},{18,2},{3,19},{19,3},{4,20},{20... | collective-permute-start | bytes 86312 | tf_op jit(solution)/shard_map/ppermute | solution.py:1108
  662.3 29.2 %collective-permute-start.54 = (bf16[384,1536]{1,0:T(8,128)(2,1)}, bf16[384,1536]{1,0:T(8,128)(2,1)}, u32[]{:S(2)}, u32[]{:S(2)}) collective-permute-start(bf16[384,1536]{1,0:T(8,128)(2,1)} %get-tuple-element.382), channel_id=1, source_target_pairs={{0,16},{16,0},{1,17},{17,1},{2,18},{18,2},{3,19},{19,3},{4,20},{20... | collective-permute-start | bytes 3538952 | tf_op jit(solution)/shard_map/ppermute | solution.py:1108
  670.2 39.5 %collective-permute-start.45 = (bf16[1024,384]{1,0:T(8,128)(2,1)}, bf16[1024,384]{1,0:T(8,128)(2,1)}, u32[]{:S(2)}, u32[]{:S(2)}) collective-permute-start(bf16[1024,384]{1,0:T(8,128)(2,1)} %get-tuple-element.384), channel_id=1, source_target_pairs={{0,16},{16,0},{1,17},{17,1},{2,18},{18,2},{3,19},{19,3},{4,20},{20... | collective-permute-start | bytes 2359304 | tf_op jit(solution)/shard_map/ppermute | solution.py:1108
  672.3 26.3 %collective-permute-start.51 = (f32[2560]{0:T(1024)}, f32[2560]{0:T(1024)}, u32[]{:S(2)}, u32[]{:S(2)}) collective-permute-start(f32[2560]{0:T(1024)} %slice.344), channel_id=1, source_target_pairs={{0,1},{1,0},{2,3},{3,2},{4,5},{5,4},{6,7},{7,6},{8,9},{9,8},{10,11... | collective-permute-start | bytes 30728 | tf_op jit(solution)/shard_map/ppermute | solution.py:1108
  676.8 23.8 %collective-permute-start.56 = (bf16[2,384,64]{1,2,0:T(8,128)(2,1)S(1)}, bf16[2,384,64]{1,2,0:T(8,128)(2,1)S(1)}, u32[]{:S(2)}, u32[]{:S(2)}) collective-permute-start(bf16[2,384,64]{1,2,0:T(8,128)(2,1)S(1)} %dynamic-slice_bitcast_fusion.8), channel_id=1, source_target_pairs={{0,1},{1,0},{2,3},{3,2},{4,5},{5,4},{6,7},{7,6},{8,9},{9,8},{10,11... | collective-permute-start | bytes 294920 | tf_op jit(solution)/shard_map/ppermute | solution.py:1108
  (103 other events, 1197.4 us)
Sparse Core Ops, SparseCore 0:
  114.4 61.0 reduce-scatter.3
  178.2 62.9 all-gather.2
  376.8 61.4 reduce-scatter.5
  441.7 63.5 all-gather.4
  600.8 59.4 reduce-scatter.7

commit v4 on v3

--- a/solution.py
+++ b/solution.py
@@ -59,8 +59,12 @@
     return product[:, :columns] + product[:, columns : 2 * columns] + product[:, 2 * columns :]
 
 
+def sigmoid(values):
+    return 0.5 * jnp.tanh(0.5 * values) + 0.5
+
+
 def silu_parts(values):
-    gate = jax.nn.sigmoid(values)
+    gate = sigmoid(values)
     return gate, values * gate
 
 
@@ -439,8 +443,6 @@
                 payload = arrived[distance - 1]
                 held[...] = decay_of(payload, state) * held[...] + payload[:state].astype(f32)
 
-        weight_wait(out_sources, w_out, out_sem)
-
     square_rows = []
     ones = jnp.ones((8, LANES), f32)
     for sub in range(ROWS // CHUNK):
@@ -474,6 +476,11 @@
                 square = jnp.concatenate([square, fill], axis=1)
             squares = squares + square
         square_rows.append(lane_sums(squares))
+
+    @pl.when(pl.program_id(0) == 0)
+    def _():
+        weight_wait(out_sources, w_out, out_sem)
+
     part = dot_nt(scaled_out[...], w_out[...])
     if pieces == 1:
         part_out[...] = part.astype(bf16)
@@ -811,7 +818,7 @@
             )
             adjoint[:, cols] = lam_decayed + dot_nn(c_turned, dy_grown_low)
             pre = pre_x[at, cols].astype(f32)
-            d_pre_x[8 : CHUNK + 8, cols] = d_x * silu_slope(pre, jax.nn.sigmoid(pre))
+            d_pre_x[8 : CHUNK + 8, cols] = d_x * silu_slope(pre, sigmoid(pre))
         member = members[...]
         kept = dot_nt(member, carry_ref[0])
         fed = dot_nt(member, carry_ref[1])
@@ -826,7 +833,7 @@
         d_log_rate = d_log * rate_rows[...]
         rate_sum[...] += d_log_rate * dt_turned
         square_ref[0:padded] = d_log_rate + inside_rows + kept
-        d_step_exact = square_ref[...].T * jax.nn.sigmoid(step_raw[at] + dt_bias[...])
+        d_step_exact = square_ref[...].T * sigmoid(step_raw[at] + dt_bias[...])
         bias_sum[0:1] += jnp.sum(d_step_exact, axis=0, keepdims=True)
         packed[at, shared : shared + LANES] = d_step_exact.astype(bf16)
         if sub == ROWS // CHUNK - 1:
@@ -839,7 +846,7 @@
         d_b = d_b + dot_nn(d_product_low, c_part)
         d_c = d_c + dot_nn(d_product.T.astype(bf16), b_part)
         pre = pre_bc[at].astype(f32)
-        slope = silu_slope(pre, jax.nn.sigmoid(pre))
+        slope = silu_slope(pre, sigmoid(pre))
         d_pre_bc[8 : CHUNK + 8, :state] = d_b * slope[:, :state]
         d_pre_bc[8 : CHUNK + 8, state:] = d_c * slope[:, state:]
         for d_pre, raw, taps, place, tap_sum in (
@@ -1149,7 +1156,8 @@
 
     def summed(at):
         own = lax.dynamic_index_in_dim(kept, at, 0, False)
-        return after(own + lax.dynamic_index_in_dim(arrived, at, 0, False), earlier)
+        both = own + lax.dynamic_index_in_dim(arrived, at, 0, False)
+        return both if earlier is None else after(both, earlier)
 
     return summed(1 - high), summed(high)
 
@@ -1425,7 +1433,7 @@
     )
     late_sent = weights_backward([normed], [packed], False)
     kept = weights_backward([normed], [packed], True)
-    late_sent, late = core_sum(kept, traded(late_sent, "seq", 1), tail)
+    late_sent, late = core_sum(kept, traded(late_sent, "seq", 1), None)
     packed, late_sent, late = tied(packed, late_sent, late)
     part, row_sum, norm_sum = part_backward(
         head_size, 0, grad_gate, packed, weights[0]["w_z"], weights[0]["pack"], first,

time: 730 us -> 726 us (level)
  no operation moved by 1% of the time
where the time goes in v4:
time: 726 us; the launch traced here: 716 us
  waiting for transfers between devices  287 us (40%)
  Pallas kernels  239 us (33%)
  other arithmetic  59.9 us (8%)
  starting transfers between devices  58.1 us (8%)
  local copies, waits for them, and re-layouts  54.6 us (8%)
  between operations  17.4 us (2%)
    ppermute x30, waiting for transfers between devices, traded(): lax.ppermute(block, axis, [(i, i ^ bit) for i in range(lax.axis_size(axis...  113 us
    all_gather x1, waiting for transfers between devices, shards(): lax.all_gather(second_share.astype(bf16), 'head', axis=0, tiled=True)  58.8 us
    pallas_call x2, Pallas kernels, states_backward(): pl.pallas_call(partial(states_kernel, heads, len(arrived) + 1), grid=(ste...  57.8 us
    reduce_scatter x1, waiting for transfers between devices, shards(): lax.psum_scatter(part, 'head', scatter_dimension=0, tiled=True).astype(f32)  48.8 us
    pallas_call x8, Pallas kernels, weights_backward(): pl.pallas_call(partial(weights_kernel, len(lefts)), grid_spec=pltpu.Prefe...  47.3 us
    pallas_call x2, Pallas kernels, project_forward(): pl.pallas_call(partial(project_kernel, heads, block, len(pack)), grid=(co...  34.5 us
    reduce_scatter x1, waiting for transfers between devices, shards(): rows_part = lax.psum_scatter(part, 'head', scatter_dimension=0, tiled=True)  34 us
    ppermute x28, starting transfers between devices, rotated(): lax.ppermute(block, axis, [(i, (i + distance) % size) for i in range(size)])  29.6 us
  transfers between devices with their start and end apart: 63, of which 26 were waited for; matrix products, arithmetic and copies ran while one was open for 13% of the time, Pallas kernels for 21%

profile of v4, /device:TPU:0, one launch (start us, length us, event | category | flops | bytes accessed | tf_op | source)
XLA Modules:
  0.0 716.0 jit_solution(8601835083672027726)
XLA Ops:
  18.1 16.3 %collective-permute-done.refs_1_.refs_4_ = bf16[384,1152]{1,0:T(8,128)(2,1)} collective-permute-done((bf16[384,1152]{1,0:T(8,128)(2,1)}, bf16[384,1152]{1,0:T(8,128)(2,1)}, u32[]{:S(2)}, u32[]{:S(2)}) %collective-permute-start) | collective-permute-done | bytes 884768 | tf_op jit(solution)/shard_map/ppermute | solution.py:1115
  45.6 16.7 %collective-permute-done.4 = f32[6436]{0:T(1024)S(1)} collective-permute-done((f32[6436]{0:T(1024)S(1)}, f32[6436]{0:T(1024)S(1)}, u32[]{:S(2)}, u32[]{:S(2)}) %collective-permute-start.4) | collective-permute-done | bytes 25776 | tf_op jit(solution)/shard_map/ppermute | solution.py:1115
  66.8 17.3 %project_forward.2 = (bf16[1024,1536]{1,0:T(8,128)(2,1)}, f32[1024,1]{1,0:T(8,128)}, bf16[1024,768]{1,0:T(8,128)(2,1)}, bf16[1024,256]{1,0:T(8,128)(2,1)}, f32[8...) custom-call(bf16[1024,1536]{1,0:T(8,128)(2,1)} %dynamic-slice_bitcas, ...), custom_call_target="tpu_custom_call" | custom-call | flops 3623878656 | bytes 16121856 | tf_op jit(solution)/shard_map/project_forward/pallas_call | solution.py:282
  85.9 10.0 %inner_forward.2 = (f32[1024,768]{1,0:T(8,128)}, f32[1024,768]{1,0:T(8,128)}) custom-call(bf16[1024,768]{1,0:T(8,128)(2,1)} %get-tuple-element.196.act_x, bf16[1024,256]{1,0:T(8,128)(2,1)} %get-tuple-element.197.act_bc, f32[1024,128]{1,0:T(8,128)} %get-tuple-element.198.dt_in, f32[1024,128]{1,0:T(8,128)} %get-tuple-element.199.run_in, ...), custom_call_target="tpu_custom_call" | custom-call | flops 3221225472 | bytes 13369344 | tf_op jit(solution)/shard_map/inner_forward/pallas_call | solution.py:385
  100.8 12.4 %outer_forward.2 = (bf16[1024,768]{1,0:T(8,128)(2,1)}, bf16[1024,768]{1,0:T(8,128)(2,1)}, bf16[1024,1536]{1,0:T(8,128)(2,1)}, f32[8,1024]{1,0:T(8,128)}, bf16[8,128,768]{2,1,0:T(8,128)(2,1)}) custom-call(bf16[1024,768]{1,0:T(8,128)(2,1)} %get-tuple-element.196.act_x, bf16[1024,256]{1,0:T(8,128)(2,1)} %get-tuple-element.197.act_bc, ...), custom_call_target="tpu_custom_call" | custom-call | flops 2818572288 | bytes 14155776 | tf_op jit(solution)/shard_map/outer_forward/pallas_call | solution.py:516
  125.7 48.8 %reduce-scatter.4.cloned.1.call-done = bf16[256,1536]{1,0:T(8,128)(2,1)} async-done(((bf16[1024,1536]{1,0:T(8,128)(2,1)}), bf16[256,1536]{1,0:T(8,128)(2,1)}) %reduce-scatter.4.cloned.1.call-update) | async-done | bytes 786448 | tf_op jit(solution)/shard_map/reduce_scatter | solution.py:1358
  181.4 58.8 %all-gather.3.cloned.1.call-done.x_in.refs_7_ = bf16[1024,1536]{1,0:T(8,128)(2,1)} async-done(((bf16[256,1536]{1,0:T(8,128)(2,1)}), bf16[1024,1536]{1,0:T(8,128)(2,1)}) %all-gather.3.cloned.1.call-update) | async-done | bytes 3145744 | tf_op jit(solution)/shard_map/all_gather | solution.py:1362
  245.6 17.2 %project_forward.3 = (bf16[1024,1536]{1,0:T(8,128)(2,1)}, f32[1024,1]{1,0:T(8,128)}, bf16[1024,768]{1,0:T(8,128)(2,1)}, bf16[1024,256]{1,0:T(8,128)(2,1)}, f32[8...) custom-call(bf16[1024,1536]{1,0:T(8,128)(2,1)} %all-gather.3.cloned., ...), custom_call_target="tpu_custom_call" | custom-call | flops 3623878656 | bytes 16121856 | tf_op jit(solution)/shard_map/project_forward/pallas_call | solution.py:282
  266.0 9.9 %inner_forward.3 = (f32[1024,768]{1,0:T(8,128)}, f32[1024,768]{1,0:T(8,128)}) custom-call(bf16[1024,768]{1,0:T(8,128)(2,1)} %get-tuple-element.215.act_x, bf16[1024,256]{1,0:T(8,128)(2,1)} %get-tuple-element.216.act_bc, f32[1024,128]{1,0:T(8,128)} %get-tuple-element.217.dt_in, f32[1024,128]{1,0:T(8,128)} %get-tuple-element.218.run_in, ...), custom_call_target="tpu_custom_call" | custom-call | flops 3221225472 | bytes 13369344 | tf_op jit(solution)/shard_map/inner_forward/pallas_call | solution.py:385
  277.5 13.3 %outer_forward.3 = (bf16[1024,768]{1,0:T(8,128)(2,1)}, bf16[1024,768]{1,0:T(8,128)(2,1)}, bf16[4,1024,384]{2,1,0:T(8,128)(2,1)}, f32[8,1024]{1,0:T(8,128)}, bf16[8,128,768]{2,1,0:T(8,128)(2,1)}) custom-call(bf16[1024,768]{1,0:T(8,128)(2,1)} %get-tuple-element.215.act_x, bf16[1024,256]{1,0:T(8,128)(2,1)} %get-tuple-element.216.act_bc, ...), custom_call_target="tpu_custom_call" | custom-call | flops 2818572288 | bytes 14155776 | tf_op jit(solution)/shard_map/outer_forward/pallas_call | solution.py:516
  298.6 12.3 %gate_backward.2 = (bf16[1024,768]{1,0:T(8,128)(2,1)}, bf16[1024,768]{1,0:T(8,128)(2,1)}, bf16[1024,768]{1,0:T(8,128)(2,1)}, f32[8,768]{1,0:T(8,128)}, f32[8,768]{1,0:T(8,128)}, /*index=5*/bf16[128,768]{1,0:T(8,128)(2,1)}) custom-call(bf16[1024,1536]{1,0:T(8,128)(2,1)} %dynamic-slice_bitcast_fusion.refs_8_.grad.refs_0_, ...), custom_call_target="tpu_custom_call" | custom-call | flops 2617245696 | bytes 12582912 | tf_op jit(solution)/shard_map/gate_backward/pallas_call | solution.py:648
  313.6 6.4 weights_backward.8
  324.4 28.9 %states_backward.2 = (bf16[1024,1152]{1,0:T(8,128)(2,1)}, f32[16,1152]{1,0:T(8,128)}, f32[16,1152]{1,0:T(8,128)}, f32[8,768]{1,0:T(8,128)}, f32[8,256]{1,0:T(8,1...) custom-call(bf16[1024,768]{1,0:T(8,128)(2,1)} %get-tuple-element.231.grad_mixed, bf16[1024,768]{1,0:T(8,128)(2,1)} %get-tuple-element.215.act_x, ...), custom_call_target="tpu_custom_call" | custom-call | flops 2013265920 | bytes 12582912 | tf_op jit(solution)/shard_map/states_backward/pallas_call | solution.py:918
  360.3 13.8 %part_backward.2 = (bf16[1024,1536]{1,0:T(8,128)(2,1)}, f32[8,1024]{1,0:T(8,128)}, f32[8,1536]{1,0:T(8,128)}) custom-call(bf16[1024,768]{1,0:T(8,128)(2,1)} %get-tuple-element.251.refs_3_.grad_gate, bf16[1024,1152]{1,0:T(8,128)(2,1)} %fusion.10.packed.refs_1_, bf16[1024,1536]{1,0:T(8,128)(2,1)} %all-gather.3.cloned.1.call-done.x_in.refs_7_, ...), custom_call_target="tpu_custom_call" | custom-call | flops 6039797760 | bytes 18481152 | tf_op jit(solution)/shard_map/part_backward/pallas_call | solution.py:1046
  401.7 34.0 %reduce-scatter.6.cloned.1.call-done = bf16[256,1536]{1,0:T(8,128)(2,1)} async-done(((bf16[1024,1536]{1,0:T(8,128)(2,1)}), bf16[256,1536]{1,0:T(8,128)(2,1)}) %reduce-scatter.6.cloned.1.call-update) | async-done | bytes 786448 | tf_op jit(solution)/shard_map/reduce_scatter | solution.py:1397
  447.2 14.7 %collective-permute-done.34 = bf16[384,1152]{1,0:T(8,128)(2,1)} collective-permute-done((bf16[384,1152]{1,0:T(8,128)(2,1)S(1)}, bf16[384,1152]{1,0:T(8,128)(2,1)}, u32[]{:S(2)}, u32[]{:S(2)}) %collective-permute-start.34) | collective-permute-done | bytes 884768 | tf_op jit(solution)/shard_map/ppermute | solution.py:1115
  463.8 22.1 %collective-permute-done.33 = bf16[384,1536]{1,0:T(8,128)(2,1)} collective-permute-done((bf16[384,1536]{1,0:T(8,128)(2,1)}, bf16[384,1536]{1,0:T(8,128)(2,1)}, u32[]{:S(2)}, u32[]{:S(2)}) %collective-permute-start.33) | collective-permute-done | bytes 1179680 | tf_op jit(solution)/shard_map/ppermute | solution.py:1115
  488.6 14.1 %all-gather.5.cloned.1.call-done.grad.refs_0_ = bf16[1024,1536]{1,0:T(8,128)(2,1)} async-done(((bf16[256,1536]{1,0:T(8,128)(2,1)}), bf16[1024,1536]{1,0:T(8,128)(2,1)}) %all-gather.5.cloned.1.call-update) | async-done | bytes 3145744 | tf_op jit(solution)/shard_map/all_gather | solution.py:1412
  502.8 14.4 %gate_backward.3 = (bf16[1024,768]{1,0:T(8,128)(2,1)}, bf16[1024,768]{1,0:T(8,128)(2,1)}, bf16[1024,768]{1,0:T(8,128)(2,1)}, f32[8,768]{1,0:T(8,128)}, f32[8,768]{1,0:T(8,128)}, /*index=5*/bf16[128,768]{1,0:T(8,128)(2,1)}) custom-call(bf16[1024,1536]{1,0:T(8,128)(2,1)} %all-gather.5.cloned.1.call-done.grad.refs_0_, f32[1024,768]{1,0:T(8,128)} %get-tuple-element.202.gate_in, ...), custom_call_target="tpu_custom_call" | custom-call | flops 2617245696 | bytes 12582912 | tf_op jit(solution)/shard_map/gate_backward/pallas_call | solution.py:648
  521.4 6.6 weights_backward.12
  529.9 29.0 %states_backward.3 = (bf16[1024,1152]{1,0:T(8,128)(2,1)}, f32[16,1152]{1,0:T(8,128)}, f32[16,1152]{1,0:T(8,128)}, f32[8,768]{1,0:T(8,128)}, f32[8,256]{1,0:T(8,1...) custom-call(bf16[1024,768]{1,0:T(8,128)(2,1)} %get-tuple-element.283.grad_mixed, bf16[1024,768]{1,0:T(8,128)(2,1)} %get-tuple-element.196.act_x, ...), custom_call_target="tpu_custom_call" | custom-call | flops 2013265920 | bytes 12582912 | tf_op jit(solution)/shard_map/states_backward/pallas_call | solution.py:918
  579.4 13.6 %part_backward.3 = (bf16[4,1024,384]{2,1,0:T(8,128)(2,1)}, f32[8,1024]{1,0:T(8,128)}, f32[8,1536]{1,0:T(8,128)}) custom-call(bf16[1024,768]{1,0:T(8,128)(2,1)} %get-tuple-element.313.refs_3_.grad_gate, bf16[1024,1152]{1,0:T(8,128)(2,1)} %fusion.11.refs_1_.packed, bf16[1024,1536]{1,0:T(8,128)(2,1)} %dynamic-slice_bitcast_fusion.1.x_in.refs_8_, ...), custom_call_target="tpu_custom_call" | custom-call | flops 6039797760 | bytes 18481152 | tf_op jit(solution)/shard_map/part_backward/pallas_call | solution.py:1046
  629.7 25.6 %collective-permute-done.53 = bf16[384,1536]{1,0:T(8,128)(2,1)S(1)} collective-permute-done((bf16[384,1536]{1,0:T(8,128)(2,1)}, bf16[384,1536]{1,0:T(8,128)(2,1)S(1)}, u32[]{:S(2)}, u32[]{:S(2)}) %collective-permute-start.53) | collective-permute-done | bytes 1179680 | tf_op jit(solution)/shard_map/ppermute | solution.py:1115
  679.3 8.5 %collective-permute-done.54 = bf16[384,1536]{1,0:T(8,128)(2,1)} collective-permute-done((bf16[384,1536]{1,0:T(8,128)(2,1)}, bf16[384,1536]{1,0:T(8,128)(2,1)}, u32[]{:S(2)}, u32[]{:S(2)}) %collective-permute-start.54) | collective-permute-done | bytes 1179680 | tf_op jit(solution)/shard_map/ppermute | solution.py:1115
  (406 shorter events, 234.1 us)
Async XLA Ops:
  7.2 167.3 %reduce-scatter.4.cloned.1.call-start = ((), (), s32[]{:S(2)}) async-start(), calls=%async_computation.3 | async-start | bytes 3932160 | tf_op jit(solution)/shard_map/reduce_scatter | solution.py:1358
  15.2 29.8 %collective-permute-start.3 = (bf16[3,1536]{1,0:T(4,128)(2,1)S(1)}, bf16[3,1536]{1,0:T(4,128)(2,1)S(1)}, u32[]{:S(2)}, u32[]{:S(2)}) collective-permute-start(bf16[3,1536]{1,0:T(4,128)(2,1)S(1)} %fusion.14), channel_id=1, source_target_pairs={{0,4},{4,8},{8,12},{12,0},{1,5},{5,9},{9,13},{13,1},{2,6},{6,10},{... | collective-permute-start | bytes 27656 | tf_op jit(solution)/shard_map/ppermute | solution.py:1120
  34.4 28.0 %collective-permute-start.2 = (bf16[2,384,768]{2,1,0:T(8,128)(2,1)}, bf16[2,384,768]{2,1,0:T(8,128)(2,1)}, u32[]{:S(2)}, u32[]{:S(2)}) collective-permute-start(bf16[2,384,768]{2,1,0:T(8,128)(2,1)} %dynamic-slice_bitcast_fusion.5), channel_id=1, source_target_pairs={{0,16},{16,0},{1,17},{17,1},{2,18},{18,2},{3,19},{19,3},{4,20},{20... | collective-permute-start | bytes 3538952 | tf_op jit(solution)/shard_map/ppermute | solution.py:1115
  63.0 33.9 %collective-permute-start.8 = (bf16[2,384,768]{2,1,0:T(8,128)(2,1)S(1)}, bf16[2,384,768]{2,1,0:T(8,128)(2,1)S(1)}, u32[]{:S(2)}, u32[]{:S(2)}) collective-permute-start(bf16[2,384,768]{2,1,0:T(8,128)(2,1)S(1)} %dynamic-slice_bitcast_fusion.4), channel_id=1, source_target_pairs={{0,16},{16,0},{1,17},{17,1},{2,18},{18,2},{3,19},{19,3},{4,20},{20... | collective-permute-start | bytes 3538952 | tf_op jit(solution)/shard_map/ppermute | solution.py:1115
  113.3 126.9 %all-gather.3.cloned.1.call-start = ((), (), s32[]{:S(2)}) async-start(), calls=%async_computation.4 | async-start | bytes 3932160 | tf_op jit(solution)/shard_map/all_gather | solution.py:1362
  177.0 258.7 %reduce-scatter.6.cloned.1.call-start = ((), (), s32[]{:S(2)}) async-start(), calls=%async_computation.5 | async-start | bytes 3932160 | tf_op jit(solution)/shard_map/reduce_scatter | solution.py:1397
  323.1 37.2 %collective-permute-start.27 = (bf16[2,1024,384]{2,1,0:T(8,128)(2,1)}, bf16[2,1024,384]{2,1,0:T(8,128)(2,1)S(1)}, u32[]{:S(2)}, u32[]{:S(2)}) collective-permute-start(bf16[2,1024,384]{2,1,0:T(8,128)(2,1)} %get-tuple-element.392), channel_id=1, source_target_pairs={{0,1},{1,0},{2,3},{3,2},{4,5},{5,4},{6,7},{7,6},{8,9},{9,8},{10,11... | collective-permute-start | bytes 4718600 | tf_op jit(solution)/shard_map/ppermute | solution.py:1115
  374.1 128.7 %all-gather.5.cloned.1.call-start = ((), (), s32[]{:S(2)}) async-start(), calls=%async_computation.6 | async-start | bytes 3932160 | tf_op jit(solution)/shard_map/all_gather | solution.py:1412
  374.2 23.7 %collective-permute-start.28 = (bf16[2,384,1536]{2,1,0:T(8,128)(2,1)}, bf16[2,384,1536]{2,1,0:T(8,128)(2,1)}, u32[]{:S(2)}, u32[]{:S(2)}) collective-permute-start(bf16[2,384,1536]{2,1,0:T(8,128)(2,1)} %weights_backward.8), channel_id=1, source_target_pairs={{0,4},{4,0},{8,12},{12,8},{1,5},{5,1},{9,13},{13,9},{2,6},{6,2},{1... | collective-permute-start | bytes 7077896 | tf_op jit(solution)/shard_map/ppermute | solution.py:1115
  439.0 220.2 %reduce-scatter.8.cloned.1.call-start = ((), (), s32[]{:S(2)}) async-start(), calls=%async_computation.7 | async-start | bytes 3932160 | tf_op jit(solution)/shard_map/reduce_scatter | solution.py:1446
  444.9 40.9 %collective-permute-start.33 = (bf16[384,1536]{1,0:T(8,128)(2,1)}, bf16[384,1536]{1,0:T(8,128)(2,1)}, u32[]{:S(2)}, u32[]{:S(2)}) collective-permute-start(bf16[384,1536]{1,0:T(8,128)(2,1)} %add_bitcast_fusion.1), channel_id=1, source_target_pairs={{0,8},{4,12},{8,0},{12,4},{1,9},{5,13},{9,1},{13,5},{2,10},{6,14},... | collective-permute-start | bytes 3538952 | tf_op jit(solution)/shard_map/ppermute | solution.py:1115
  528.1 36.4 %collective-permute-start.39 = (bf16[1,1024,384]{2,1,0:T(8,128)(2,1)S(1)}, bf16[1,1024,384]{2,1,0:T(8,128)(2,1)S(1)}, u32[]{:S(2)}, u32[]{:S(2)}) collective-permute-start(bf16[1,1024,384]{2,1,0:T(8,128)(2,1)S(1)} %copy-done.27), channel_id=1, source_target_pairs={{0,2},{1,3},{2,0},{3,1},{4,6},{5,7},{6,4},{7,5},{8,10},{9,11},{10,... | collective-permute-start | bytes 2359304 | tf_op jit(solution)/shard_map/ppermute | solution.py:1115
  570.6 38.9 %collective-permute-start.46 = (bf16[2,384,1536]{2,1,0:T(8,128)(2,1)}, bf16[2,384,1536]{2,1,0:T(8,128)(2,1)}, u32[]{:S(2)}, u32[]{:S(2)}) collective-permute-start(bf16[2,384,1536]{2,1,0:T(8,128)(2,1)} %weights_backward.12), channel_id=1, source_target_pairs={{0,4},{4,0},{8,12},{12,8},{1,5},{5,1},{9,13},{13,9},{2,6},{6,2},{1... | collective-permute-start | bytes 7077896 | tf_op jit(solution)/shard_map/ppermute | solution.py:1115
  593.0 29.5 %collective-permute-start.44 = (f32[8,1024]{1,0:T(8,128)}, f32[8,1024]{1,0:T(8,128)S(1)}, u32[]{:S(2)}, u32[]{:S(2)}) collective-permute-start(f32[8,1024]{1,0:T(8,128)} %get-tuple-element.310), channel_id=1, source_target_pairs={{0,3},{1,0},{2,1},{3,2},{4,7},{5,4},{6,5},{7,6},{8,11},{9,8},{10,9... | collective-permute-start | bytes 98312 | tf_op jit(solution)/shard_map/ppermute | solution.py:1120
  595.1 27.4 %collective-permute-start.43 = (f32[8,1024]{1,0:T(8,128)}, f32[8,1024]{1,0:T(8,128)S(1)}, u32[]{:S(2)}, u32[]{:S(2)}) collective-permute-start(f32[8,1024]{1,0:T(8,128)} %get-tuple-element.310), channel_id=1, source_target_pairs={{0,2},{1,3},{2,0},{3,1},{4,6},{5,7},{6,4},{7,5},{8,10},{9,11},{10,... | collective-permute-start | bytes 98312 | tf_op jit(solution)/shard_map/ppermute | solution.py:1120
  595.1 27.4 %collective-permute-start.42 = (f32[8,1024]{1,0:T(8,128)}, f32[8,1024]{1,0:T(8,128)S(1)}, u32[]{:S(2)}, u32[]{:S(2)}) collective-permute-start(f32[8,1024]{1,0:T(8,128)} %get-tuple-element.310), channel_id=1, source_target_pairs={{0,1},{1,2},{2,3},{3,0},{4,5},{5,6},{6,7},{7,4},{8,9},{9,10},{10,1... | collective-permute-start | bytes 98312 | tf_op jit(solution)/shard_map/ppermute | solution.py:1120
  609.5 81.7 %collective-permute-start.41 = (bf16[1024,384]{1,0:T(8,128)(2,1)}, bf16[1024,384]{1,0:T(8,128)(2,1)}, u32[]{:S(2)}, u32[]{:S(2)}) collective-permute-start(bf16[1024,384]{1,0:T(8,128)(2,1)} %fusion.7), channel_id=1, source_target_pairs={{0,16},{16,0},{1,17},{17,1},{2,18},{18,2},{3,19},{19,3},{4,20},{20... | collective-permute-start | bytes 2359304 | tf_op jit(solution)/shard_map/ppermute | solution.py:1115
  626.2 43.5 %collective-permute-start.55 = (bf16[384,1152]{1,0:T(8,128)(2,1)}, bf16[384,1152]{1,0:T(8,128)(2,1)}, u32[]{:S(2)}, u32[]{:S(2)}) collective-permute-start(bf16[384,1152]{1,0:T(8,128)(2,1)} %broadcast_select_fusion.1), channel_id=1, source_target_pairs={{0,16},{16,0},{1,17},{17,1},{2,18},{18,2},{3,19},{19,3},{4,20},{20... | collective-permute-start | bytes 2654216 | tf_op jit(solution)/shard_map/ppermute | solution.py:1115
  627.6 27.7 %collective-permute-start.53 = (bf16[384,1536]{1,0:T(8,128)(2,1)}, bf16[384,1536]{1,0:T(8,128)(2,1)S(1)}, u32[]{:S(2)}, u32[]{:S(2)}) collective-permute-start(bf16[384,1536]{1,0:T(8,128)(2,1)} %add_bitcast_fusion), channel_id=1, source_target_pairs={{0,8},{4,12},{8,0},{12,4},{1,9},{5,13},{9,1},{13,5},{2,10},{6,14},... | collective-permute-start | bytes 3538952 | tf_op jit(solution)/shard_map/ppermute | solution.py:1115
  628.5 39.4 %collective-permute-start.50 = (f32[7192]{0:T(1024)S(1)}, f32[7192]{0:T(1024)S(1)}, u32[]{:S(2)}, u32[]{:S(2)}) collective-permute-start(f32[7192]{0:T(1024)S(1)} %get-tuple-element.380), channel_id=1, source_target_pairs={{0,16},{16,0},{1,17},{17,1},{2,18},{18,2},{3,19},{19,3},{4,20},{20... | collective-permute-start | bytes 86312 | tf_op jit(solution)/shard_map/ppermute | solution.py:1115
  658.6 29.2 %collective-permute-start.54 = (bf16[384,1536]{1,0:T(8,128)(2,1)}, bf16[384,1536]{1,0:T(8,128)(2,1)}, u32[]{:S(2)}, u32[]{:S(2)}) collective-permute-start(bf16[384,1536]{1,0:T(8,128)(2,1)} %get-tuple-element.382), channel_id=1, source_target_pairs={{0,16},{16,0},{1,17},{17,1},{2,18},{18,2},{3,19},{19,3},{4,20},{20... | collective-permute-start | bytes 3538952 | tf_op jit(solution)/shard_map/ppermute | solution.py:1115
  666.5 39.5 %collective-permute-start.45 = (bf16[1024,384]{1,0:T(8,128)(2,1)}, bf16[1024,384]{1,0:T(8,128)(2,1)}, u32[]{:S(2)}, u32[]{:S(2)}) collective-permute-start(bf16[1024,384]{1,0:T(8,128)(2,1)} %get-tuple-element.384), channel_id=1, source_target_pairs={{0,16},{16,0},{1,17},{17,1},{2,18},{18,2},{3,19},{19,3},{4,20},{20... | collective-permute-start | bytes 2359304 | tf_op jit(solution)/shard_map/ppermute | solution.py:1115
  668.5 26.3 %collective-permute-start.51 = (f32[2560]{0:T(1024)}, f32[2560]{0:T(1024)}, u32[]{:S(2)}, u32[]{:S(2)}) collective-permute-start(f32[2560]{0:T(1024)} %slice.338), channel_id=1, source_target_pairs={{0,1},{1,0},{2,3},{3,2},{4,5},{5,4},{6,7},{7,6},{8,9},{9,8},{10,11... | collective-permute-start | bytes 30728 | tf_op jit(solution)/shard_map/ppermute | solution.py:1115
  673.0 23.9 %collective-permute-start.56 = (bf16[2,384,64]{1,2,0:T(8,128)(2,1)S(1)}, bf16[2,384,64]{1,2,0:T(8,128)(2,1)S(1)}, u32[]{:S(2)}, u32[]{:S(2)}) collective-permute-start(bf16[2,384,64]{1,2,0:T(8,128)(2,1)S(1)} %dynamic-slice_bitcast_fusion.8), channel_id=1, source_target_pairs={{0,1},{1,0},{2,3},{3,2},{4,5},{5,4},{6,7},{7,6},{8,9},{9,8},{10,11... | collective-permute-start | bytes 294920 | tf_op jit(solution)/shard_map/ppermute | solution.py:1115
  (102 other events, 1186.7 us)
Sparse Core Ops, SparseCore 0:
  113.4 61.0 reduce-scatter.3
  177.1 62.9 all-gather.2
  374.2 61.5 reduce-scatter.5
  439.2 63.5 all-gather.4
  597.0 59.4 reduce-scatter.7

commit v5 on v4

--- a/solution.py
+++ b/solution.py
@@ -556,6 +556,37 @@
     )
 
 
+def ahead_kernel(block, sources, grad, *refs):
+    *out_sources, out, w_out, out_sem = refs
+
+    @pl.when(pl.program_id(0) == 0)
+    def _():
+        weight_fetch(block, out_sources, w_out, out_sem)
+        weight_wait(out_sources, w_out, out_sem)
+
+    out[...] = dot_nn(grad[...], w_out[...])
+
+
+def ahead_backward(block, grad, w_out):
+    count, model = grad.shape
+    width = w_out[0].shape[1]
+    return pl.pallas_call(
+        partial(ahead_kernel, block, len(w_out)),
+        grid=(count // ROWS,),
+        in_specs=[rows_of(model), *[anywhere() for _ in w_out]],
+        out_specs=rows_of(width),
+        out_shape=jax.ShapeDtypeStruct((count, width), f32),
+        scratch_shapes=weight_scratch(w_out[0]),
+        compiler_params=params(),
+        cost_estimate=pl.CostEstimate(
+            flops=2 * count * width * model,
+            bytes_accessed=count * (2 * model + 4 * width) + 2 * model * width,
+            transcendentals=0,
+        ),
+        name="ahead_backward",
+    )(grad, *w_out)
+
+
 def gate_kernel(
     heads,
     block,
@@ -577,21 +608,27 @@
     later, earlier = refs[:2] if between else (None, None)
     refs = refs[2:] if between else refs
     grad_mixed, grad_gate, scaled_out, gain_sum, skip_sum, adjoint_out, *refs = refs
-    grad_in, adjoint, scales, w_out, out_sem = refs
+    if sources:
+        grad_in, adjoint, scales, w_out, out_sem = refs
+    else:
+        grad_in, (adjoint, scales) = grad, refs
     step = pl.program_id(0)
     groups = head_groups(act_x.shape[1], heads)
     state = act_bc.shape[1] // 2
 
     @pl.when(step == 0)
     def _():
-        weight_fetch(block, out_sources, w_out, out_sem)
+        if sources:
+            weight_fetch(block, out_sources, w_out, out_sem)
         gain_sum[...] = jnp.zeros_like(gain_sum)
         skip_sum[...] = jnp.zeros_like(skip_sum)
         adjoint[...] = jnp.zeros_like(adjoint)
         scales[...] = jnp.zeros_like(scales)
-        weight_wait(out_sources, w_out, out_sem)
-
-    grad_in[...] = dot_nn(grad[...], w_out[...])
+        if sources:
+            weight_wait(out_sources, w_out, out_sem)
+
+    if sources:
+        grad_in[...] = dot_nn(grad[...], w_out[...])
     total = sums[0][...]
     for more in sums[1:]:
         total = total + more[...]
@@ -678,10 +715,10 @@
             jax.ShapeDtypeStruct((state, width), bf16),
         ],
         scratch_shapes=[
-            pltpu.VMEM((ROWS, width), f32),
+            *([pltpu.VMEM((ROWS, width), f32)] if w_out else []),
             pltpu.VMEM((state, width), f32),
             pltpu.VMEM((CHUNK, CHUNK), f32),
-            *weight_scratch(w_out[0]),
+            *(weight_scratch(w_out[0]) if w_out else []),
         ],
         compiler_params=params(),
         cost_estimate=pl.CostEstimate(
@@ -1206,9 +1243,9 @@
     return part, sums, kept
 
 
-def gate_step(block, grad, sums, ends, kept, weights):
+def gate_step(block, grad, w_out, sums, ends, kept, weights):
     return gate_backward(
-        weights["heads"], block, grad, weights["w_out"], kept["gate_in"], kept["mixed"],
+        weights["heads"], block, grad, w_out, kept["gate_in"], kept["mixed"],
         kept["scaled"], kept["act_x"], kept["act_bc"], kept["run"], weights["gain"], sums, ends,
     )
 
@@ -1355,7 +1392,12 @@
     part, sums, kept_first = block_forward(
         0, first, first_edge, weights[0], None, 1, fetch_out
     )
-    summed = lax.psum_scatter(part, "head", scatter_dimension=0, tiled=True).astype(f32)
+    sums, last_grad = tied(sums, last_grad)
+    summed, grad_ahead = tied(
+        lax.psum_scatter(part, "head", scatter_dimension=0, tiled=True),
+        ahead_backward(1, last_grad, weights[1]["w_out"]),
+    )
+    summed = summed.astype(f32)
     sums_first = [sums, *others(sums, "head", 1)]
     scale_first = lax.rsqrt(sum(part[0] for part in sums_first) / INNER + epsilon)
     second_share = own_rows(first).astype(f32) + own_rows(scale_first)[:, None] * summed
@@ -1368,7 +1410,7 @@
     bits = list(bits_of("head"))
 
     grad_mixed, grad_gate, scaled, gain_sum, skip_sum, adjoint = gate_step(
-        1, last_grad, sums_second, (), kept_second, weights[1]
+        1, grad_ahead, (), sums_second, (), kept_second, weights[1]
     )
     normed = kept_second["normed"]
     early_sent = weights_backward([last_grad, normed], [scaled, grad_gate], False)
@@ -1418,7 +1460,7 @@
     out_kept, out_sent = parted(outward, "head", bits[-1])
 
     grad_mixed, grad_gate, scaled, gain_sum, skip_sum, adjoint = gate_step(
-        0, middle_grad, sums_first, (second, first), kept_first, weights[0]
+        0, middle_grad, weights[0]["w_out"], sums_first, (second, first), kept_first, weights[0]
     )
     normed = kept_first["normed"]
     early_sent = weights_backward([middle_grad, normed], [scaled, grad_gate], False)

time: 726 us -> 725 us (level)
    pallas_call x0 -> x1, Pallas kernels: none -> 7.54 us  [ahead_backward(): pl.pallas_call(partial(ahead_kernel, block, len(w_out)), grid=(count // R...]
  transfers between devices with their start and end apart: 63 -> 63, of which waited for: 26 -> 25; matrix products, arithmetic and copies ran while one was open for 13% -> 13% of each run, Pallas kernels for 21% -> 22%
where the time goes in v5:
time: 725 us; the launch traced here: 715 us
  waiting for transfers between devices  281 us (39%)
  Pallas kernels  244 us (34%)
  other arithmetic  59.8 us (8%)
  starting transfers between devices  58.1 us (8%)
  local copies, waits for them, and re-layouts  54.1 us (7%)
  between operations  17.4 us (2%)
    ppermute x30, waiting for transfers between devices, traded(): lax.ppermute(block, axis, [(i, i ^ bit) for i in range(lax.axis_size(axis...  112 us
    all_gather x1, waiting for transfers between devices, shards(): lax.all_gather(second_share.astype(bf16), 'head', axis=0, tiled=True)  64 us
    pallas_call x2, Pallas kernels, states_backward(): pl.pallas_call(partial(states_kernel, heads, len(arrived) + 1), grid=(ste...  57.9 us
    pallas_call x8, Pallas kernels, weights_backward(): pl.pallas_call(partial(weights_kernel, len(lefts)), grid_spec=pltpu.Prefe...  47.3 us
    reduce_scatter x1, waiting for transfers between devices, shards(): lax.psum_scatter(part, 'head', scatter_dimension=0, tiled=True)  45.3 us
    pallas_call x2, Pallas kernels, project_forward(): pl.pallas_call(partial(project_kernel, heads, block, len(pack)), grid=(co...  34.5 us
    reduce_scatter x1, waiting for transfers between devices, shards(): rows_part = lax.psum_scatter(part, 'head', scatter_dimension=0, tiled=True)  34 us
    ppermute x28, starting transfers between devices, rotated(): lax.ppermute(block, axis, [(i, (i + distance) % size) for i in range(size)])  29.7 us
  transfers between devices with their start and end apart: 63, of which 25 were waited for; matrix products, arithmetic and copies ran while one was open for 13% of the time, Pallas kernels for 22%

profile of v5, /device:TPU:0, one launch (start us, length us, event | category | flops | bytes accessed | tf_op | source)
XLA Modules:
  0.0 714.7 jit_solution(7153424833749737499)
XLA Ops:
  18.1 16.3 %collective-permute-done.refs_1_.refs_4_ = bf16[384,1152]{1,0:T(8,128)(2,1)} collective-permute-done((bf16[384,1152]{1,0:T(8,128)(2,1)}, bf16[384,1152]{1,0:T(8,128)(2,1)}, u32[]{:S(2)}, u32[]{:S(2)}) %collective-permute-start) | collective-permute-done | bytes 884768 | tf_op jit(solution)/shard_map/ppermute | solution.py:1152
  45.7 16.6 %collective-permute-done.4 = f32[6436]{0:T(1024)S(1)} collective-permute-done((f32[6436]{0:T(1024)S(1)}, f32[6436]{0:T(1024)S(1)}, u32[]{:S(2)}, u32[]{:S(2)}) %collective-permute-start.4) | collective-permute-done | bytes 25776 | tf_op jit(solution)/shard_map/ppermute | solution.py:1152
  66.8 17.3 %project_forward.2 = (bf16[1024,1536]{1,0:T(8,128)(2,1)}, f32[1024,1]{1,0:T(8,128)}, bf16[1024,768]{1,0:T(8,128)(2,1)}, bf16[1024,256]{1,0:T(8,128)(2,1)}, f32[8...) custom-call(bf16[1024,1536]{1,0:T(8,128)(2,1)} %dynamic-slice_bitcas, ...), custom_call_target="tpu_custom_call" | custom-call | flops 3623878656 | bytes 16121856 | tf_op jit(solution)/shard_map/project_forward/pallas_call | solution.py:282
  85.9 10.0 %inner_forward.2 = (f32[1024,768]{1,0:T(8,128)}, f32[1024,768]{1,0:T(8,128)}) custom-call(bf16[1024,768]{1,0:T(8,128)(2,1)} %get-tuple-element.200.act_x, bf16[1024,256]{1,0:T(8,128)(2,1)} %get-tuple-element.201.act_bc, f32[1024,128]{1,0:T(8,128)} %get-tuple-element.202.dt_in, f32[1024,128]{1,0:T(8,128)} %get-tuple-element.203.run_in, ...), custom_call_target="tpu_custom_call" | custom-call | flops 3221225472 | bytes 13369344 | tf_op jit(solution)/shard_map/inner_forward/pallas_call | solution.py:385
  100.8 12.4 %outer_forward.2 = (bf16[1024,768]{1,0:T(8,128)(2,1)}, bf16[1024,768]{1,0:T(8,128)(2,1)}, bf16[1024,1536]{1,0:T(8,128)(2,1)}, f32[8,1024]{1,0:T(8,128)}, bf16[8,128,768]{2,1,0:T(8,128)(2,1)}) custom-call(bf16[1024,768]{1,0:T(8,128)(2,1)} %get-tuple-element.200.act_x, bf16[1024,256]{1,0:T(8,128)(2,1)} %get-tuple-element.201.act_bc, ...), custom_call_target="tpu_custom_call" | custom-call | flops 2818572288 | bytes 14155776 | tf_op jit(solution)/shard_map/outer_forward/pallas_call | solution.py:516
  121.8 7.5 %ahead_backward.1.grad = f32[1024,768]{1,0:T(8,128)} custom-call(bf16[1024,1536]{1,0:T(8,128)(2,1)} %dynamic-slice_bitcast_fusion.grad.refs_8_.refs_0_, bf16[1536,768]{1,0:T(8,128)(2,1)} %bitcast.143, bf16[2,384,768]{2,1,0:T(8,128)(2,1)} %copy-done.2, bf16[2,384,768]{2,1,0:T(8,128)(2,1)} %copy-done.3), custom_call_target="tpu_custom_call" | custom-call | flops 2415919104 | bytes 8650752 | tf_op jit(solution)/shard_map/ahead_backward/pallas_call | solution.py:573
  129.5 45.3 %reduce-scatter.4.cloned.1.call-done = bf16[256,1536]{1,0:T(8,128)(2,1)} async-done(((bf16[1024,1536]{1,0:T(8,128)(2,1)}), bf16[256,1536]{1,0:T(8,128)(2,1)}) %reduce-scatter.4.cloned.1.call-update) | async-done | bytes 786448 | tf_op jit(solution)/shard_map/reduce_scatter | solution.py:1397
  178.1 64.0 %all-gather.3.cloned.1.call-done.x_in.refs_7_ = bf16[1024,1536]{1,0:T(8,128)(2,1)} async-done(((bf16[256,1536]{1,0:T(8,128)(2,1)}), bf16[1024,1536]{1,0:T(8,128)(2,1)}) %all-gather.3.cloned.1.call-update) | async-done | bytes 3145744 | tf_op jit(solution)/shard_map/all_gather | solution.py:1404
  247.5 17.2 %project_forward.3 = (bf16[1024,1536]{1,0:T(8,128)(2,1)}, f32[1024,1]{1,0:T(8,128)}, bf16[1024,768]{1,0:T(8,128)(2,1)}, bf16[1024,256]{1,0:T(8,128)(2,1)}, f32[8...) custom-call(bf16[1024,1536]{1,0:T(8,128)(2,1)} %all-gather.3.cloned., ...), custom_call_target="tpu_custom_call" | custom-call | flops 3623878656 | bytes 16121856 | tf_op jit(solution)/shard_map/project_forward/pallas_call | solution.py:282
  268.0 9.9 %inner_forward.3 = (f32[1024,768]{1,0:T(8,128)}, f32[1024,768]{1,0:T(8,128)}) custom-call(bf16[1024,768]{1,0:T(8,128)(2,1)} %get-tuple-element.223.act_x, bf16[1024,256]{1,0:T(8,128)(2,1)} %get-tuple-element.224.act_bc, f32[1024,128]{1,0:T(8,128)} %get-tuple-element.225.dt_in, f32[1024,128]{1,0:T(8,128)} %get-tuple-element.226.run_in, ...), custom_call_target="tpu_custom_call" | custom-call | flops 3221225472 | bytes 13369344 | tf_op jit(solution)/shard_map/inner_forward/pallas_call | solution.py:385
  279.5 13.3 %outer_forward.3 = (bf16[1024,768]{1,0:T(8,128)(2,1)}, bf16[1024,768]{1,0:T(8,128)(2,1)}, bf16[4,1024,384]{2,1,0:T(8,128)(2,1)}, f32[8,1024]{1,0:T(8,128)}, bf16[8,128,768]{2,1,0:T(8,128)(2,1)}) custom-call(bf16[1024,768]{1,0:T(8,128)(2,1)} %get-tuple-element.223.act_x, bf16[1024,256]{1,0:T(8,128)(2,1)} %get-tuple-element.224.act_bc, ...), custom_call_target="tpu_custom_call" | custom-call | flops 2818572288 | bytes 14155776 | tf_op jit(solution)/shard_map/outer_forward/pallas_call | solution.py:516
  300.5 9.5 %gate_backward.2 = (bf16[1024,768]{1,0:T(8,128)(2,1)}, bf16[1024,768]{1,0:T(8,128)(2,1)}, bf16[1024,768]{1,0:T(8,128)(2,1)}, f32[8,768]{1,0:T(8,128)}, f32[8,768]{1,0:T(8,128)}, /*index=5*/bf16[128,768]{1,0:T(8,128)(2,1)}) custom-call(f32[1024,768]{1,0:T(8,128)} %ahead_backward.1.grad, f32[1024,768]{1,0:T(8,128)} %get-tuple-element.228.gate_in, ...), custom_call_target="tpu_custom_call" | custom-call | flops 1409286144 | bytes 12582912 | tf_op jit(solution)/shard_map/gate_backward/pallas_call | solution.py:685
  323.6 28.9 %states_backward.2 = (bf16[1024,1152]{1,0:T(8,128)(2,1)}, f32[16,1152]{1,0:T(8,128)}, f32[16,1152]{1,0:T(8,128)}, f32[8,768]{1,0:T(8,128)}, f32[8,256]{1,0:T(8,1...) custom-call(bf16[1024,768]{1,0:T(8,128)(2,1)} %get-tuple-element.239.grad_mixed, bf16[1024,768]{1,0:T(8,128)(2,1)} %get-tuple-element.223.act_x, ...), custom_call_target="tpu_custom_call" | custom-call | flops 2013265920 | bytes 12582912 | tf_op jit(solution)/shard_map/states_backward/pallas_call | solution.py:955
  359.4 13.8 %part_backward.2 = (bf16[1024,1536]{1,0:T(8,128)(2,1)}, f32[8,1024]{1,0:T(8,128)}, f32[8,1536]{1,0:T(8,128)}) custom-call(bf16[1024,768]{1,0:T(8,128)(2,1)} %get-tuple-element.259.refs_3_.grad_gate, bf16[1024,1152]{1,0:T(8,128)(2,1)} %fusion.9.packed.refs_1_, bf16[1024,1536]{1,0:T(8,128)(2,1)} %all-gather.3.cloned.1.call-done.x_in.refs_7_, ...), custom_call_target="tpu_custom_call" | custom-call | flops 6039797760 | bytes 18481152 | tf_op jit(solution)/shard_map/part_backward/pallas_call | solution.py:1083
  400.9 34.0 %reduce-scatter.6.cloned.1.call-done = bf16[256,1536]{1,0:T(8,128)(2,1)} async-done(((bf16[1024,1536]{1,0:T(8,128)(2,1)}), bf16[256,1536]{1,0:T(8,128)(2,1)}) %reduce-scatter.6.cloned.1.call-update) | async-done | bytes 786448 | tf_op jit(solution)/shard_map/reduce_scatter | solution.py:1439
  446.0 14.7 %collective-permute-done.34 = bf16[384,1152]{1,0:T(8,128)(2,1)} collective-permute-done((bf16[384,1152]{1,0:T(8,128)(2,1)S(1)}, bf16[384,1152]{1,0:T(8,128)(2,1)}, u32[]{:S(2)}, u32[]{:S(2)}) %collective-permute-start.34) | collective-permute-done | bytes 884768 | tf_op jit(solution)/shard_map/ppermute | solution.py:1152
  462.6 22.1 %collective-permute-done.33 = bf16[384,1536]{1,0:T(8,128)(2,1)} collective-permute-done((bf16[384,1536]{1,0:T(8,128)(2,1)}, bf16[384,1536]{1,0:T(8,128)(2,1)}, u32[]{:S(2)}, u32[]{:S(2)}) %collective-permute-start.33) | collective-permute-done | bytes 1179680 | tf_op jit(solution)/shard_map/ppermute | solution.py:1152
  487.5 14.2 %all-gather.5.cloned.1.call-done.grad.refs_0_ = bf16[1024,1536]{1,0:T(8,128)(2,1)} async-done(((bf16[256,1536]{1,0:T(8,128)(2,1)}), bf16[1024,1536]{1,0:T(8,128)(2,1)}) %all-gather.5.cloned.1.call-update) | async-done | bytes 3145744 | tf_op jit(solution)/shard_map/all_gather | solution.py:1454
  501.6 14.4 %gate_backward.3 = (bf16[1024,768]{1,0:T(8,128)(2,1)}, bf16[1024,768]{1,0:T(8,128)(2,1)}, bf16[1024,768]{1,0:T(8,128)(2,1)}, f32[8,768]{1,0:T(8,128)}, f32[8,768]{1,0:T(8,128)}, /*index=5*/bf16[128,768]{1,0:T(8,128)(2,1)}) custom-call(bf16[1024,1536]{1,0:T(8,128)(2,1)} %all-gather.5.cloned.1.call-done.grad.refs_0_, f32[1024,768]{1,0:T(8,128)} %get-tuple-element.206.gate_in, ...), custom_call_target="tpu_custom_call" | custom-call | flops 2617245696 | bytes 12582912 | tf_op jit(solution)/shard_map/gate_backward/pallas_call | solution.py:685
  520.1 6.5 weights_backward.12
  528.6 28.9 %states_backward.3 = (bf16[1024,1152]{1,0:T(8,128)(2,1)}, f32[16,1152]{1,0:T(8,128)}, f32[16,1152]{1,0:T(8,128)}, f32[8,768]{1,0:T(8,128)}, f32[8,256]{1,0:T(8,1...) custom-call(bf16[1024,768]{1,0:T(8,128)(2,1)} %get-tuple-element.291.grad_mixed, bf16[1024,768]{1,0:T(8,128)(2,1)} %get-tuple-element.200.act_x, ...), custom_call_target="tpu_custom_call" | custom-call | flops 2013265920 | bytes 12582912 | tf_op jit(solution)/shard_map/states_backward/pallas_call | solution.py:955
  578.3 13.5 %part_backward.3 = (bf16[4,1024,384]{2,1,0:T(8,128)(2,1)}, f32[8,1024]{1,0:T(8,128)}, f32[8,1536]{1,0:T(8,128)}) custom-call(bf16[1024,768]{1,0:T(8,128)(2,1)} %get-tuple-element.321.refs_3_.grad_gate, bf16[1024,1152]{1,0:T(8,128)(2,1)} %fusion.10.refs_1_.packed, bf16[1024,1536]{1,0:T(8,128)(2,1)} %dynamic-slice_bitcast_fusion.1.x_in.refs_8_, ...), custom_call_target="tpu_custom_call" | custom-call | flops 6039797760 | bytes 18481152 | tf_op jit(solution)/shard_map/part_backward/pallas_call | solution.py:1083
  628.5 25.6 %collective-permute-done.53 = bf16[384,1536]{1,0:T(8,128)(2,1)S(1)} collective-permute-done((bf16[384,1536]{1,0:T(8,128)(2,1)}, bf16[384,1536]{1,0:T(8,128)(2,1)S(1)}, u32[]{:S(2)}, u32[]{:S(2)}) %collective-permute-start.53) | collective-permute-done | bytes 1179680 | tf_op jit(solution)/shard_map/ppermute | solution.py:1152
  678.0 8.6 %collective-permute-done.54 = bf16[384,1536]{1,0:T(8,128)(2,1)} collective-permute-done((bf16[384,1536]{1,0:T(8,128)(2,1)}, bf16[384,1536]{1,0:T(8,128)(2,1)}, u32[]{:S(2)}, u32[]{:S(2)}) %collective-permute-start.54) | collective-permute-done | bytes 1179680 | tf_op jit(solution)/shard_map/ppermute | solution.py:1152
  (407 shorter events, 232.9 us)
Async XLA Ops:
  7.2 167.6 %reduce-scatter.4.cloned.1.call-start = ((), (), s32[]{:S(2)}) async-start(), calls=%async_computation.3 | async-start | bytes 3932160 | tf_op jit(solution)/shard_map/reduce_scatter | solution.py:1397
  15.2 29.9 %collective-permute-start.3 = (bf16[3,1536]{1,0:T(4,128)(2,1)S(1)}, bf16[3,1536]{1,0:T(4,128)(2,1)S(1)}, u32[]{:S(2)}, u32[]{:S(2)}) collective-permute-start(bf16[3,1536]{1,0:T(4,128)(2,1)S(1)} %fusion.13), channel_id=1, source_target_pairs={{0,4},{4,8},{8,12},{12,0},{1,5},{5,9},{9,13},{13,1},{2,6},{6,10},{... | collective-permute-start | bytes 27656 | tf_op jit(solution)/shard_map/ppermute | solution.py:1157
  34.4 28.0 %collective-permute-start.2 = (bf16[2,384,768]{2,1,0:T(8,128)(2,1)}, bf16[2,384,768]{2,1,0:T(8,128)(2,1)}, u32[]{:S(2)}, u32[]{:S(2)}) collective-permute-start(bf16[2,384,768]{2,1,0:T(8,128)(2,1)} %dynamic-slice_bitcast_fusion.5), channel_id=1, source_target_pairs={{0,16},{16,0},{1,17},{17,1},{2,18},{18,2},{3,19},{19,3},{4,20},{20... | collective-permute-start | bytes 3538952 | tf_op jit(solution)/shard_map/ppermute | solution.py:1152
  63.0 33.9 %collective-permute-start.8 = (bf16[2,384,768]{2,1,0:T(8,128)(2,1)S(1)}, bf16[2,384,768]{2,1,0:T(8,128)(2,1)S(1)}, u32[]{:S(2)}, u32[]{:S(2)}) collective-permute-start(bf16[2,384,768]{2,1,0:T(8,128)(2,1)S(1)} %dynamic-slice_bitcast_fusion.4), channel_id=1, source_target_pairs={{0,16},{16,0},{1,17},{17,1},{2,18},{18,2},{3,19},{19,3},{4,20},{20... | collective-permute-start | bytes 3538952 | tf_op jit(solution)/shard_map/ppermute | solution.py:1152
  113.2 128.8 %all-gather.3.cloned.1.call-start = ((), (), s32[]{:S(2)}) async-start(), calls=%async_computation.4 | async-start | bytes 3932160 | tf_op jit(solution)/shard_map/all_gather | solution.py:1404
  177.4 257.4 %reduce-scatter.6.cloned.1.call-start = ((), (), s32[]{:S(2)}) async-start(), calls=%async_computation.5 | async-start | bytes 3932160 | tf_op jit(solution)/shard_map/reduce_scatter | solution.py:1439
  322.2 37.3 %collective-permute-start.27 = (bf16[2,1024,384]{2,1,0:T(8,128)(2,1)}, bf16[2,1024,384]{2,1,0:T(8,128)(2,1)S(1)}, u32[]{:S(2)}, u32[]{:S(2)}) collective-permute-start(bf16[2,1024,384]{2,1,0:T(8,128)(2,1)} %get-tuple-element.400), channel_id=1, source_target_pairs={{0,1},{1,0},{2,3},{3,2},{4,5},{5,4},{6,7},{7,6},{8,9},{9,8},{10,11... | collective-permute-start | bytes 4718600 | tf_op jit(solution)/shard_map/ppermute | solution.py:1152
  373.3 128.4 %all-gather.5.cloned.1.call-start = ((), (), s32[]{:S(2)}) async-start(), calls=%async_computation.6 | async-start | bytes 3932160 | tf_op jit(solution)/shard_map/all_gather | solution.py:1454
  373.3 23.6 %collective-permute-start.28 = (bf16[2,384,1536]{2,1,0:T(8,128)(2,1)}, bf16[2,384,1536]{2,1,0:T(8,128)(2,1)}, u32[]{:S(2)}, u32[]{:S(2)}) collective-permute-start(bf16[2,384,1536]{2,1,0:T(8,128)(2,1)} %weights_backward.8), channel_id=1, source_target_pairs={{0,4},{4,0},{8,12},{12,8},{1,5},{5,1},{9,13},{13,9},{2,6},{6,2},{1... | collective-permute-start | bytes 7077896 | tf_op jit(solution)/shard_map/ppermute | solution.py:1152
  437.9 220.1 %reduce-scatter.8.cloned.1.call-start = ((), (), s32[]{:S(2)}) async-start(), calls=%async_computation.7 | async-start | bytes 3932160 | tf_op jit(solution)/shard_map/reduce_scatter | solution.py:1488
  443.7 40.9 %collective-permute-start.33 = (bf16[384,1536]{1,0:T(8,128)(2,1)}, bf16[384,1536]{1,0:T(8,128)(2,1)}, u32[]{:S(2)}, u32[]{:S(2)}) collective-permute-start(bf16[384,1536]{1,0:T(8,128)(2,1)} %add_bitcast_fusion.1), channel_id=1, source_target_pairs={{0,8},{4,12},{8,0},{12,4},{1,9},{5,13},{9,1},{13,5},{2,10},{6,14},... | collective-permute-start | bytes 3538952 | tf_op jit(solution)/shard_map/ppermute | solution.py:1152
  526.8 36.5 %collective-permute-start.39 = (bf16[1,1024,384]{2,1,0:T(8,128)(2,1)S(1)}, bf16[1,1024,384]{2,1,0:T(8,128)(2,1)S(1)}, u32[]{:S(2)}, u32[]{:S(2)}) collective-permute-start(bf16[1,1024,384]{2,1,0:T(8,128)(2,1)S(1)} %copy-done.27), channel_id=1, source_target_pairs={{0,2},{1,3},{2,0},{3,1},{4,6},{5,7},{6,4},{7,5},{8,10},{9,11},{10,... | collective-permute-start | bytes 2359304 | tf_op jit(solution)/shard_map/ppermute | solution.py:1152
  569.5 38.8 %collective-permute-start.46 = (bf16[2,384,1536]{2,1,0:T(8,128)(2,1)}, bf16[2,384,1536]{2,1,0:T(8,128)(2,1)}, u32[]{:S(2)}, u32[]{:S(2)}) collective-permute-start(bf16[2,384,1536]{2,1,0:T(8,128)(2,1)} %weights_backward.12), channel_id=1, source_target_pairs={{0,4},{4,0},{8,12},{12,8},{1,5},{5,1},{9,13},{13,9},{2,6},{6,2},{1... | collective-permute-start | bytes 7077896 | tf_op jit(solution)/shard_map/ppermute | solution.py:1152
  591.8 29.5 %collective-permute-start.44 = (f32[8,1024]{1,0:T(8,128)}, f32[8,1024]{1,0:T(8,128)S(1)}, u32[]{:S(2)}, u32[]{:S(2)}) collective-permute-start(f32[8,1024]{1,0:T(8,128)} %get-tuple-element.318), channel_id=1, source_target_pairs={{0,3},{1,0},{2,1},{3,2},{4,7},{5,4},{6,5},{7,6},{8,11},{9,8},{10,9... | collective-permute-start | bytes 98312 | tf_op jit(solution)/shard_map/ppermute | solution.py:1157
  594.0 27.3 %collective-permute-start.43 = (f32[8,1024]{1,0:T(8,128)}, f32[8,1024]{1,0:T(8,128)S(1)}, u32[]{:S(2)}, u32[]{:S(2)}) collective-permute-start(f32[8,1024]{1,0:T(8,128)} %get-tuple-element.318), channel_id=1, source_target_pairs={{0,2},{1,3},{2,0},{3,1},{4,6},{5,7},{6,4},{7,5},{8,10},{9,11},{10,... | collective-permute-start | bytes 98312 | tf_op jit(solution)/shard_map/ppermute | solution.py:1157
  594.0 27.3 %collective-permute-start.42 = (f32[8,1024]{1,0:T(8,128)}, f32[8,1024]{1,0:T(8,128)S(1)}, u32[]{:S(2)}, u32[]{:S(2)}) collective-permute-start(f32[8,1024]{1,0:T(8,128)} %get-tuple-element.318), channel_id=1, source_target_pairs={{0,1},{1,2},{2,3},{3,0},{4,5},{5,6},{6,7},{7,4},{8,9},{9,10},{10,1... | collective-permute-start | bytes 98312 | tf_op jit(solution)/shard_map/ppermute | solution.py:1157
  608.2 81.7 %collective-permute-start.41 = (bf16[1024,384]{1,0:T(8,128)(2,1)}, bf16[1024,384]{1,0:T(8,128)(2,1)}, u32[]{:S(2)}, u32[]{:S(2)}) collective-permute-start(bf16[1024,384]{1,0:T(8,128)(2,1)} %fusion.6), channel_id=1, source_target_pairs={{0,16},{16,0},{1,17},{17,1},{2,18},{18,2},{3,19},{19,3},{4,20},{20... | collective-permute-start | bytes 2359304 | tf_op jit(solution)/shard_map/ppermute | solution.py:1152
  625.0 43.3 %collective-permute-start.55 = (bf16[384,1152]{1,0:T(8,128)(2,1)}, bf16[384,1152]{1,0:T(8,128)(2,1)}, u32[]{:S(2)}, u32[]{:S(2)}) collective-permute-start(bf16[384,1152]{1,0:T(8,128)(2,1)} %broadcast_select_fusion.1), channel_id=1, source_target_pairs={{0,16},{16,0},{1,17},{17,1},{2,18},{18,2},{3,19},{19,3},{4,20},{20... | collective-permute-start | bytes 2654216 | tf_op jit(solution)/shard_map/ppermute | solution.py:1152
  626.4 27.7 %collective-permute-start.53 = (bf16[384,1536]{1,0:T(8,128)(2,1)}, bf16[384,1536]{1,0:T(8,128)(2,1)S(1)}, u32[]{:S(2)}, u32[]{:S(2)}) collective-permute-start(bf16[384,1536]{1,0:T(8,128)(2,1)} %add_bitcast_fusion), channel_id=1, source_target_pairs={{0,8},{4,12},{8,0},{12,4},{1,9},{5,13},{9,1},{13,5},{2,10},{6,14},... | collective-permute-start | bytes 3538952 | tf_op jit(solution)/shard_map/ppermute | solution.py:1152
  627.3 39.4 %collective-permute-start.50 = (f32[7192]{0:T(1024)S(1)}, f32[7192]{0:T(1024)S(1)}, u32[]{:S(2)}, u32[]{:S(2)}) collective-permute-start(f32[7192]{0:T(1024)S(1)} %get-tuple-element.388), channel_id=1, source_target_pairs={{0,16},{16,0},{1,17},{17,1},{2,18},{18,2},{3,19},{19,3},{4,20},{20... | collective-permute-start | bytes 86312 | tf_op jit(solution)/shard_map/ppermute | solution.py:1152
  657.4 29.2 %collective-permute-start.54 = (bf16[384,1536]{1,0:T(8,128)(2,1)}, bf16[384,1536]{1,0:T(8,128)(2,1)}, u32[]{:S(2)}, u32[]{:S(2)}) collective-permute-start(bf16[384,1536]{1,0:T(8,128)(2,1)} %get-tuple-element.390), channel_id=1, source_target_pairs={{0,16},{16,0},{1,17},{17,1},{2,18},{18,2},{3,19},{19,3},{4,20},{20... | collective-permute-start | bytes 3538952 | tf_op jit(solution)/shard_map/ppermute | solution.py:1152
  665.2 39.5 %collective-permute-start.45 = (bf16[1024,384]{1,0:T(8,128)(2,1)}, bf16[1024,384]{1,0:T(8,128)(2,1)}, u32[]{:S(2)}, u32[]{:S(2)}) collective-permute-start(bf16[1024,384]{1,0:T(8,128)(2,1)} %get-tuple-element.392), channel_id=1, source_target_pairs={{0,16},{16,0},{1,17},{17,1},{2,18},{18,2},{3,19},{19,3},{4,20},{20... | collective-permute-start | bytes 2359304 | tf_op jit(solution)/shard_map/ppermute | solution.py:1152
  667.3 26.3 %collective-permute-start.51 = (f32[2560]{0:T(1024)}, f32[2560]{0:T(1024)}, u32[]{:S(2)}, u32[]{:S(2)}) collective-permute-start(f32[2560]{0:T(1024)} %slice.338), channel_id=1, source_target_pairs={{0,1},{1,0},{2,3},{3,2},{4,5},{5,4},{6,7},{7,6},{8,9},{9,8},{10,11... | collective-permute-start | bytes 30728 | tf_op jit(solution)/shard_map/ppermute | solution.py:1152
  671.6 24.1 %collective-permute-start.56 = (bf16[2,384,64]{1,2,0:T(8,128)(2,1)S(1)}, bf16[2,384,64]{1,2,0:T(8,128)(2,1)S(1)}, u32[]{:S(2)}, u32[]{:S(2)}) collective-permute-start(bf16[2,384,64]{1,2,0:T(8,128)(2,1)S(1)} %dynamic-slice_bitcast_fusion.8), channel_id=1, source_target_pairs={{0,1},{1,0},{2,3},{3,2},{4,5},{5,4},{6,7},{7,6},{8,9},{9,8},{10,11... | collective-permute-start | bytes 294920 | tf_op jit(solution)/shard_map/ppermute | solution.py:1152
  (102 other events, 1180.5 us)
Sparse Core Ops, SparseCore 0:
  113.4 61.3 reduce-scatter.3
  177.5 64.5 all-gather.2
  373.4 61.3 reduce-scatter.5
  438.0 63.5 all-gather.4
  595.8 59.4 reduce-scatter.7
